TPU v7x, 128 devices: a whole 4x4x4 slice. The times are simulated.
128 devices in a mesh: row: 16 (over y_hi, z, core), col: 8 (over x, y_lo).
Axes of the slice: x: 4, y: 4 (y_hi: 2, y_lo: 2; y = y_hi * 2 + y_lo), z: 4, core: 2. Of those that a mesh axis runs over, the one named last changes fastest.
Arguments:
- pair_input: bfloat16 [512, 512, 128], P('row', 'col'), may hold values from -18 to 18
- token_mask: int32 [512], replicated, may hold values 0 or 1
- out_check_weights: int32 [512], replicated, may hold values from 1 to 5, as said below
- in_check_weights: int32 [512], replicated, may hold values from 1 to 5, as said below
- out_norm_gain: float32 [128], replicated, may hold values from 0.25 to 1.75
- out_proj: bfloat16 [128, 256], replicated, may hold values from -0.5 to 0.5
- out_gate: bfloat16 [128, 128], replicated, may hold values from -0.5 to 0.5
- out_final_gain: float32 [64], replicated, may hold values from 0.25 to 1.75
- out_final: bfloat16 [64, 128], replicated, may hold values from -0.75 to 0.75
- in_norm_gain: float32 [128], replicated, may hold values from 0.25 to 1.75
- in_proj: bfloat16 [128, 256], replicated, may hold values from -0.5 to 0.5
- in_gate: bfloat16 [128, 128], replicated, may hold values from -0.5 to 0.5
- in_final_gain: float32 [64], replicated, may hold values from 0.25 to 1.75
- in_final: bfloat16 [64, 128], replicated, may hold values from -0.75 to 0.75
- att_norm_gain: float32 [128], replicated, may hold values from 0.25 to 1.75
- att_qkv: bfloat16 [128, 384], replicated, may hold values from -0.5 to 0.5
- att_bias: bfloat16 [128, 4], replicated, may hold values from -20 to 20
- att_gate: bfloat16 [128, 128], replicated, may hold values from -0.5 to 0.5
- att_out: bfloat16 [128, 128], replicated, may hold values from -0.5 to 0.5
Outputs:
- pair_output: bfloat16 [512, 512, 128], P('row', 'col')
- out_checksum: float32 [512, 64], P('row')
- in_checksum: float32 [512, 64], P('col')
Inputs may be any that keep to these rules, and one draw needn't show every extreme that they name: `out_check_weights`: entry j lies between 1 + (4 * j) // 512 and 2 + (4 * j) // 512. `in_check_weights`: entry j lies between 1 + (4 * j) // 512 and 2 + (4 * j) // 512.
All inputs are finite; a program needn't handle non-finite values.
Results may differ from a plain program's by a relative error of at most 0.019.
Values may be sent and summed in bfloat16 or wider, within the bound.
No kernel may reach another device: no remote copies, remote signals or barrier semaphores. Data moves between devices by JAX's collectives and lax.ppermute only.
A program may use at most 128 MiB of HBM per device.

v0:
```python
import jax
import jax.numpy as jnp
from jax import lax
from jax.sharding import PartitionSpec as P

CM = 64
HEADS = 4
DH = 32


def spread(block, axis, holder):
    block = jnp.where(lax.axis_index(axis) == holder, block, jnp.zeros_like(block))
    return lax.psum(block, axis)


def layer_norm(values_in, gain_vec):
    chan_mean = jnp.mean(values_in, axis=-1, keepdims=True)
    centered = values_in - chan_mean
    variance = jnp.mean(centered * centered, axis=-1, keepdims=True)
    return centered * lax.rsqrt(variance + 1e-05) * gain_vec


def projections(state, gain_vec, proj_weight, gate_weight, tile_mask):
    normed = layer_norm(state, gain_vec).astype(jnp.bfloat16)
    mixed = jnp.einsum("rcz,zm->mrc", normed, proj_weight, preferred_element_type=jnp.float32)
    left_proj = (jax.nn.sigmoid(mixed[0:CM]) * mixed[CM : 2 * CM] * tile_mask).astype(jnp.bfloat16)
    right_proj = (
        jax.nn.sigmoid(mixed[2 * CM : 3 * CM]) * mixed[3 * CM : 4 * CM] * tile_mask
    ).astype(jnp.bfloat16)
    gated = jax.nn.sigmoid(jnp.dot(normed, gate_weight, preferred_element_type=jnp.float32)).astype(
        jnp.bfloat16
    )
    return (left_proj, right_proj, gated)


def finish_update(state, product, gated, final_gain, final_weight):
    normed_product = layer_norm(jnp.transpose(product, (1, 2, 0)), final_gain).astype(jnp.bfloat16)
    update = jnp.dot(normed_product, final_weight, preferred_element_type=jnp.float32)
    return state + gated.astype(jnp.float32) * update


def on_device(
    pair_input,
    token_mask,
    out_check_weights,
    in_check_weights,
    out_norm_gain,
    out_proj,
    out_gate,
    out_final_gain,
    out_final,
    in_norm_gain,
    in_proj,
    in_gate,
    in_final_gain,
    in_final,
    att_norm_gain,
    att_qkv,
    att_bias,
    att_gate,
    att_out,
):
    tile_rows = pair_input.shape[0]
    tile_cols = pair_input.shape[1]
    row_count = lax.axis_size("row")
    col_count = lax.axis_size("col")
    mirror_ratio = row_count // col_count
    token_total = tile_rows * row_count
    row_place = lax.axis_index("row")
    col_place = lax.axis_index("col")
    mask_float = token_mask.astype(jnp.float32)
    row_mask = lax.dynamic_slice_in_dim(mask_float, row_place * tile_rows, tile_rows)
    col_mask = lax.dynamic_slice_in_dim(mask_float, col_place * tile_cols, tile_cols)
    tile_mask = row_mask[:, None] * col_mask[None, :]
    state = pair_input.astype(jnp.float32)
    left_proj, right_proj, gated = projections(state, out_norm_gain, out_proj, out_gate, tile_mask)
    left_rows, right_rows = (
        lax.all_gather(left_proj, "col", axis=2, tiled=True),
        lax.all_gather(right_proj, "col", axis=2, tiled=True),
    )
    mirrored = [
        spread(right_rows, "row", col_place * mirror_ratio + sub_index)
        for sub_index in range(mirror_ratio)
    ]
    right_panel = jnp.concatenate(mirrored, axis=1)
    product = jnp.einsum("mik,mjk->mij", left_rows, right_panel, preferred_element_type=jnp.float32)
    col_weights = lax.dynamic_slice_in_dim(
        out_check_weights.astype(jnp.float32), col_place * tile_cols, tile_cols
    )
    out_terms = jnp.einsum("mij,j->im", product, col_weights, precision=lax.Precision.HIGHEST)
    out_checksum = lax.psum(out_terms, "col") / token_total
    state = finish_update(state, product, gated, out_final_gain, out_final)
    left_proj, right_proj, gated = projections(state, in_norm_gain, in_proj, in_gate, tile_mask)
    left_cols, right_cols = (
        lax.all_gather(left_proj, "row", axis=1, tiled=True),
        lax.all_gather(right_proj, "row", axis=1, tiled=True),
    )
    own_slice = lax.dynamic_slice_in_dim(
        left_cols, row_place % mirror_ratio * tile_rows, tile_rows, 2
    )
    left_panel = spread(own_slice, "col", row_place // mirror_ratio)
    product = jnp.einsum("mki,mkj->mij", left_panel, right_cols, preferred_element_type=jnp.float32)
    row_weights = lax.dynamic_slice_in_dim(
        in_check_weights.astype(jnp.float32), row_place * tile_rows, tile_rows
    )
    in_terms = jnp.einsum("mij,i->jm", product, row_weights, precision=lax.Precision.HIGHEST)
    in_checksum = lax.psum(in_terms, "row") / token_total
    state = finish_update(state, product, gated, in_final_gain, in_final)
    width = HEADS * DH
    normed = layer_norm(state, att_norm_gain).astype(jnp.bfloat16)
    projected = jnp.dot(normed, att_qkv, preferred_element_type=jnp.float32)
    queries = (projected[..., 0:width] * DH ** (-0.5)).astype(jnp.bfloat16)
    keys_tile = projected[..., width : 2 * width].astype(jnp.bfloat16)
    values_tile = projected[..., 2 * width : 3 * width].astype(jnp.bfloat16)
    bias_heads = jnp.einsum("rcz,zh->hrc", normed, att_bias, preferred_element_type=jnp.float32)
    gate_att = jax.nn.sigmoid(jnp.dot(normed, att_gate, preferred_element_type=jnp.float32))
    keys_all, values_all = (
        lax.all_gather(keys_tile, "col", axis=1, tiled=True),
        lax.all_gather(values_tile, "col", axis=1, tiled=True),
    )
    bias_rowwise = lax.all_gather(
        bias_heads.astype(jnp.bfloat16), "col", axis=2, tiled=True
    ).astype(bias_heads.dtype)
    bias_pieces = [
        spread(
            bias_rowwise.astype(jnp.bfloat16), "row", col_place * mirror_ratio + sub_index
        ).astype(bias_rowwise.dtype)
        for sub_index in range(mirror_ratio)
    ]
    bias_panel = jnp.concatenate(bias_pieces, axis=1)
    key_bias = jnp.where(token_mask > 0, 0.0, -1000000000.0).astype(jnp.float32)
    query_heads = queries.reshape(tile_rows, tile_cols, HEADS, DH)
    key_heads = keys_all.reshape(tile_rows, token_total, HEADS, DH)
    value_heads = values_all.reshape(tile_rows, token_total, HEADS, DH)
    scores = jnp.einsum(
        "rchd,rkhd->rhck", query_heads, key_heads, preferred_element_type=jnp.float32
    )
    scores = scores + bias_panel[None] + key_bias
    attn_probs = jax.nn.softmax(scores, axis=-1).astype(jnp.bfloat16)
    attended = jnp.einsum(
        "rhck,rkhd->rchd", attn_probs, value_heads, preferred_element_type=jnp.float32
    )
    attended = attended.reshape(tile_rows, tile_cols, width)
    gated_att = (attended * gate_att).astype(jnp.bfloat16)
    state = state + jnp.dot(gated_att, att_out, preferred_element_type=jnp.float32)
    return (state.astype(jnp.bfloat16), out_checksum, in_checksum)


def solution(mesh):
    in_specs = (
        P("row", "col", None),
        P(),
        P(),
        P(),
        P(),
        P(),
        P(),
        P(),
        P(),
        P(),
        P(),
        P(),
        P(),
        P(),
        P(),
        P(),
        P(),
        P(),
        P(),
    )
    out_specs = (P("row", "col", None), P("row", None), P("col", None))
    return jax.shard_map(
        on_device, mesh=mesh, in_specs=in_specs, out_specs=out_specs, check_vma=False
    )
```

profile of v0, /device:TPU:0, one launch (start us, length us, event | category | flops | bytes accessed | tf_op | source)
XLA Modules:
  0.0 1056.0 jit_solution(13048204633825726701)
XLA Ops:
  7.2 0.7 convert_element_type.80
  8.1 1.4 convert_reduce_fusion
  9.5 1.7 fusion.29
  11.2 1.8 convolution_bitcast_fusion.1
  13.0 1.9 fusion.44
  15.0 0.7 all-gather.7.cloned.1.call-update
  15.8 91.5 %all-gather.9.cloned.1.call-done = bf16[64,32,512]{0,2,1:T(8,128)(2,1)} async-done(((bf16[64,32,64]{0,2,1:T(8,128)(2,1)}), bf16[64,32,512]{0,2,1:T(8,128)(2,1)}) %all-gather.9.cloned.1.call-update) | async-done | bytes 2097168 | tf_op jit(solution)/shard_map/all_gather | solution.py:79
  107.3 5.9 broadcast_select_fusion.1
  113.3 1.0 copy-done.4
  114.3 1.8 fusion.25
  116.1 85.2 %all-gather.7.cloned.1.call-done = bf16[64,32,512]{0,2,1:T(8,128)(2,1)} async-done(((bf16[64,32,64]{0,2,1:T(8,128)(2,1)}), bf16[64,32,512]{0,2,1:T(8,128)(2,1)}) %all-gather.7.cloned.1.call-update) | async-done | bytes 2097168 | tf_op jit(solution)/shard_map/all_gather | solution.py:78
  201.2 4.7 copy.58
  205.9 165.0 %all-reduce.10.cloned.1.call-done = (bf16[64,32,512]{0,2,1:T(8,128)(2,1)}, bf16[64,32,512]{0,2,1:T(8,128)(2,1)}) async-done(((bf16[64,32,512]{0,2,1:T(8,128)(2,1)}, bf16[64,32,512]{0,2,1:T(8,128)(2,1)}), (bf16[64,32,512]{0,2,1:T(8,128)(2,1)}, bf16[64,32,512]{0,2,1:T(8,128)(2,1)})) %all-reduce.10.cloned.1.call-update) | async-done | bytes 4194320 | tf_op jit(solution)/shard_map/psum | solution.py:13
  370.9 8.3 pad_maximum_fusion
  379.2 10.1 copy.59
  389.3 3.5 bitcast_reduce_fusion.1
  394.5 0.7 convolution_bitcast_fusion
  395.3 0.9 fusion.34
  396.2 1.0 copy.61
  397.2 1.1 copy.63
  398.6 72.0 %all-gather.11.cloned.1.call-done = bf16[64,512,64]{2,0,1:T(8,128)(2,1)} async-done(((bf16[64,32,64]{2,0,1:T(8,128)(2,1)}), bf16[64,512,64]{2,0,1:T(8,128)(2,1)}) %all-gather.11.cloned.1.call-update) | async-done | bytes 4194320 | tf_op jit(solution)/shard_map/all_gather | solution.py:95
  470.6 9.4 constant_dynamic-slice_fusion
  480.0 9.4 copy.75
  489.5 3.1 broadcast_select_fusion.2
  492.6 1.8 fusion.23
  494.4 49.3 %all-gather.13.cloned.1.call-done = bf16[64,512,64]{2,0,1:T(8,128)(2,1)} async-done(((bf16[64,32,64]{2,0,1:T(8,128)(2,1)}), bf16[64,512,64]{2,0,1:T(8,128)(2,1)}) %all-gather.13.cloned.1.call-update) | async-done | bytes 4194320 | tf_op jit(solution)/shard_map/all_gather | solution.py:96
  543.8 103.9 %all-reduce.6.cloned.1.call-done = bf16[64,512,32]{1,2,0:T(8,128)(2,1)} async-done(((bf16[64,512,32]{1,2,0:T(8,128)(2,1)}), bf16[64,512,32]{1,2,0:T(8,128)(2,1)}) %all-reduce.6.cloned.1.call-update) | async-done | bytes 2097168 | tf_op jit(solution)/shard_map/psum | solution.py:13
  647.7 20.8 %bitcast_reduce_fusion = (f32[32,64]{1,0:T(8,128)S(1)}, f32[64,32,64]{2,1,0:T(8,128)S(1)}) fusion(bf16[64,512,32]{1,2,0:T(8,128)(2,1)} %all-reduce.6.cloned.1.call-done, bf16[64,512,64]{2,0,1:T(8,128)(2,1)} %all-gather.13.cloned.1.call-done), kind=kOutput, calls=%fused_computation.81 | convolution fusion | flops 134346752 | bytes 6823936 | tf_op jit(solution)/shard_map/mki,mkj->mij/dot_general | solution.py:102
  670.3 0.7 fusion.28
  671.2 28.9 %all_gather.27 = bf16[4,32,512]{1,0,2:T(4,128)(2,1)S(1)} all-gather(bf16[4,32,64]{1,0,2:T(4,128)(2,1)S(1)} %copy.69), channel_id=1, replica_groups=mesh['row'=16,'col'=8] {'col'}, dimensions={2}, use_global_device_ids=true | all-gather | bytes 147456 | tf_op jit(solution)/shard_map/all_gather | solution.py:121
  700.4 0.7 broadcast_select_fusion.4
  701.1 2.7 fusion.80
  703.9 2.3 fusion.77
  706.3 0.7 all-gather.15.cloned.1.call-update
  707.0 4.2 fusion.72
  711.3 32.5 %psum.54 = f32[32,64]{1,0:T(8,128)S(1)} all-reduce(f32[32,64]{1,0:T(8,128)S(1)} %bitcast.90), channel_id=1, replica_groups=mesh['row'=16,'col'=8] {'col'}, use_global_device_ids=true, to_apply=%region_17.18 | all-reduce | flops 2048 | bytes 16384 | tf_op jit(solution)/shard_map/psum | solution.py:91
  745.1 1.4 fusion.32
  747.0 65.7 %psum.55 = f32[64,64]{1,0:T(8,128)S(1)} all-reduce(f32[64,64]{1,0:T(8,128)S(1)} %bitcast.89), channel_id=1, replica_groups=mesh['row'=16,'col'=8] {'row'}, use_global_device_ids=true, to_apply=%region_18.19 | all-reduce | flops 4096 | bytes 32768 | tf_op jit(solution)/shard_map/psum | solution.py:107
  813.3 28.5 %all-reduce.8.cloned.1.call-done = (bf16[4,32,512]{2,1,0:T(8,128)(2,1)}, bf16[4,32,512]{2,1,0:T(8,128)(2,1)}) async-done(((bf16[4,32,512]{2,1,0:T(8,128)(2,1)}, bf16[4,32,512]{2,1,0:T(8,128)(2,1)}), (bf16[4,32,512]{2,1,0:T(8,128)(2,1)}, bf16[4,32,512]{2,1,0:T(8,128)(2,1)})) %all-reduce.8.cloned.1.call-update) | async-done | bytes 262160 | tf_op jit(solution)/shard_map/psum | solution.py:13
  841.9 1.0 maximum_convert_fusion
  842.9 92.0 %all-gather.17.cloned.1.call-done = bf16[32,512,128]{2,1,0:T(8,128)(2,1)} async-done(((bf16[32,64,128]{2,1,0:T(8,128)(2,1)}), bf16[32,512,128]{2,1,0:T(8,128)(2,1)}) %all-gather.17.cloned.1.call-update) | async-done | bytes 4194320 | tf_op jit(solution)/shard_map/all_gather | solution.py:118
  934.9 6.5 copy.68
  941.4 11.2 %fusion.81 = (f32[32,4,64]{2,1,0:T(4,128)S(1)}, f32[32,4,64,512]{3,2,1,0:T(8,128)}) fusion(f32[512]{0:T(512)S(1)} %compare_select_fusion, f32[4,64,512]{2,1,0:T(8,128)S(1)} %maximum_convert_fusion, bf16[32,64,4,32]{1,3,2,0:T(8,128)(2,1)S(1)} %bitcast.86, bf16[32,512,4,32]{1,3,2,0:T(8,128)(2,1)} %bitcast.85), kind=kOutput, calls=%fused_computation.135 | convolution fusion | flops 285213184 | bytes 22054912 | tf_op jit(solution)/shard_map/sub | solution.py:139
  952.6 76.3 %all-gather.15.cloned.1.call-done = bf16[32,512,128]{2,1,0:T(8,128)(2,1)} async-done(((bf16[32,64,128]{2,1,0:T(8,128)(2,1)}), bf16[32,512,128]{2,1,0:T(8,128)(2,1)}) %all-gather.15.cloned.1.call-update) | async-done | bytes 4194320 | tf_op jit(solution)/shard_map/all_gather | solution.py:119
  1028.9 6.5 copy.66
  1035.4 9.7 fusion.6
  1045.2 2.2 copy.72
  1047.4 1.7 fusion.21
  (95 shorter events, 7.2 us)
Async XLA Ops:
  7.2 693.9 %copy-start = (bf16[128,384]{1,0:T(8,128)(2,1)S(1)}, bf16[128,384]{1,0:T(8,128)(2,1)}, u32[]{:S(2)}) copy-start(bf16[128,384]{1,0:T(8,128)(2,1)} %param.34) | copy-start | bytes 294916
  7.2 100.1 %all-gather.9.cloned.1.call-start = ((), (), s32[]{:S(2)}) async-start(), calls=%async_computation.1 | async-start | bytes 4718592 | tf_op jit(solution)/shard_map/all_gather | solution.py:79
  15.0 186.3 %all-gather.7.cloned.1.call-start = ((), (), s32[]{:S(2)}) async-start(), calls=%async_computation | async-start | bytes 4718592 | tf_op jit(solution)/shard_map/all_gather | solution.py:78
  15.7 355.2 %all-reduce.10.cloned.1.call-start = ((), (), s32[]{:S(2)}) async-start(), calls=%async_computation.8 | async-start | bytes 16777216 | tf_op jit(solution)/shard_map/psum | solution.py:13
  113.2 1.0 copy-start.4
  113.2 1.0 copy-start.16
  113.2 1.0 copy-start.20
  113.3 357.3 %all-gather.11.cloned.1.call-start = ((), (), s32[]{:S(2)}) async-start(), calls=%async_computation.2 | async-start | bytes 8912896 | tf_op jit(solution)/shard_map/all_gather | solution.py:95
  389.2 3.8 copy-start.17
  389.2 3.9 copy-start.5
  389.2 4.0 copy-start.6
  389.2 4.0 copy-start.9
  392.8 1.7 copy-start.8
  392.8 1.7 copy-start.19
  397.2 146.6 %all-gather.13.cloned.1.call-start = ((), (), s32[]{:S(2)}) async-start(), calls=%async_computation.4 | async-start | bytes 8912896 | tf_op jit(solution)/shard_map/all_gather | solution.py:96
  398.3 249.4 %all-reduce.6.cloned.1.call-start = ((), (), s32[]{:S(2)}) async-start(), calls=%async_computation.3 | async-start | bytes 4194304 | tf_op jit(solution)/shard_map/psum | solution.py:13
  489.5 3.2 copy-start.21
  492.6 349.3 %all-reduce.8.cloned.1.call-start = ((), (), s32[]{:S(2)}) async-start(), calls=%async_computation.7 | async-start | bytes 524288 | tf_op jit(solution)/shard_map/psum | solution.py:13
  494.4 174.4 %copy-start.18 = (f32[64]{0:T(128)S(1)}, f32[64]{0:T(128)}, u32[]{:S(2)}) copy-start(f32[64]{0:T(128)} %param.31) | copy-start | bytes 772
  494.4 174.5 %copy-start.10 = (bf16[64,128]{1,0:T(8,128)(2,1)S(1)}, bf16[64,128]{1,0:T(8,128)(2,1)}, u32[]{:S(2)}) copy-start(bf16[64,128]{1,0:T(8,128)(2,1)} %param.32) | copy-start | bytes 49156
  647.7 21.3 %copy-start.7 = (f32[32,64,128]{2,1,0:T(8,128)S(1)}, f32[32,64,128]{2,1,0:T(8,128)}, u32[]{:S(2)}) copy-start(f32[32,64,128]{2,1,0:T(8,128)} %fusion.23) | copy-start | bytes 3145732
  668.5 1.1 copy-start.2
  668.6 1.8 copy-start.12
  668.6 1.8 copy-start.15
  701.1 5.9 copy-start.13
  701.1 5.9 copy-start.14
  701.1 5.9 copy-start.11
  701.1 43.3 %copy-start.3 = (f32[64,32,64]{2,1,0:T(8,128)S(1)}, f32[64,32,64]{2,1,0:T(8,128)}, u32[]{:S(2)}) copy-start(f32[64,32,64]{2,1,0:T(8,128)} %copy-done.2) | copy-start | bytes 1572868
  703.9 231.0 %all-gather.17.cloned.1.call-start = ((), (), s32[]{:S(2)}) async-start(), calls=%async_computation.6 | async-start | bytes 4718592 | tf_op jit(solution)/shard_map/all_gather | solution.py:118
  706.2 322.7 %all-gather.15.cloned.1.call-start = ((), (), s32[]{:S(2)}) async-start(), calls=%async_computation.5 | async-start | bytes 4718592 | tf_op jit(solution)/shard_map/all_gather | solution.py:119
  1035.4 11.9 %copy-start.22 = (bf16[128,128]{1,0:T(8,128)(2,1)S(1)}, bf16[128,128]{1,0:T(8,128)(2,1)}, u32[]{:S(2)}) copy-start(bf16[128,128]{1,0:T(8,128)(2,1)} %param.37) | copy-start | bytes 98308
  1035.4 11.9 %copy-start.23 = (bf16[128,128]{1,0:T(8,128)(2,1)S(1)}, bf16[128,128]{1,0:T(8,128)(2,1)}, u32[]{:S(2)}) copy-start(bf16[128,128]{1,0:T(8,128)(2,1)} %param.36) | copy-start | bytes 98308
  1045.2 3.9 copy-start.1
Sparse Core Ops, SparseCore 0:
  15.1 92.1 all-gather.8
  109.0 92.2 all-gather.6
  203.8 167.0 all-reduce.9
  397.3 73.2 all-gather.10
  472.9 70.7 all-gather.12
  546.1 101.5 all-reduce.5
  704.0 137.8 all-reduce.7
  844.2 90.6 all-gather.16
  936.7 92.2 all-gather.14
where the time goes:
time: 1070 us; the launch traced here: 1060 us
  waiting for transfers between devices  765 us (71%)
  blocking collectives  127 us (12%)
  matrix products  62.5 us (6%)
  local copies, waits for them, and re-layouts  55.4 us (5%)
  other arithmetic  30.3 us (3%)
  between operations  14.8 us (1%)
    psum x3, waiting for transfers between devices, spread(): return lax.psum(block, axis)  297 us
    all_gather x1, waiting for transfers between devices, on_device(): lax.all_gather(keys_tile, 'col', axis=1, tiled=True)  92 us
    all_gather x1, waiting for transfers between devices, on_device(): lax.all_gather(right_proj, 'col', axis=2, tiled=True)  91.5 us
    all_gather x1, waiting for transfers between devices, on_device(): lax.all_gather(left_proj, 'col', axis=2, tiled=True)  85.2 us
    all_gather x1, waiting for transfers between devices, on_device(): lax.all_gather(values_tile, 'col', axis=1, tiled=True)  76.3 us
    all_gather x1, waiting for transfers between devices, on_device(): lax.all_gather(left_proj, 'row', axis=1, tiled=True)  72 us
    psum x1, blocking collectives, on_device(): in_checksum = lax.psum(in_terms, 'row') / token_total  65.7 us
    all_gather x1, waiting for transfers between devices, on_device(): lax.all_gather(right_proj, 'row', axis=1, tiled=True)  49.3 us
  transfers between devices with their start and end apart: 9, of which 9 were waited for; matrix products, arithmetic and copies ran while one was open for 6% of the time, Pallas kernels for 0%

commit v1 on v0

v1 whole, which is shorter than its diff:
```python
import jax
import jax.numpy as jnp
from jax import lax
from jax.experimental import pallas as pl
from jax.experimental.pallas import tpu as pltpu
from jax.sharding import Mesh, PartitionSpec as P

F32 = jnp.float32
BF16 = jnp.bfloat16
NT = 512
CZ = 128
CM = 64
HEADS = 4
DH = 32
LANES = 128
CHUNKS = NT // LANES
PLANE = ("p", "q")
PARAMS = pltpu.CompilerParams(vmem_limit_bytes=48 * 1024 * 1024)
VMEM = pl.BlockSpec(memory_space=pltpu.VMEM)
SMEM = pl.BlockSpec(memory_space=pltpu.SMEM)


def dot(left, right, left_dim, right_dim):
    return lax.dot_general(
        left, right, (((left_dim,), (right_dim,)), ((), ())), preferred_element_type=F32
    )


def column(row):
    return jnp.transpose(jnp.broadcast_to(row, (8, row.shape[1])))[:, 0:1]


def flipped(weight):
    return jnp.transpose(weight.astype(F32)).astype(BF16)


def eye():
    rows = lax.broadcasted_iota(jnp.int32, (LANES, LANES), 0)
    cols = lax.broadcasted_iota(jnp.int32, (LANES, LANES), 1)
    return jnp.where(rows == cols, 1.0, 0.0).astype(BF16)


def norm(values, gain_col):
    mean = jnp.mean(values, axis=0, keepdims=True)
    centered = values - mean
    variance = jnp.mean(centered * centered, axis=0, keepdims=True)
    return (centered * lax.rsqrt(variance + 1e-05) * gain_col).astype(BF16)


def sigmoid(values):
    return jax.nn.sigmoid(values)


def thirds(values):
    high = values.astype(BF16)
    rest = values - high.astype(F32)
    middle = rest.astype(BF16)
    return high, middle, (rest - middle.astype(F32)).astype(BF16)


def call(kernel, outs, scratch, ins, cost=None):
    return pl.pallas_call(
        kernel,
        out_shape=tuple(jax.ShapeDtypeStruct(shape, kind) for shape, kind in outs),
        in_specs=[SMEM if kind == "s" else VMEM for kind, _ in ins],
        out_specs=tuple(VMEM for _ in outs),
        scratch_shapes=[pltpu.VMEM(shape, kind) for shape, kind in scratch],
        compiler_params=PARAMS,
    )(*[value for _, value in ins])


def first_row():
    return (2 * lax.axis_index("p") + lax.axis_index("core")) * 32


def project_tile(mask_s, mask_v, x, gain, weight, out, stage):
    row0 = first_row()
    shift = lax.rem(NT - 64 * lax.axis_index("q"), NT)
    mask_all = jnp.broadcast_to(mask_v[...].astype(F32), (8, NT))
    col_mask = pltpu.roll(mask_all, shift, 1)[0:1, 0:64]
    gain_col = column(gain[...])
    weight_t = flipped(weight[...])
    unit = eye()
    for group in range(4):
        steps = range(group * 4, group * 4 + 4)
        pieces, masks = [], []
        for s in steps:
            for i in (s, s + 16):
                pieces.append(x[i * 64 : (i + 1) * 64, :])
                masks.append(col_mask * mask_s[row0 + i].astype(F32))
        state = dot(unit, jnp.concatenate(pieces, axis=0), 1, 1)
        mask = jnp.concatenate(masks, axis=1)
        mixed = dot(weight_t, norm(state, gain_col), 1, 0)
        left = sigmoid(mixed[0:CM]) * mixed[CM : 2 * CM] * mask
        right = sigmoid(mixed[2 * CM : 3 * CM]) * mixed[3 * CM : 4 * CM] * mask
        for at, s in enumerate(steps):
            lanes = slice(at * LANES, (at + 1) * LANES)
            stage[pl.ds(s, CM, stride=32), :] = left[:, lanes]
            stage[pl.ds(16 + s, CM, stride=32), :] = right[:, lanes]
    out[...] = stage[...].astype(BF16).reshape(CM, 32, LANES)


def gate_rows(x, gain, weight, state_out, gate_out):
    gain_col = column(gain[...])
    weight_t = flipped(weight[...])
    unit = eye()
    for r in range(4):
        rows = jnp.concatenate([x[q, r] for q in range(8)], axis=0)
        state = dot(unit, rows, 1, 1)
        span = slice(r * NT, (r + 1) * NT)
        state_out[:, span] = state.astype(BF16)
        gate_out[:, span] = sigmoid(dot(weight_t, norm(state, gain_col), 1, 0)).astype(BF16)


def product_rows(mine, other, weights, out, check_out, left, right, stage):
    core = lax.axis_index("core")
    low = lax.broadcasted_iota(jnp.int32, (16, LANES), 1) < 64

    def paired(ref, src, rows):
        first = ref[src, rows, :].astype(F32)
        second = ref[src + 1, rows, :].astype(F32)
        head = jnp.where(low, first, pltpu.roll(second, 64, 1))
        tail = jnp.where(low, pltpu.roll(first, 64, 1), second)
        return jnp.concatenate([head, tail], axis=0).astype(BF16)

    for p in range(8):
        for a in range(CHUNKS):
            lanes = slice(a * LANES, (a + 1) * LANES)
            src = p * 8 + 2 * a
            left[p * 32 : (p + 1) * 32, lanes] = paired(mine, src, slice(0, 16))
            at = pl.multiple_of(p * 64 + core * 32, 32)
            right[pl.ds(at, 32), lanes] = paired(mine, src, slice(16, 32))
            at = pl.multiple_of(p * 64 + (1 - core) * 32, 32)
            right[pl.ds(at, 32), lanes] = paired(other, src, slice(16, 32))
    product = dot(left[...], right[...], 1, 1)
    for chunk in range(CHUNKS):
        stage[pl.ds(chunk, 256, stride=4), :] = product[:, chunk * LANES : (chunk + 1) * LANES]
    out[...] = stage[...].astype(BF16).reshape(64, 16, LANES)
    weight_rows = jnp.broadcast_to(weights[...].astype(F32), (8, NT)).astype(BF16)
    total = sum(dot(part, left[...], 1, 1) for part in thirds(dot(weight_rows, right[...], 1, 0)))
    check_out[...] = total / NT


def update_rows(recv_stage, stride, r, state, gate, final_gain, final_t):
    product = jnp.concatenate(
        [recv_stage[pl.ds(r * 4 + chunk, CM, stride=stride), :] for chunk in range(CHUNKS)], axis=1
    )
    update = dot(final_t, norm(product, final_gain), 1, 0)
    return state + gate.astype(F32) * update


def project_rows(
    mask_s, mask_v, recv, state_in, gate, final_gain, final_weight, gain, weight,
    out, state_out, normed_out, stage, recv_stage,
):
    row0 = first_row() + 4 * lax.axis_index("q")
    mask_all = mask_v[...].astype(F32)
    gain_col = column(gain[...])
    final_col = column(final_gain[...])
    final_t = flipped(final_weight[...])
    weight_t = flipped(weight[...])
    recv_stage[...] = recv[...].astype(F32).reshape(CM * 16, LANES)
    for r in range(4):
        span = slice(r * NT, (r + 1) * NT)
        state = update_rows(
            recv_stage, 16, r, state_in[:, span].astype(F32), gate[:, span], final_col, final_t
        )
        state_out[:, span] = state
        normed = norm(state, gain_col)
        normed_out[:, span] = normed
        mixed = dot(weight_t, normed, 1, 0)
        mask = mask_all * mask_s[row0 + r].astype(F32)
        left = sigmoid(mixed[0:CM]) * mixed[CM : 2 * CM] * mask
        right = sigmoid(mixed[2 * CM : 3 * CM]) * mixed[3 * CM : 4 * CM] * mask
        for chunk in range(CHUNKS):
            lanes = slice(chunk * LANES, (chunk + 1) * LANES)
            stage[pl.ds(r * 8 + chunk, CM, stride=32), :] = left[:, lanes]
            stage[pl.ds(r * 8 + 4 + chunk, CM, stride=32), :] = right[:, lanes]
    out[...] = stage[...].astype(BF16).reshape(CM, 32, LANES)


def gate_only(normed, weight, gate_out):
    weight_t = flipped(weight[...])
    for r in range(4):
        span = slice(r * NT, (r + 1) * NT)
        gate_out[:, span] = sigmoid(dot(weight_t, normed[:, span], 1, 0)).astype(BF16)


def product_cols(mine, other, weights, check_in, out, left, right, product, stage, stage_out):
    core = lax.axis_index("core")
    for side, buf in enumerate((mine, other)):
        stage[...] = buf[...].astype(F32).reshape(64 * 32, LANES)
        rows = slice(side * 256, (side + 1) * 256)
        for chunk in range(CHUNKS):
            lanes = slice(chunk * LANES, (chunk + 1) * LANES)
            left[rows, lanes] = stage[pl.ds(chunk, 256, stride=8), :].astype(BF16)
            right[rows, lanes] = stage[pl.ds(4 + chunk, 256, stride=8), :].astype(BF16)
    product[...] = dot(left[...], right[...], 0, 0)
    for p in range(8):
        rows = product[pl.ds(pl.multiple_of(p * 64 + core * 32, 32), 32), :]
        for chunk in range(CHUNKS):
            stage_out[pl.ds(p * 128 + chunk, 32, stride=4), :] = rows[
                :, chunk * LANES : (chunk + 1) * LANES
            ]
    out[:, 0:16, :] = stage_out[...].astype(BF16).reshape(64, 16, LANES)
    weight_rows = jnp.broadcast_to(weights[...].astype(F32), (8, NT)).astype(BF16)
    total = sum(dot(part, right[...], 1, 0) for part in thirds(dot(weight_rows, left[...], 1, 1)))
    lines = []
    for check, count in ((check_in[...], 2), (total / NT, 4)):
        high = check.astype(BF16).astype(F32)
        for part in (high, check - high):
            lines += [part[0:1, c * LANES : (c + 1) * LANES] for c in range(count)]
    lines.append(jnp.zeros((4, LANES), F32))
    tail = jnp.concatenate(lines, axis=0).astype(BF16)
    out[:, 16:32, :] = jnp.broadcast_to(tail[None], (64, 16, LANES))


def bias_rows(
    recv, state_in, gate, final_gain, final_weight, gain, weight, out, state_out, normed_out,
    recv_stage, bias_stage,
):
    gain_col = column(gain[...])
    final_col = column(final_gain[...])
    final_t = flipped(final_weight[...])
    weight_t = flipped(weight[...])
    recv_stage[...] = recv[...].astype(F32).reshape(CM * 32, LANES)
    for r in range(4):
        span = slice(r * NT, (r + 1) * NT)
        state = update_rows(recv_stage, 32, r, state_in[:, span], gate[:, span], final_col, final_t)
        state_out[:, span] = state
        normed = norm(state, gain_col)
        normed_out[:, span] = normed
        bias = dot(weight_t, normed, 1, 0)
        for chunk in range(CHUNKS):
            bias_stage[pl.ds(r * 16 + chunk, HEADS, stride=4), :] = bias[
                0:HEADS, chunk * LANES : (chunk + 1) * LANES
            ]
    out[...] = jnp.broadcast_to(bias_stage[...].astype(BF16)[None], (64, 64, LANES))


def attention_inputs(
    recv, normed, qkv, gate_weight, query_out, key_out, value_out, gate_out, check_row, check_col,
    recv_stage, turn,
):
    width = HEADS * DH
    qkv_all = qkv[...]
    query_t = flipped(qkv_all[:, 0:width])
    value_t = flipped(qkv_all[:, 2 * width : 3 * width])
    gate_t = flipped(gate_weight[...])
    for r in range(4):
        span = slice(r * NT, (r + 1) * NT)
        rows = normed[:, span]
        query_out[:, span] = (dot(query_t, rows, 1, 0) * DH ** (-0.5)).astype(BF16)
        key_out[span, :] = dot(rows, qkv_all[:, width : 2 * width], 0, 0).astype(BF16)
        value_out[:, span] = dot(value_t, rows, 1, 0).astype(BF16)
        gate_out[:, span] = sigmoid(dot(gate_t, rows, 1, 0))
    recv_stage[...] = recv[:, 16:32, :].astype(F32).reshape(CM * 16, LANES)
    p, q = lax.axis_index("p"), lax.axis_index("q")

    def rows_of(at, gap):
        high = recv_stage[pl.ds(at, CM, stride=16), :]
        return jnp.transpose(high + recv_stage[pl.ds(at + gap, CM, stride=16), :])

    turn[...] = rows_of(p // 4, 2)
    check_row[...] = turn[pl.ds(pl.multiple_of(lax.rem(p, 4) * 32, 32), 32), :]
    turn[...] = rows_of(4 + q // 2, 4)
    check_col[...] = turn[pl.ds(pl.multiple_of(lax.rem(q, 2) * 64, 64), 64), :]


def attend(
    mask_v, mine, other, query, key, value, gate, state, weight, out, bias_stage, bias,
):
    core = lax.axis_index("core")
    bias_stage[core] = mine[...].astype(F32).reshape(64 * 64, LANES)
    bias_stage[1 - core] = other[...].astype(F32).reshape(64 * 64, LANES)
    key_bias = jnp.where(mask_v[...] > 0, 0.0, -1000000000.0).astype(F32)
    for chunk in range(CHUNKS):
        key_col = column(key_bias[:, chunk * LANES : (chunk + 1) * LANES])
        for h in range(HEADS):
            blocks = [
                bias_stage[plane, pl.ds(p * 512 + h * 4 + chunk, 32, stride=16), :]
                for p in range(8)
                for plane in range(2)
            ]
            turned = jnp.transpose(jnp.concatenate(blocks, axis=0))
            bias[h, chunk * LANES : (chunk + 1) * LANES, :] = turned + key_col
    weight_t = flipped(weight[...])

    def one_row(r, carry):
        span = pl.ds(pl.multiple_of(r * NT, NT), NT)
        query_row = query[:, span]
        key_row = key[span, :]
        value_row = value[:, span]
        zeros = jnp.zeros((DH, NT), BF16)
        parts = []
        for h in range(HEADS):
            head = slice(h * DH, (h + 1) * DH)
            masked = jnp.concatenate(
                [query_row[head] if at == h else zeros for at in range(HEADS)], axis=0
            )
            scores = dot(key_row, masked, 1, 0) + bias[h]
            top = jnp.max(scores, axis=0, keepdims=True)
            weights = jnp.exp(scores - top)
            total = jnp.sum(weights, axis=0, keepdims=True)
            parts.append(dot(value_row[head], weights.astype(BF16), 1, 0) / total)
        attended = jnp.concatenate(parts, axis=0) * gate[:, span]
        result = state[:, span] + dot(weight_t, attended.astype(BF16), 1, 0)
        out[:, r, :, :] = jnp.transpose(result).astype(BF16).reshape(8, 64, CZ)
        return carry

    lax.fori_loop(0, 4, one_row, 0)


def swap(values):
    return lax.ppermute(values, "core", [(0, 1), (1, 0)])


def exchange(values, axes):
    return lax.all_to_all(values, axes, 0, 0, tiled=True)


def on_device(
    pair_input,
    token_mask,
    out_check_weights,
    in_check_weights,
    out_norm_gain,
    out_proj,
    out_gate,
    out_final_gain,
    out_final,
    in_norm_gain,
    in_proj,
    in_gate,
    in_final_gain,
    in_final,
    att_norm_gain,
    att_qkv,
    att_bias,
    att_gate,
    att_out,
):
    def row(vector):
        return vector.reshape(1, vector.shape[0])

    tokens = 4 * NT
    mask_v = row(token_mask)
    state_rows = exchange(pair_input.reshape(8, 4, 64, CZ), "q")
    (sent,) = call(
        project_tile,
        [((CM, 32, LANES), BF16)],
        [((CM * 32, LANES), F32)],
        [("s", token_mask), ("v", mask_v), ("v", pair_input.reshape(tokens, CZ)),
         ("v", row(out_norm_gain)), ("v", out_proj)],
    )
    mine = exchange(sent, PLANE)
    state, gate = call(
        gate_rows,
        [((CZ, tokens), BF16), ((CZ, tokens), BF16)],
        [],
        [("v", state_rows), ("v", row(out_norm_gain)), ("v", out_gate)],
    )
    other = swap(mine)
    sent, check_out = call(
        product_rows,
        [((64, 16, LANES), BF16), ((8, 256), F32)],
        [((256, NT), BF16), ((NT, NT), BF16), ((1024, LANES), F32)],
        [("v", mine), ("v", other), ("v", row(out_check_weights))],
    )
    recv = exchange(sent, PLANE)
    sent, state, normed = call(
        project_rows,
        [((CM, 32, LANES), BF16), ((CZ, tokens), F32), ((CZ, tokens), BF16)],
        [((CM * 32, LANES), F32), ((CM * 16, LANES), F32)],
        [("s", token_mask), ("v", mask_v), ("v", recv), ("v", state), ("v", gate),
         ("v", row(out_final_gain)), ("v", out_final), ("v", row(in_norm_gain)), ("v", in_proj)],
    )
    mine = exchange(sent, PLANE)
    (gate,) = call(
        gate_only, [((CZ, tokens), BF16)], [], [("v", normed), ("v", in_gate)]
    )
    other = swap(mine)
    (sent,) = call(
        product_cols,
        [((64, 32, LANES), BF16)],
        [((NT, NT), BF16), ((NT, NT), BF16), ((NT, NT), F32), ((64 * 32, LANES), F32),
         ((1024, LANES), F32)],
        [("v", mine), ("v", other), ("v", row(in_check_weights)), ("v", check_out)],
    )
    recv = exchange(sent, PLANE)
    sent, state, normed = call(
        bias_rows,
        [((64, 64, LANES), BF16), ((CZ, tokens), F32), ((CZ, tokens), BF16)],
        [((CM * 32, LANES), F32), ((64, LANES), F32)],
        [("v", recv), ("v", state), ("v", gate), ("v", row(in_final_gain)), ("v", in_final),
         ("v", row(att_norm_gain)), ("v", att_bias)],
    )
    mine = exchange(sent, PLANE)
    query, key, value, gate, check_row, check_col = call(
        attention_inputs,
        [((CZ, tokens), BF16), ((tokens, CZ), BF16), ((CZ, tokens), BF16), ((CZ, tokens), F32),
         ((32, CM), F32), ((64, CM), F32)],
        [((CM * 16, LANES), F32), ((LANES, CM), F32)],
        [("v", recv), ("v", normed), ("v", att_qkv), ("v", att_gate)],
    )
    other = swap(mine)
    (sent,) = call(
        attend,
        [((8, 4, 64, CZ), BF16)],
        [((2, 64 * 64, LANES), F32), ((HEADS, NT, NT), F32)],
        [("v", mask_v), ("v", mine), ("v", other), ("v", query), ("v", key), ("v", value),
         ("v", gate), ("v", state), ("v", att_out)],
    )
    result = exchange(sent, "q").reshape(32, 64, CZ)
    return result, check_row, check_col


def solution(mesh):
    grid = Mesh(mesh.devices.reshape(8, 2, 8), ("p", "core", "q"))
    tile = P(("p", "core"), "q", None)
    in_specs = (tile,) + (P(),) * 18
    out_specs = (tile, P(("p", "core"), None), P("q", None))
    return jax.shard_map(
        on_device, mesh=grid, in_specs=in_specs, out_specs=out_specs, check_vma=False
    )
```

time: 1070 us -> 159 us (0.15); the launches traced: 1060 us -> 158 us
  waiting for transfers between devices: 765 us -> 32.4 us
  matrix products: 62.5 us -> 0 us
  blocking collectives: 127 us -> 76.3 us
  local copies, waits for them, and re-layouts: 55.4 us -> 6.27 us
  other arithmetic: 30.3 us -> 0 us
  Pallas kernels: 0 us -> 27 us
  starting transfers between devices: 0.54 us -> 15 us
  between operations: 14.8 us -> 0.85 us
    all_gather x6 -> x0, waiting for transfers between devices: 466 us -> none  [the longest x1 92 us: on_device(): lax.all_gather(keys_tile, 'col', axis=1, tiled=True)]
    psum x3 -> x0, waiting for transfers between devices: 297 us -> none  [spread(): return lax.psum(block, axis)]
    psum x2 -> x0, blocking collectives: 98.3 us -> none  [the longest x1 65.7 us: on_device(): in_checksum = lax.psum(in_terms, 'row') / token_total]
    all_to_all x0 -> x4, blocking collectives: none -> 76.3 us  [exchange(): return lax.all_to_all(values, axes, 0, 0, tiled=True)]
    dot_general x14 -> x0, matrix products: 51.3 us -> none  [the longest x1 20.8 us: on_device(): jnp.einsum('mki,mkj->mij', left_panel, right_cols, preferred_element_type...]
    all_to_all x0 -> x3, waiting for transfers between devices: none -> 29.3 us  [exchange(): return lax.all_to_all(values, axes, 0, 0, tiled=True)]
    all_gather x1 -> x0, blocking collectives: 28.9 us -> none  [on_device(): lax.all_gather(bias_heads.astype(jnp.bfloat16), 'col', axis=2, tiled=True)]
    pallas_call x0 -> x9, Pallas kernels: none -> 27 us  [call(): pl.pallas_call(kernel, out_shape=tuple((jax.ShapeDtypeStruct(shape, kind)...]
  transfers between devices with their start and end apart: 9 -> 6, of which waited for: 9 -> 5; matrix products, arithmetic and copies ran while one was open for 6% -> 0% of each run, Pallas kernels for 0% -> 3%
where the time goes in v1:
time: 159 us; the launch traced here: 158 us
  blocking collectives  76.3 us (48%)
  waiting for transfers between devices  32.4 us (20%)
  Pallas kernels  27 us (17%)
  starting transfers between devices  15 us (9%)
  local copies, waits for them, and re-layouts  6.27 us (4%)
    all_to_all x4, blocking collectives, exchange(): return lax.all_to_all(values, axes, 0, 0, tiled=True)  76.3 us
    all_to_all x3, waiting for transfers between devices, exchange(): return lax.all_to_all(values, axes, 0, 0, tiled=True)  29.3 us
    pallas_call x9, Pallas kernels, call(): pl.pallas_call(kernel, out_shape=tuple((jax.ShapeDtypeStruct(shape, kind)...  27 us
    all_to_all x3, starting transfers between devices, exchange(): return lax.all_to_all(values, axes, 0, 0, tiled=True)  14.9 us
    unnamed x44, local copies, waits for them, and re-layouts  6.27 us
  transfers between devices with their start and end apart: 6, of which 5 were waited for; matrix products, arithmetic and copies ran while one was open for 0% of the time, Pallas kernels for 3%

profile of v1, /device:TPU:0, one launch (start us, length us, event | category | flops | bytes accessed | tf_op | source)
XLA Modules:
  0.0 157.9 jit_solution(6474345632799098878)
XLA Ops:
  0.6 0.0 copy-start.6
  0.6 0.0 copy-start.15
  0.7 0.7 copy-done.6
  1.3 0.0 copy-done.15
  1.3 0.8 copy-done.4
  2.2 2.9 %shard_map.202 = bf16[64,32,128]{2,1,0:T(8,128)(2,1)S(1)} custom-call(s32[512]{0:T(512)S(1)} %copy-done.6, s32[1,512]{1,0:T(1,128)S(1)} %bitcast.11, bf16[2048,128]{1,0:T(8,128)(2,1)} %bitcast.1.x, f32[1,128]{1,0:T(1,128)S(1)} %bitcast.16, bf16[128,256]{1,0:T(8,128)(2,1)S(1)} %copy-done.4), custom_call_target="tpu_custom_call" | custom-call | tf_op jit(solution)/shard_map/pallas_call | solution.py:62
  5.1 24.2 %all_to_all.35.mine = bf16[64,32,128]{2,1,0:T(8,128)(2,1)S(1)} all-to-all(bf16[64,32,128]{2,1,0:T(8,128)(2,1)S(1)} %shard_map.202), channel_id=1, replica_groups=mesh['p'=8,'core'=2,'q'=8] {'p','q'}, dimensions={0} | all-to-all | bytes 1048576 | tf_op jit(solution)/shard_map/all_to_all | solution.py:319
  29.3 0.0 collective-permute-start
  29.3 3.6 %all-to-all-start.2 = ((bf16[8,4,64,128]{3,2,1,0:T(8,128)(2,1)}), bf16[8,4,64,128]{3,2,1,0:T(8,128)(2,1)S(1)}, u32[]{:S(2)}, u32[]{:S(2)}) async-start(bf16[8,4,64,128]{3,2,1,0:T(8,128)(2,1)} %bitcast.4), calls=%async_computation.2 | async-start | bytes 1048576 | tf_op jit(solution)/shard_map/all_to_all | solution.py:319
  33.0 0.0 collective-permute-done.other
  33.0 1.4 shard_map.203
  34.3 9.1 %all-to-all-done.2.x = bf16[8,4,64,128]{3,2,1,0:T(8,128)(2,1)S(1)} async-done(((bf16[8,4,64,128]{3,2,1,0:T(8,128)(2,1)}), bf16[8,4,64,128]{3,2,1,0:T(8,128)(2,1)S(1)}, u32[]{:S(2)}, u32[]{:S(2)}) %all-to-all-start.2) | async-done | bytes 524320 | tf_op jit(solution)/shard_map/all_to_all | solution.py:319
  43.4 5.6 %all-to-all-start.1 = ((bf16[64,16,128]{2,1,0:T(8,128)(2,1)}), bf16[64,16,128]{2,1,0:T(8,128)(2,1)S(1)}, u32[]{:S(2)}, u32[]{:S(2)}) async-start(bf16[64,16,128]{2,1,0:T(8,128)(2,1)} %get-tuple-element.19), calls=%async_computation.1 | async-start | bytes 524288 | tf_op jit(solution)/shard_map/all_to_all | solution.py:319
  49.1 0.0 copy-done.8
  49.1 0.0 copy-start.5
  49.1 0.0 copy-start.11
  49.1 1.3 shard_map.204
  50.4 0.0 copy-start.1
  50.4 0.8 copy-done.1
  51.2 8.3 %all-to-all-done.1.recv = bf16[64,16,128]{2,1,0:T(8,128)(2,1)S(1)} async-done(((bf16[64,16,128]{2,1,0:T(8,128)(2,1)}), bf16[64,16,128]{2,1,0:T(8,128)(2,1)S(1)}, u32[]{:S(2)}, u32[]{:S(2)}) %all-to-all-start.1) | async-done | bytes 262176 | tf_op jit(solution)/shard_map/all_to_all | solution.py:319
  59.5 0.6 copy-done.16
  60.1 0.0 copy-done.17
  60.1 1.0 copy-done.2
  61.2 2.7 %shard_map.205 = (bf16[64,32,128]{2,1,0:T(8,128)(2,1)S(1)}, f32[128,2048]{1,0:T(8,128)S(1)}, bf16[128,2048]{1,0:T(8,128)(2,1)S(1)}) custom-call(s32[512]{0:T(512)S(1)} %copy-done.6, s32[1,512]{1,0:T(1,128)S(1)} %bitcast.12, bf16[64,16,128]{2,1,0:T(8,128)(2,1)S(1)} %all-to-all-done.1.recv, bf16[128,2048]{1,0:T(8,128)(2,1)S(1)} %get-tuple-element.20.state_in, ...), custom_call_target="tpu_custom_call" | custom-call | tf_op jit(solution)/shard_map/pallas_call | solution.py:62
  63.9 16.6 %all_to_all.36.mine = bf16[64,32,128]{2,1,0:T(8,128)(2,1)S(1)} all-to-all(bf16[64,32,128]{2,1,0:T(8,128)(2,1)S(1)} %get-tuple-element.22), channel_id=1, replica_groups=mesh['p'=8,'core'=2,'q'=8] {'p','q'}, dimensions={0} | all-to-all | bytes 1048576 | tf_op jit(solution)/shard_map/all_to_all | solution.py:319
  80.5 0.0 collective-permute-start.1
  80.5 1.9 %collective-permute-done.1.other = bf16[64,32,128]{2,1,0:T(8,128)(2,1)S(1)} collective-permute-done((bf16[64,32,128]{2,1,0:T(8,128)(2,1)S(1)}, bf16[64,32,128]{2,1,0:T(8,128)(2,1)S(1)}, u32[]{:S(2)}, u32[]{:S(2)}) %collective-permute-start.1) | collective-permute-done | bytes 524320 | tf_op jit(solution)/shard_map/ppermute | solution.py:315
  82.4 0.0 copy-done.14
  82.5 2.2 %shard_map.206 = bf16[64,32,128]{2,1,0:T(8,128)(2,1)} custom-call(bf16[64,32,128]{2,1,0:T(8,128)(2,1)S(1)} %all_to_all.36.mine, bf16[64,32,128]{2,1,0:T(8,128)(2,1)S(1)} %collective-permute-done.1.other, s32[1,512]{1,0:T(1,128)S(1)} %bitcast.15, f32[8,256]{1,0:T(8,128)S(1)} %get-tuple-element.23.check_in), custom_call_target="tpu_custom_call" | custom-call | tf_op jit(solution)/shard_map/pallas_call | solution.py:62
  84.6 5.7 %all-to-all-start.4 = ((bf16[64,32,128]{2,1,0:T(8,128)(2,1)}), bf16[64,32,128]{2,1,0:T(8,128)(2,1)S(1)}, u32[]{:S(2)}, u32[]{:S(2)}) async-start(bf16[64,32,128]{2,1,0:T(8,128)(2,1)} %shard_map.206), calls=%async_computation.4 | async-start | bytes 1048576 | tf_op jit(solution)/shard_map/all_to_all | solution.py:319
  90.3 0.0 copy-start.9
  90.3 0.1 copy.22.weight
  90.5 0.6 copy-done.9
  91.1 0.3 shard_map.207.gate
  91.4 11.9 %all-to-all-done.4.recv = bf16[64,32,128]{2,1,0:T(8,128)(2,1)S(1)} async-done(((bf16[64,32,128]{2,1,0:T(8,128)(2,1)}), bf16[64,32,128]{2,1,0:T(8,128)(2,1)S(1)}, u32[]{:S(2)}, u32[]{:S(2)}) %all-to-all-start.4) | async-done | bytes 524320 | tf_op jit(solution)/shard_map/all_to_all | solution.py:319
  103.4 0.6 copy-done.18
  104.0 0.0 copy-done.19
  104.0 1.4 shard_map.208
  105.5 0.0 copy-start.3
  105.5 0.0 copy-start.10
  105.5 22.3 %all_to_all.37.mine = bf16[64,64,128]{2,1,0:T(8,128)(2,1)S(1)} all-to-all(bf16[64,64,128]{2,1,0:T(8,128)(2,1)S(1)} %get-tuple-element.26), channel_id=1, replica_groups=mesh['p'=8,'core'=2,'q'=8] {'p','q'}, dimensions={0} | all-to-all | bytes 2097152 | tf_op jit(solution)/shard_map/all_to_all | solution.py:319
  127.7 0.0 collective-permute-start.2
  127.8 0.0 copy-start.7
  127.8 1.4 shard_map.209
  129.2 1.2 collective-permute-done.2.other
  130.4 13.4 %shard_map.210 = bf16[8,4,64,128]{3,2,1,0:T(8,128)(2,1)S(1)} custom-call(s32[1,512]{1,0:T(1,128)S(1)} %bitcast.13, bf16[64,64,128]{2,1,0:T(8,128)(2,1)S(1)} %all_to_all.37.mine, bf16[64,64,128]{2,1,0:T(8,128)(2,1)S(1)} %collective-permute-done.2.other, bf16[128,2048]{1,0:T(8,128)(2,1)S(1)} %get-tuple-element.28.query, ...), custom_call_target="tpu_custom_call" | custom-call | tf_op jit(solution)/shard_map/pallas_call | solution.py:62
  143.8 13.3 %all_to_all.38 = bf16[8,4,64,128]{3,2,1,0:T(8,128)(2,1)S(1)} all-to-all(bf16[8,4,64,128]{3,2,1,0:T(8,128)(2,1)S(1)} %shard_map.210), channel_id=1, replica_groups=mesh['p'=8,'core'=2,'q'=8] {'q'}, dimensions={0} | all-to-all | bytes 1048576 | tf_op jit(solution)/shard_map/all_to_all | solution.py:319
  157.1 0.8 copy.24
  (21 shorter events, 0.0 us)
Async XLA Ops:
  0.6 0.7 copy-start.6
  0.6 0.7 copy-start.15
  1.3 0.8 copy-start.4
  29.3 3.6 %collective-permute-start = (bf16[64,32,128]{2,1,0:T(8,128)(2,1)S(1)}, bf16[64,32,128]{2,1,0:T(8,128)(2,1)S(1)}, u32[]{:S(2)}, u32[]{:S(2)}) collective-permute-start(bf16[64,32,128]{2,1,0:T(8,128)(2,1)S(1)} %all_to_all.35.mine), channel_id=1, source_target_pairs={{0,8},{8,0},{1,9},{9,1},{2,10},{10,2},{3,11},{11,3},{4,12},{12,4},... | collective-permute-start | bytes 1572872 | tf_op jit(solution)/shard_map/ppermute | solution.py:315
  29.3 3.6 %copy-start.13 = (s32[512]{0:T(512)S(1)}, s32[512]{0:T(512)}, u32[]{:S(2)}) copy-start(s32[512]{0:T(512)} %param.21) | copy-start | bytes 6148
  29.3 14.1 %all-to-all-start.2 = ((bf16[8,4,64,128]{3,2,1,0:T(8,128)(2,1)}), bf16[8,4,64,128]{3,2,1,0:T(8,128)(2,1)S(1)}, u32[]{:S(2)}, u32[]{:S(2)}) async-start(bf16[8,4,64,128]{3,2,1,0:T(8,128)(2,1)} %bitcast.4), calls=%async_computation.2 | async-start | bytes 1048576 | tf_op jit(solution)/shard_map/all_to_all | solution.py:319
  43.4 5.7 %copy-start.8 = (bf16[128,128]{1,0:T(8,128)(2,1)S(1)}, bf16[128,128]{1,0:T(8,128)(2,1)}, u32[]{:S(2)}) copy-start(bf16[128,128]{1,0:T(8,128)(2,1)} %weight.7) | copy-start | bytes 98308
  43.4 16.1 %all-to-all-start.1 = ((bf16[64,16,128]{2,1,0:T(8,128)(2,1)}), bf16[64,16,128]{2,1,0:T(8,128)(2,1)S(1)}, u32[]{:S(2)}, u32[]{:S(2)}) async-start(bf16[64,16,128]{2,1,0:T(8,128)(2,1)} %get-tuple-element.19), calls=%async_computation.1 | async-start | bytes 524288 | tf_op jit(solution)/shard_map/all_to_all | solution.py:319
  49.1 10.4 %copy-start.5 = (bf16[128,256]{1,0:T(8,128)(2,1)S(1)}, bf16[128,256]{1,0:T(8,128)(2,1)}, u32[]{:S(2)}) copy-start(bf16[128,256]{1,0:T(8,128)(2,1)} %weight.8) | copy-start | bytes 196612
  49.1 10.4 %copy-start.11 = (bf16[64,128]{1,0:T(8,128)(2,1)S(1)}, bf16[64,128]{1,0:T(8,128)(2,1)}, u32[]{:S(2)}) copy-start(bf16[64,128]{1,0:T(8,128)(2,1)} %final_weight.2) | copy-start | bytes 49156
  50.4 0.8 copy-start.1
  59.5 0.7 copy-start.16
  59.5 0.7 copy-start.17
  60.1 1.0 copy-start.2
  80.5 1.9 %copy-start.14 = (s32[512]{0:T(512)S(1)}, s32[512]{0:T(512)}, u32[]{:S(2)}) copy-start(s32[512]{0:T(512)} %param.22) | copy-start | bytes 6148
  80.5 1.9 %collective-permute-start.1 = (bf16[64,32,128]{2,1,0:T(8,128)(2,1)S(1)}, bf16[64,32,128]{2,1,0:T(8,128)(2,1)S(1)}, u32[]{:S(2)}, u32[]{:S(2)}) collective-permute-start(bf16[64,32,128]{2,1,0:T(8,128)(2,1)S(1)} %all_to_all.36.mine), channel_id=1, source_target_pairs={{0,8},{8,0},{1,9},{9,1},{2,10},{10,2},{3,11},{11,3},{4,12},{12,4},... | collective-permute-start | bytes 1572872 | tf_op jit(solution)/shard_map/ppermute | solution.py:315
  84.6 5.7 %copy-start.20 = (bf16[128,4]{0,1:T(4,128)(2,1)S(1)}, bf16[128,4]{0,1:T(4,128)(2,1)}, u32[]{:S(2)}) copy-start(bf16[128,4]{0,1:T(4,128)(2,1)} %param.35) | copy-start | bytes 3076
  84.6 18.7 %all-to-all-start.4 = ((bf16[64,32,128]{2,1,0:T(8,128)(2,1)}), bf16[64,32,128]{2,1,0:T(8,128)(2,1)S(1)}, u32[]{:S(2)}, u32[]{:S(2)}) async-start(bf16[64,32,128]{2,1,0:T(8,128)(2,1)} %shard_map.206), calls=%async_computation.4 | async-start | bytes 1048576 | tf_op jit(solution)/shard_map/all_to_all | solution.py:319
  90.3 0.8 copy-start.9
  91.1 12.3 %copy-start.12 = (bf16[64,128]{1,0:T(8,128)(2,1)S(1)}, bf16[64,128]{1,0:T(8,128)(2,1)}, u32[]{:S(2)}) copy-start(bf16[64,128]{1,0:T(8,128)(2,1)} %final_weight.3) | copy-start | bytes 49156
  103.4 0.7 copy-start.18
  103.4 0.7 copy-start.19
  105.4 22.3 %copy-start = (f32[128,2048]{1,0:T(8,128)}, f32[128,2048]{1,0:T(8,128)S(1)}, u32[]{:S(2)}) copy-start(f32[128,2048]{1,0:T(8,128)S(1)} %get-tuple-element.32.state) | copy-start | bytes 3145732
  105.5 22.3 %copy-start.3 = (bf16[128,384]{1,0:T(8,128)(2,1)S(1)}, bf16[128,384]{1,0:T(8,128)(2,1)}, u32[]{:S(2)}) copy-start(bf16[128,384]{1,0:T(8,128)(2,1)} %qkv.1) | copy-start | bytes 294916
  105.5 22.3 %copy-start.10 = (bf16[128,128]{1,0:T(8,128)(2,1)S(1)}, bf16[128,128]{1,0:T(8,128)(2,1)}, u32[]{:S(2)}) copy-start(bf16[128,128]{1,0:T(8,128)(2,1)} %gate_weight.1) | copy-start | bytes 98308
  127.7 2.7 %collective-permute-start.2 = (bf16[64,64,128]{2,1,0:T(8,128)(2,1)S(1)}, bf16[64,64,128]{2,1,0:T(8,128)(2,1)S(1)}, u32[]{:S(2)}, u32[]{:S(2)}) collective-permute-start(bf16[64,64,128]{2,1,0:T(8,128)(2,1)S(1)} %all_to_all.37.mine), channel_id=1, source_target_pairs={{0,8},{8,0},{1,9},{9,1},{2,10},{10,2},{3,11},{11,3},{4,12},{12,4},... | collective-permute-start | bytes 3145736 | tf_op jit(solution)/shard_map/ppermute | solution.py:315
  127.8 2.6 %copy-start.7 = (bf16[128,128]{1,0:T(8,128)(2,1)S(1)}, bf16[128,128]{1,0:T(8,128)(2,1)}, u32[]{:S(2)}) copy-start(bf16[128,128]{1,0:T(8,128)(2,1)} %weight.10) | copy-start | bytes 98308

commit v2 on v1

v2 whole, which is shorter than its diff:
```python
import jax
import jax.numpy as jnp
from jax import lax
from jax.experimental import pallas as pl
from jax.experimental.pallas import tpu as pltpu
from jax.sharding import Mesh, PartitionSpec as P

F32 = jnp.float32
BF16 = jnp.bfloat16
NT = 512
CZ = 128
CM = 64
HEADS = 4
DH = 32
LANES = 128
CHUNKS = NT // LANES
PLANE = ("p", "q")
VMEM = pl.BlockSpec(memory_space=pltpu.VMEM)
SMEM = pl.BlockSpec(memory_space=pltpu.SMEM)
HBM = pl.BlockSpec(memory_space=pltpu.HBM)
SPECS = {"s": SMEM, "v": VMEM, "h": HBM, "w": VMEM}
LOG2E = 1.4426950408889634


def dot(left, right, left_dim, right_dim):
    return lax.dot_general(
        left, right, (((left_dim,), (right_dim,)), ((), ())), preferred_element_type=F32
    )


def column(row):
    return jnp.transpose(jnp.broadcast_to(row, (8, row.shape[1])))[:, 0:1]


def flipped(weight):
    return jnp.transpose(weight.astype(F32)).astype(BF16)


def eye():
    rows = lax.broadcasted_iota(jnp.int32, (LANES, LANES), 0)
    cols = lax.broadcasted_iota(jnp.int32, (LANES, LANES), 1)
    return jnp.where(rows == cols, 1.0, 0.0).astype(BF16)


def norm(values, gain_col):
    mean = jnp.mean(values, axis=0, keepdims=True)
    centered = values - mean
    variance = jnp.mean(centered * centered, axis=0, keepdims=True)
    return (centered * lax.rsqrt(variance + 1e-05) * gain_col).astype(BF16)


def sigmoid(values):
    return jax.nn.sigmoid(values)


def thirds(values):
    high = values.astype(BF16)
    rest = values - high.astype(F32)
    middle = rest.astype(BF16)
    return high, middle, (rest - middle.astype(F32)).astype(BF16)


def call(kernel, outs, scratch, ins, mib=48):
    def shape_of(shape, kind, place="v"):
        return (pltpu.HBM if place == "h" else jax.ShapeDtypeStruct)(shape, kind)

    def placed(place, value):
        return pltpu.with_memory_space_constraint(value, pltpu.HBM) if place in "hw" else value

    return pl.pallas_call(
        kernel,
        out_shape=tuple(shape_of(*out) for out in outs),
        in_specs=[SPECS[place] for place, _ in ins],
        out_specs=tuple(HBM if out[2:] == ("h",) else VMEM for out in outs),
        scratch_shapes=[
            pltpu.SemaphoreType.DMA(shape) if kind is None else pltpu.VMEM(shape, kind)
            for shape, kind in scratch
        ],
        compiler_params=pltpu.CompilerParams(vmem_limit_bytes=mib * 1024 * 1024),
    )(*[placed(place, value) for place, value in ins])


def span_of(r):
    return pl.ds(r * NT, NT)


def start(copies):
    for copy in copies:
        copy.start()
    return copies


def wait(copies):
    for copy in copies:
        copy.wait()


def first_row():
    return (2 * lax.axis_index("p") + lax.axis_index("core")) * 32


def project_tile(mask_s, mask_v, x, gain, weight, out, stage):
    row0 = first_row()
    shift = lax.rem(NT - 64 * lax.axis_index("q"), NT)
    mask_all = jnp.broadcast_to(mask_v[...].astype(F32), (8, NT))
    col_mask = pltpu.roll(mask_all, shift, 1)[0:1, 0:64]
    gain_col = column(gain[...])
    weight_t = flipped(weight[...])
    unit = eye()
    for group in range(4):
        steps = range(group * 4, group * 4 + 4)
        pieces, masks = [], []
        for s in steps:
            for i in (s, s + 16):
                pieces.append(x[i * 64 : (i + 1) * 64, :])
                masks.append(col_mask * mask_s[row0 + i].astype(F32))
        state = dot(unit, jnp.concatenate(pieces, axis=0), 1, 1)
        mask = jnp.concatenate(masks, axis=1)
        mixed = dot(weight_t, norm(state, gain_col), 1, 0)
        left = sigmoid(mixed[0:CM]) * mixed[CM : 2 * CM] * mask
        right = sigmoid(mixed[2 * CM : 3 * CM]) * mixed[3 * CM : 4 * CM] * mask
        for at, s in enumerate(steps):
            lanes = slice(at * LANES, (at + 1) * LANES)
            stage[pl.ds(s, CM, stride=32), :] = left[:, lanes]
            stage[pl.ds(16 + s, CM, stride=32), :] = right[:, lanes]
    out[...] = stage[...].astype(BF16).reshape(CM, 32, LANES)


OUT_GATE = slice(0, 128)
IN_PROJ = slice(128, 384)
IN_GATE = slice(384, 512)
QUERY = slice(512, 640)
KEY = slice(640, 768)
VALUE = slice(768, 896)
ATT_GATE = slice(896, 1024)
ATT_OUT = slice(1024, 1152)
BIAS = slice(1152, 1156)
PACKED = 1168


def prepare(
    out_norm_gain, out_gate, out_final_gain, out_final, in_norm_gain, in_proj, in_gate,
    in_final_gain, in_final, att_norm_gain, att_qkv, att_bias, att_gate, att_out,
    packed, finals, gains,
):
    packed[OUT_GATE, :] = flipped(out_gate[...])
    packed[IN_PROJ, :] = flipped(in_proj[...])
    packed[IN_GATE, :] = flipped(in_gate[...])
    packed[QUERY, :] = flipped(att_qkv[:, 0:128])
    packed[KEY, :] = att_qkv[:, 128:256]
    packed[VALUE, :] = flipped(att_qkv[:, 256:384])
    packed[ATT_GATE, :] = flipped(att_gate[...])
    packed[ATT_OUT, :] = flipped(att_out[...])
    turned = jnp.concatenate([flipped(att_bias[...]), jnp.zeros((16 - HEADS, CZ), BF16)], axis=0)
    packed[BIAS.start : PACKED, :] = turned
    finals[:, 0:CM] = flipped(out_final[...])
    finals[:, CM : 2 * CM] = flipped(in_final[...])
    pad = jnp.zeros((1, CM), F32)
    rows = [
        out_norm_gain[...],
        in_norm_gain[...],
        att_norm_gain[...],
        jnp.concatenate([out_final_gain[...], pad], axis=1),
        jnp.concatenate([in_final_gain[...], pad], axis=1),
        jnp.zeros((3, CZ), F32),
    ]
    gains[...] = jnp.transpose(jnp.concatenate(rows, axis=0))


def gate_rows(x, packed, gains, state_out, gate_out):
    gain_col = gains[:, 0:1]
    weight_t = packed[OUT_GATE, :]
    unit = eye()
    for r in range(4):
        rows = jnp.concatenate([x[q, r] for q in range(8)], axis=0)
        state = dot(unit, rows, 1, 1)
        span = slice(r * NT, (r + 1) * NT)
        state_out[:, span] = state.astype(BF16)
        gate_out[:, span] = sigmoid(dot(weight_t, norm(state, gain_col), 1, 0)).astype(BF16)


def product_rows(mine, other, weights, out, check_out, left, right, stage):
    core = lax.axis_index("core")
    low = lax.broadcasted_iota(jnp.int32, (16, LANES), 1) < 64

    def paired(ref, src, rows):
        first = ref[src, rows, :].astype(F32)
        second = ref[src + 1, rows, :].astype(F32)
        head = jnp.where(low, first, pltpu.roll(second, 64, 1))
        tail = jnp.where(low, pltpu.roll(first, 64, 1), second)
        return jnp.concatenate([head, tail], axis=0).astype(BF16)

    for p in range(8):
        for a in range(CHUNKS):
            lanes = slice(a * LANES, (a + 1) * LANES)
            src = p * 8 + 2 * a
            left[p * 32 : (p + 1) * 32, lanes] = paired(mine, src, slice(0, 16))
            at = pl.multiple_of(p * 64 + core * 32, 32)
            right[pl.ds(at, 32), lanes] = paired(mine, src, slice(16, 32))
            at = pl.multiple_of(p * 64 + (1 - core) * 32, 32)
            right[pl.ds(at, 32), lanes] = paired(other, src, slice(16, 32))
    product = dot(left[...], right[...], 1, 1)
    for chunk in range(CHUNKS):
        stage[pl.ds(chunk, 256, stride=4), :] = product[:, chunk * LANES : (chunk + 1) * LANES]
    out[...] = stage[...].astype(BF16).reshape(64, 16, LANES)
    weight_rows = jnp.broadcast_to(weights[...].astype(F32), (8, NT)).astype(BF16)
    total = sum(dot(part, left[...], 1, 1) for part in thirds(dot(weight_rows, right[...], 1, 0)))
    check_out[...] = total / NT


def update_rows(recv_stage, stride, r, state, gate, final_gain, final_t):
    product = jnp.concatenate(
        [recv_stage[pl.ds(r * 4 + chunk, CM, stride=stride), :] for chunk in range(CHUNKS)], axis=1
    )
    update = dot(final_t, norm(product, final_gain), 1, 0)
    return state.astype(F32) + gate.astype(F32) * update


def project_rows(
    mask_s, mask_v, recv, state_in, gate, packed, finals, gains, out, state_out, stage, recv_stage
):
    row0 = first_row() + 4 * lax.axis_index("q")
    mask_all = mask_v[...].astype(F32)
    gain_col = gains[:, 1:2]
    final_col = gains[0:CM, 3:4]
    final_t = finals[:, 0:CM]
    weight_t = packed[IN_PROJ, :]
    recv_stage[...] = recv[...].astype(F32).reshape(CM * 16, LANES)
    for r in range(4):
        span = slice(r * NT, (r + 1) * NT)
        state = update_rows(
            recv_stage, 16, r, state_in[:, span], gate[:, span], final_col, final_t
        )
        state_out[:, span] = state.astype(BF16)
        mixed = dot(weight_t, norm(state, gain_col), 1, 0)
        mask = mask_all * mask_s[row0 + r].astype(F32)
        left = sigmoid(mixed[0:CM]) * mixed[CM : 2 * CM] * mask
        right = sigmoid(mixed[2 * CM : 3 * CM]) * mixed[3 * CM : 4 * CM] * mask
        for chunk in range(CHUNKS):
            lanes = slice(chunk * LANES, (chunk + 1) * LANES)
            stage[pl.ds(r * 8 + chunk, CM, stride=32), :] = left[:, lanes]
            stage[pl.ds(r * 8 + 4 + chunk, CM, stride=32), :] = right[:, lanes]
    out[...] = stage[...].astype(BF16).reshape(CM, 32, LANES)


def gate_only(state, packed, gains, gate_out):
    gain_col = gains[:, 1:2]
    weight_t = packed[IN_GATE, :]
    for r in range(4):
        span = slice(r * NT, (r + 1) * NT)
        normed = norm(state[:, span].astype(F32), gain_col)
        gate_out[:, span] = sigmoid(dot(weight_t, normed, 1, 0)).astype(BF16)


def product_cols(mine, other, weights, check_in, out, left, right, product, stage, stage_out):
    core = lax.axis_index("core")
    for side, buf in enumerate((mine, other)):
        stage[...] = buf[...].astype(F32).reshape(64 * 32, LANES)
        rows = slice(side * 256, (side + 1) * 256)
        for chunk in range(CHUNKS):
            lanes = slice(chunk * LANES, (chunk + 1) * LANES)
            left[rows, lanes] = stage[pl.ds(chunk, 256, stride=8), :].astype(BF16)
            right[rows, lanes] = stage[pl.ds(4 + chunk, 256, stride=8), :].astype(BF16)
    product[...] = dot(left[...], right[...], 0, 0)
    for p in range(8):
        rows = product[pl.ds(pl.multiple_of(p * 64 + core * 32, 32), 32), :]
        for chunk in range(CHUNKS):
            stage_out[pl.ds(p * 128 + chunk, 32, stride=4), :] = rows[
                :, chunk * LANES : (chunk + 1) * LANES
            ]
    out[:, 0:16, :] = stage_out[...].astype(BF16).reshape(64, 16, LANES)
    weight_rows = jnp.broadcast_to(weights[...].astype(F32), (8, NT)).astype(BF16)
    total = sum(dot(part, right[...], 1, 0) for part in thirds(dot(weight_rows, left[...], 1, 1)))
    high = check_in[...].astype(BF16).astype(F32)
    lines = []
    for part, count in ((high, 2), (check_in[...] - high, 2), (total / NT, 4)):
        lines += [part[0:1, c * LANES : (c + 1) * LANES] for c in range(count)]
    tail = jnp.concatenate(lines, axis=0).astype(BF16)
    out[:, 16:24, :] = jnp.broadcast_to(tail[None], (64, 8, LANES))


def bias_rows(
    recv, state_in, gate, packed, finals, gains, out, state_out_h, check_row, check_col,
    recv_stage, bias_stage, turn, state_out, sems,
):
    gain_col = gains[:, 2:3]
    final_col = gains[0:CM, 4:5]
    final_t = finals[:, CM : 2 * CM]
    weight_t = packed[BIAS.start : PACKED, :]
    recv_stage[...] = recv[...].astype(F32).reshape(CM * 24, LANES)
    p, q = lax.axis_index("p"), lax.axis_index("q")

    def rows_of(at):
        return recv_stage[pl.ds(at, CM, stride=24), :]

    turn[0] = jnp.transpose(rows_of(16 + p // 4) + rows_of(18 + p // 4))
    check_row[...] = turn[0, pl.ds(pl.multiple_of(lax.rem(p, 4) * 32, 32), 32), :]
    turn[1] = jnp.transpose(rows_of(20 + q // 2))
    check_col[...] = turn[1, pl.ds(pl.multiple_of(lax.rem(q, 2) * 64, 64), 64), :]
    stores = []
    for r in range(4):
        span = slice(r * NT, (r + 1) * NT)
        state = update_rows(recv_stage, 24, r, state_in[:, span], gate[:, span], final_col, final_t)
        state_out[:, span] = state.astype(BF16)
        copy = pltpu.make_async_copy(
            state_out.at[:, span_of(r)], state_out_h.at[:, span_of(r)], sems.at[r]
        )
        stores += start([copy])
        normed = norm(state, gain_col)
        bias = dot(weight_t, normed, 1, 0) * LOG2E
        for chunk in range(CHUNKS):
            bias_stage[pl.ds(r * 16 + chunk, HEADS, stride=4), :] = bias[
                0:HEADS, chunk * LANES : (chunk + 1) * LANES
            ]
    out[...] = jnp.broadcast_to(bias_stage[...].astype(BF16)[None], (64, 64, LANES))
    wait(stores)


def attention_inputs(
    state, packed, gains, query_h, key_h, value_h, gate_h,
    query_out, key_out, value_out, gate_out, sems,
):
    gain_col = gains[:, 2:3]
    query_t = packed[QUERY, :]
    value_t = packed[VALUE, :]
    gate_t = packed[ATT_GATE, :]
    for r in range(4):
        span = slice(r * NT, (r + 1) * NT)
        rows = norm(state[:, span].astype(F32), gain_col)
        query_out[:, span] = (dot(query_t, rows, 1, 0) * (LOG2E * DH ** (-0.5))).astype(BF16)
        key_out[span, :] = dot(rows, packed[KEY, :], 0, 0).astype(BF16)
        value_out[:, span] = dot(value_t, rows, 1, 0).astype(BF16)
        gate_out[:, span] = sigmoid(dot(gate_t, rows, 1, 0))
    pairs = ((query_out, query_h), (key_out, key_h), (value_out, value_h), (gate_out, gate_h))
    wait(
        start(
            [
                pltpu.make_async_copy(source, target, sems.at[at])
                for at, (source, target) in enumerate(pairs)
            ]
        )
    )


def attend(
    mask_v, mine, other, query_h, key_h, value_h, gate_h, state_h, packed, out,
    bias_stage, bias, query, key, value, gate, state, sems,
):
    pairs = ((query_h, query), (key_h, key), (value_h, value), (gate_h, gate), (state_h, state))
    loads = start(
        [
            pltpu.make_async_copy(source, target, sems.at[at])
            for at, (source, target) in enumerate(pairs)
        ]
    )
    core = lax.axis_index("core")
    bias_stage[core] = mine[...].astype(F32).reshape(64 * 64, LANES)
    bias_stage[1 - core] = other[...].astype(F32).reshape(64 * 64, LANES)
    key_bias = jnp.where(mask_v[...] > 0, 0.0, -1000000000.0 * LOG2E).astype(F32)
    key_cols = [column(key_bias[:, c * LANES : (c + 1) * LANES]) for c in range(CHUNKS)]
    weight_t = packed[ATT_OUT, :]

    def turn_bias(h):
        for chunk in range(CHUNKS):
            blocks = [
                bias_stage[plane, pl.ds(p * 512 + h * 4 + chunk, 32, stride=16), :]
                for p in range(8)
                for plane in range(2)
            ]
            turned = jnp.transpose(jnp.concatenate(blocks, axis=0))
            bias[h, chunk * LANES : (chunk + 1) * LANES, :] = turned + key_cols[chunk]

    def scores(h, query_row, key_row):
        zeros = jnp.zeros((DH, NT), BF16)
        masked = jnp.concatenate(
            [query_row[h * DH : (h + 1) * DH] if at == h else zeros for at in range(HEADS)], axis=0
        )
        return dot(key_row, masked, 1, 0) + bias[h]

    def weighted(h, weights, value_row):
        padded = jnp.concatenate(
            [value_row[h * DH : (h + 1) * DH], jnp.ones((16, NT), BF16)], axis=0
        )
        both = dot(padded, weights.astype(BF16), 1, 0)
        return both[0:DH] / both[DH : DH + 1], both[DH : DH + 1]

    def finish(r, span, parts):
        attended = jnp.concatenate(parts, axis=0) * gate[:, span]
        result = state[:, span].astype(F32) + dot(weight_t, attended.astype(BF16), 1, 0)
        out[:, r, :, :] = jnp.transpose(result).astype(BF16).reshape(8, 64, CZ)

    low = high = jnp.ones((1, NT), F32)
    parts = [[] for _ in range(4)]
    for h in range(HEADS):
        turn_bias(h)
        if h == 0:
            wait(loads)
        for r in range(4):
            span = slice(r * NT, (r + 1) * NT)
            weights = jnp.exp2(scores(h, query[:, span], key[span, :]))
            part, total = weighted(h, weights, value[:, span])
            low, high = jnp.minimum(low, total), jnp.maximum(high, total)
            parts[r].append(part)
    for r in range(4):
        finish(r, slice(r * NT, (r + 1) * NT), parts[r])
    in_range = jnp.logical_and(jnp.min(low) > 1e-25, jnp.max(high) < 1e30)

    @pl.when(jnp.logical_not(in_range))
    def _():
        def one_row(r, carry):
            span = pl.ds(pl.multiple_of(r * NT, NT), NT)
            again = []
            for h in range(HEADS):
                values = scores(h, query[:, span], key[span, :])
                weights = jnp.exp2(values - jnp.max(values, axis=0, keepdims=True))
                again.append(weighted(h, weights, value[:, span])[0])
            finish(r, span, again)
            return carry

        lax.fori_loop(0, 4, one_row, 0)


def swap(values):
    return lax.ppermute(values, "core", [(0, 1), (1, 0)])


def exchange(values, axes):
    return lax.all_to_all(values, axes, 0, 0, tiled=True)


def on_device(
    pair_input,
    token_mask,
    out_check_weights,
    in_check_weights,
    out_norm_gain,
    out_proj,
    out_gate,
    out_final_gain,
    out_final,
    in_norm_gain,
    in_proj,
    in_gate,
    in_final_gain,
    in_final,
    att_norm_gain,
    att_qkv,
    att_bias,
    att_gate,
    att_out,
):
    def row(vector):
        return vector.reshape(1, vector.shape[0])

    tokens = 4 * NT
    mask_v = row(token_mask)
    state_rows = exchange(pair_input.reshape(8, 4, 64, CZ), "q")
    (sent,) = call(
        project_tile,
        [((CM, 32, LANES), BF16)],
        [((CM * 32, LANES), F32)],
        [("s", token_mask), ("v", mask_v), ("v", pair_input.reshape(tokens, CZ)),
         ("v", row(out_norm_gain)), ("v", out_proj)],
    )
    state_rows, sent = lax.optimization_barrier((state_rows, sent))
    mine = exchange(sent, PLANE)
    gain_out, _ = lax.optimization_barrier((row(out_norm_gain), sent))
    packed, finals, gains = call(
        prepare,
        [((PACKED, CZ), BF16), ((CZ, CZ), BF16), ((CZ, 8), F32)],
        [],
        [("v", value) for value in (
            gain_out, out_gate, row(out_final_gain), out_final,
            row(in_norm_gain), in_proj, in_gate, row(in_final_gain), in_final,
            row(att_norm_gain), att_qkv, att_bias, att_gate, att_out,
        )],
    )
    wide = (CZ, tokens)
    state, gate = call(
        gate_rows,
        [(wide, BF16), (wide, BF16)],
        [],
        [("v", state_rows), ("v", packed), ("v", gains)],
    )
    mine, state, gate = lax.optimization_barrier((mine, state, gate))
    other = swap(mine)
    sent, check_out = call(
        product_rows,
        [((64, 16, LANES), BF16), ((8, 256), F32)],
        [((256, NT), BF16), ((NT, NT), BF16), ((1024, LANES), F32)],
        [("v", mine), ("v", other), ("v", row(out_check_weights))],
    )
    recv = exchange(sent, PLANE)
    sent, state = call(
        project_rows,
        [((CM, 32, LANES), BF16), (wide, BF16)],
        [((CM * 32, LANES), F32), ((CM * 16, LANES), F32)],
        [("s", token_mask), ("v", mask_v), ("v", recv), ("v", state), ("v", gate),
         ("v", packed), ("v", finals), ("v", gains)],
    )
    mine = exchange(sent, PLANE)
    (gate,) = call(
        gate_only, [(wide, BF16)], [], [("v", state), ("v", packed), ("v", gains)]
    )
    mine, gate = lax.optimization_barrier((mine, gate))
    other = swap(mine)
    (sent,) = call(
        product_cols,
        [((64, 24, LANES), BF16)],
        [((NT, NT), BF16), ((NT, NT), BF16), ((NT, NT), F32), ((64 * 32, LANES), F32),
         ((1024, LANES), F32)],
        [("v", mine), ("v", other), ("v", row(in_check_weights)), ("v", check_out)],
    )
    recv = exchange(sent, PLANE)
    sent, state, check_row, check_col = call(
        bias_rows,
        [((64, 64, LANES), BF16), (wide, BF16, "h"), ((32, CM), F32), ((64, CM), F32)],
        [((CM * 24, LANES), F32), ((64, LANES), F32), ((2, LANES, CM), F32), (wide, BF16),
         ((4,), None)],
        [("v", recv), ("v", state), ("v", gate), ("v", packed), ("v", finals), ("v", gains)],
    )
    mine = exchange(sent, PLANE)
    query, key, value, gate = call(
        attention_inputs,
        [(wide, BF16, "h"), ((tokens, CZ), BF16, "h"), (wide, BF16, "h"), (wide, F32, "h")],
        [(wide, BF16), ((tokens, CZ), BF16), (wide, BF16), (wide, F32), ((4,), None)],
        [("w", state), ("v", packed), ("v", gains)],
    )
    mine, query = lax.optimization_barrier((mine, query))
    other = swap(mine)
    (sent,) = call(
        attend,
        [((8, 4, 64, CZ), BF16)],
        [((2, 64 * 64, LANES), F32), ((HEADS, NT, NT), F32), (wide, BF16), ((tokens, CZ), BF16),
         (wide, BF16), (wide, F32), (wide, BF16), ((5,), None)],
        [("v", mask_v), ("v", mine), ("v", other), ("h", query), ("h", key), ("h", value),
         ("h", gate), ("h", state), ("v", packed)],
    )
    result = exchange(sent, "q").reshape(32, 64, CZ)
    return result, check_row, check_col


def solution(mesh):
    grid = Mesh(mesh.devices.reshape(8, 2, 8), ("p", "core", "q"))
    tile = P(("p", "core"), "q", None)
    in_specs = (tile,) + (P(),) * 18
    out_specs = (tile, P(("p", "core"), None), P("q", None))
    return jax.shard_map(
        on_device, mesh=grid, in_specs=in_specs, out_specs=out_specs, check_vma=False
    )
```

time: 159 us -> 157 us (0.987)
  blocking collectives: 76.3 us -> 46.3 us
  waiting for transfers between devices: 32.4 us -> 46.6 us
  starting transfers between devices: 15 us -> 25.6 us
  Pallas kernels: 27 us -> 34.3 us
  local copies, waits for them, and re-layouts: 6.27 us -> 2.25 us
    all_to_all x4 -> x3, blocking collectives: 76.3 us -> 46.3 us  [exchange(): return lax.all_to_all(values, axes, 0, 0, tiled=True)]
    all_to_all x3 -> x4, waiting for transfers between devices: 29.3 us -> 40.1 us  [exchange(): return lax.all_to_all(values, axes, 0, 0, tiled=True)]
    all_to_all x3 -> x4, starting transfers between devices: 14.9 us -> 25.6 us  [exchange(): return lax.all_to_all(values, axes, 0, 0, tiled=True)]
    pallas_call x9 -> x10, Pallas kernels: 27 us -> 34.3 us  [call(): pl.pallas_call(kernel, out_shape=tuple((shape_of(*out) for out in outs)),...]
    unnamed x44 -> x40, local copies, waits for them, and re-layouts: 6.27 us -> 2.25 us
    ppermute x3, waiting for transfers between devices: 3.14 us -> 6.47 us  [swap(): return lax.ppermute(values, 'core', [(0, 1), (1, 0)])]
  transfers between devices with their start and end apart: 6 -> 7, of which waited for: 5 -> 7; matrix products, arithmetic and copies ran while one was open for 0% -> 0% of each run, Pallas kernels for 3% -> 6%
where the time goes in v2:
time: 157 us; the launch traced here: 156 us
  waiting for transfers between devices  46.6 us (30%)
  blocking collectives  46.3 us (29%)
  Pallas kernels  34.3 us (22%)
  starting transfers between devices  25.6 us (16%)
  local copies, waits for them, and re-layouts  2.25 us (1%)
    all_to_all x3, blocking collectives, exchange(): return lax.all_to_all(values, axes, 0, 0, tiled=True)  46.3 us
    all_to_all x4, waiting for transfers between devices, exchange(): return lax.all_to_all(values, axes, 0, 0, tiled=True)  40.1 us
    pallas_call x10, Pallas kernels, call(): pl.pallas_call(kernel, out_shape=tuple((shape_of(*out) for out in outs)),...  34.3 us
    all_to_all x4, starting transfers between devices, exchange(): return lax.all_to_all(values, axes, 0, 0, tiled=True)  25.6 us
    ppermute x3, waiting for transfers between devices, swap(): return lax.ppermute(values, 'core', [(0, 1), (1, 0)])  6.47 us
  transfers between devices with their start and end apart: 7, of which 7 were waited for; matrix products, arithmetic and copies ran while one was open for 0% of the time, Pallas kernels for 6%

profile of v2, /device:TPU:0, one launch (start us, length us, event | category | flops | bytes accessed | tf_op | source)
XLA Modules:
  0.0 156.0 jit_solution(12954893760536873663)
XLA Ops:
  0.6 0.0 copy-start
  0.6 0.0 copy-start.2
  0.6 5.5 %all-to-all-start = ((bf16[8,4,64,128]{3,2,1,0:T(8,128)(2,1)}), bf16[8,4,64,128]{3,2,1,0:T(8,128)(2,1)S(1)}, u32[]{:S(2)}, u32[]{:S(2)}) async-start(bf16[8,4,64,128]{3,2,1,0:T(8,128)(2,1)} %bitcast.11), calls=%async_computation | async-start | bytes 1048576 | tf_op jit(solution)/shard_map/all_to_all | solution.py:428
  6.2 0.0 copy-start.13
  6.2 0.0 copy-done
  6.2 0.0 copy-done.2
  6.2 0.6 copy-done.4
  6.9 3.2 %shard_map.202 = bf16[64,32,128]{2,1,0:T(8,128)(2,1)} custom-call(s32[512]{0:T(512)S(1)} %copy-done.4, s32[1,512]{1,0:T(1,128)S(1)} %bitcast.13, bf16[2048,128]{1,0:T(8,128)(2,1)S(1)} %bitcast.12, f32[1,128]{1,0:T(1,128)S(1)} %bitcast.18, bf16[128,256]{1,0:T(8,128)(2,1)S(1)} %copy-done.2), custom_call_target="tpu_custom_call" | custom-call | tf_op jit(solution)/shard_map/pallas_call | solution.py:70
  10.1 5.5 %all-to-all-done.x = bf16[8,4,64,128]{3,2,1,0:T(8,128)(2,1)S(1)} async-done(((bf16[8,4,64,128]{3,2,1,0:T(8,128)(2,1)}), bf16[8,4,64,128]{3,2,1,0:T(8,128)(2,1)S(1)}, u32[]{:S(2)}, u32[]{:S(2)}) %all-to-all-start) | async-done | bytes 524320 | tf_op jit(solution)/shard_map/all_to_all | solution.py:428
  15.7 0.0 copy-start.8
  15.7 0.0 copy-start.9
  15.7 0.0 copy-start.10
  15.7 9.7 %all-to-all-start.1 = ((bf16[64,32,128]{2,1,0:T(8,128)(2,1)}), bf16[64,32,128]{2,1,0:T(8,128)(2,1)S(1)}, u32[]{:S(2)}, u32[]{:S(2)}) async-start(bf16[64,32,128]{2,1,0:T(8,128)(2,1)} %shard_map.202), calls=%async_computation.1 | async-start | bytes 1048576 | tf_op jit(solution)/shard_map/all_to_all | solution.py:428
  25.4 0.0 copy-start.5
  25.4 0.0 copy-start.17
  25.5 0.1 copy.22.att_bias
  25.6 0.0 copy-start.15
  25.6 0.0 copy-start.16
  25.7 0.5 copy-done.5
  26.2 0.1 copy-done.14
  26.3 0.0 copy-done.15
  26.3 0.0 copy-done.16
  26.3 0.3 shard_map.203
  26.6 1.2 shard_map.204
  27.8 9.8 %all-to-all-done.1.mine = bf16[64,32,128]{2,1,0:T(8,128)(2,1)S(1)} async-done(((bf16[64,32,128]{2,1,0:T(8,128)(2,1)}), bf16[64,32,128]{2,1,0:T(8,128)(2,1)S(1)}, u32[]{:S(2)}, u32[]{:S(2)}) %all-to-all-start.1) | async-done | bytes 524320 | tf_op jit(solution)/shard_map/all_to_all | solution.py:428
  37.6 0.0 collective-permute-start
  37.6 1.9 %collective-permute-done.other = bf16[64,32,128]{2,1,0:T(8,128)(2,1)S(1)} collective-permute-done((bf16[64,32,128]{2,1,0:T(8,128)(2,1)S(1)}, bf16[64,32,128]{2,1,0:T(8,128)(2,1)S(1)}, u32[]{:S(2)}, u32[]{:S(2)}) %collective-permute-start) | collective-permute-done | bytes 524320 | tf_op jit(solution)/shard_map/ppermute | solution.py:424
  39.6 1.1 shard_map.205
  40.7 15.9 %all_to_all.35.recv = bf16[64,16,128]{2,1,0:T(8,128)(2,1)S(1)} all-to-all(bf16[64,16,128]{2,1,0:T(8,128)(2,1)S(1)} %get-tuple-element.38), channel_id=1, replica_groups=mesh['p'=8,'core'=2,'q'=8] {'p','q'}, dimensions={0} | all-to-all | bytes 524288 | tf_op jit(solution)/shard_map/all_to_all | solution.py:428
  56.5 3.5 %shard_map.206 = (bf16[64,32,128]{2,1,0:T(8,128)(2,1)}, bf16[128,2048]{1,0:T(8,128)(2,1)S(1)}) custom-call(s32[512]{0:T(512)S(1)} %copy-done.4, s32[1,512]{1,0:T(1,128)S(1)} %bitcast.14, bf16[64,16,128]{2,1,0:T(8,128)(2,1)S(1)} %all_to_all.35.recv, bf16[128,2048]{1,0:T(8,128)(2,1)S(1)} %get-tuple-element.39.state_in, ...), custom_call_target="tpu_custom_call" | custom-call | tf_op jit(solution)/shard_map/pallas_call | solution.py:70
  60.0 5.1 %all-to-all-start.3 = ((bf16[64,32,128]{2,1,0:T(8,128)(2,1)}), bf16[64,32,128]{2,1,0:T(8,128)(2,1)S(1)}, u32[]{:S(2)}, u32[]{:S(2)}) async-start(bf16[64,32,128]{2,1,0:T(8,128)(2,1)} %get-tuple-element.42), calls=%async_computation.3 | async-start | bytes 1048576 | tf_op jit(solution)/shard_map/all_to_all | solution.py:428
  65.1 0.6 shard_map.207.gate
  65.7 0.0 copy-start.12
  65.7 11.3 %all-to-all-done.3.mine = bf16[64,32,128]{2,1,0:T(8,128)(2,1)S(1)} async-done(((bf16[64,32,128]{2,1,0:T(8,128)(2,1)}), bf16[64,32,128]{2,1,0:T(8,128)(2,1)S(1)}, u32[]{:S(2)}, u32[]{:S(2)}) %all-to-all-start.3) | async-done | bytes 524320 | tf_op jit(solution)/shard_map/all_to_all | solution.py:428
  77.0 0.0 collective-permute-start.1
  77.0 1.9 %collective-permute-done.1.other = bf16[64,32,128]{2,1,0:T(8,128)(2,1)S(1)} collective-permute-done((bf16[64,32,128]{2,1,0:T(8,128)(2,1)S(1)}, bf16[64,32,128]{2,1,0:T(8,128)(2,1)S(1)}, u32[]{:S(2)}, u32[]{:S(2)}) %collective-permute-start.1) | collective-permute-done | bytes 524320 | tf_op jit(solution)/shard_map/ppermute | solution.py:424
  78.9 0.0 copy-done.12
  79.0 1.4 shard_map.208
  80.3 17.2 %all_to_all.36.recv = bf16[64,24,128]{2,1,0:T(8,128)(2,1)S(1)} all-to-all(bf16[64,24,128]{2,1,0:T(8,128)(2,1)S(1)} %shard_map.208), channel_id=1, replica_groups=mesh['p'=8,'core'=2,'q'=8] {'p','q'}, dimensions={0} | all-to-all | bytes 786432 | tf_op jit(solution)/shard_map/all_to_all | solution.py:428
  97.5 2.8 %shard_map.209 = (bf16[64,64,128]{2,1,0:T(8,128)(2,1)}, bf16[128,2048]{1,0:T(8,128)(2,1)}, f32[32,64]{1,0:T(8,128)}, f32[64,64]{1,0:T(8,128)}) custom-call(bf16[64,24,128]{2,1,0:T(8,128)(2,1)S(1)} %all_to_all.36.recv, bf16[128,2048]{1,0:T(8,128)(2,1)S(1)} %get-tuple-element.43.state.state_in, bf16[128,2048]{1,0:T(8,128)(2,1)S(1)} %shard_map.207.gate, ...), custom_call_target="tpu_custom_call" | custom-call | tf_op jit(solution)/shard_map/pallas_call | solution.py:70
  100.3 5.2 %all-to-all-start.5 = ((bf16[64,64,128]{2,1,0:T(8,128)(2,1)}), bf16[64,64,128]{2,1,0:T(8,128)(2,1)S(1)}, u32[]{:S(2)}, u32[]{:S(2)}) async-start(bf16[64,64,128]{2,1,0:T(8,128)(2,1)} %get-tuple-element.47), calls=%async_computation.5 | async-start | bytes 2097152 | tf_op jit(solution)/shard_map/all_to_all | solution.py:428
  105.5 3.4 %shard_map.210 = (bf16[128,2048]{1,0:T(8,128)(2,1)}, bf16[2048,128]{1,0:T(8,128)(2,1)}, bf16[128,2048]{1,0:T(8,128)(2,1)}, f32[128,2048]{1,0:T(8,128)}) custom-call(bf16[128,2048]{1,0:T(8,128)(2,1)} %get-tuple-element.48.state.state_h, bf16[1168,128]{1,0:T(8,128)(2,1)S(1)} %get-tuple-element.33.packed, f32[128,8]{1,0:T(8,128)S(1)} %get-tuple-element.34.gains), custom_call_target="tpu_custom_call" | custom-call | tf_op jit(solution)/shard_map/pallas_call | solution.py:70
  108.9 13.5 %all-to-all-done.5.mine = bf16[64,64,128]{2,1,0:T(8,128)(2,1)S(1)} async-done(((bf16[64,64,128]{2,1,0:T(8,128)(2,1)}), bf16[64,64,128]{2,1,0:T(8,128)(2,1)S(1)}, u32[]{:S(2)}, u32[]{:S(2)}) %all-to-all-start.5) | async-done | bytes 1048608 | tf_op jit(solution)/shard_map/all_to_all | solution.py:428
  122.4 0.0 collective-permute-start.2
  122.4 2.7 %collective-permute-done.2.other = bf16[64,64,128]{2,1,0:T(8,128)(2,1)S(1)} collective-permute-done((bf16[64,64,128]{2,1,0:T(8,128)(2,1)S(1)}, bf16[64,64,128]{2,1,0:T(8,128)(2,1)S(1)}, u32[]{:S(2)}, u32[]{:S(2)}) %collective-permute-start.2) | collective-permute-done | bytes 1048608 | tf_op jit(solution)/shard_map/ppermute | solution.py:424
  125.1 16.8 %shard_map.211 = bf16[8,4,64,128]{3,2,1,0:T(8,128)(2,1)S(1)} custom-call(s32[1,512]{1,0:T(1,128)S(1)} %bitcast.15, bf16[64,64,128]{2,1,0:T(8,128)(2,1)S(1)} %all-to-all-done.5.mine, bf16[64,64,128]{2,1,0:T(8,128)(2,1)S(1)} %collective-permute-done.2.other, bf16[128,2048]{1,0:T(8,128)(2,1)} %get-tuple-element.51.query_h, ...), custom_call_target="tpu_custom_call" | custom-call | tf_op jit(solution)/shard_map/pallas_call | solution.py:70
  141.9 13.3 %all_to_all.37 = bf16[8,4,64,128]{3,2,1,0:T(8,128)(2,1)S(1)} all-to-all(bf16[8,4,64,128]{3,2,1,0:T(8,128)(2,1)S(1)} %shard_map.211), channel_id=1, replica_groups=mesh['p'=8,'core'=2,'q'=8] {'q'}, dimensions={0} | all-to-all | bytes 1048576 | tf_op jit(solution)/shard_map/all_to_all | solution.py:428
  155.2 0.8 copy.24
  (19 shorter events, 0.0 us)
Async XLA Ops:
  0.6 5.6 %copy-start = (bf16[32,64,128]{2,1,0:T(8,128)(2,1)S(1)}, bf16[32,64,128]{2,1,0:T(8,128)(2,1)}, u32[]{:S(2)}) copy-start(bf16[32,64,128]{2,1,0:T(8,128)(2,1)} %param.19) | copy-start | bytes 1572868
  0.6 5.6 %copy-start.2 = (bf16[128,256]{1,0:T(8,128)(2,1)S(1)}, bf16[128,256]{1,0:T(8,128)(2,1)}, u32[]{:S(2)}) copy-start(bf16[128,256]{1,0:T(8,128)(2,1)} %weight.1) | copy-start | bytes 196612
  0.6 15.0 %all-to-all-start = ((bf16[8,4,64,128]{3,2,1,0:T(8,128)(2,1)}), bf16[8,4,64,128]{3,2,1,0:T(8,128)(2,1)S(1)}, u32[]{:S(2)}, u32[]{:S(2)}) async-start(bf16[8,4,64,128]{3,2,1,0:T(8,128)(2,1)} %bitcast.11), calls=%async_computation | async-start | bytes 1048576 | tf_op jit(solution)/shard_map/all_to_all | solution.py:428
  6.2 0.7 copy-start.4
  6.2 0.7 copy-start.13
  10.1 15.3 %copy-start.18 = (bf16[128,4]{0,1:T(4,128)(2,1)S(1)}, bf16[128,4]{0,1:T(4,128)(2,1)}, u32[]{:S(2)}) copy-start(bf16[128,4]{0,1:T(4,128)(2,1)} %param.35) | copy-start | bytes 3076
  15.7 10.0 %copy-start.1 = (bf16[128,384]{1,0:T(8,128)(2,1)S(1)}, bf16[128,384]{1,0:T(8,128)(2,1)}, u32[]{:S(2)}) copy-start(bf16[128,384]{1,0:T(8,128)(2,1)} %att_qkv.1) | copy-start | bytes 294916
  15.7 10.0 %copy-start.3 = (bf16[128,256]{1,0:T(8,128)(2,1)S(1)}, bf16[128,256]{1,0:T(8,128)(2,1)}, u32[]{:S(2)}) copy-start(bf16[128,256]{1,0:T(8,128)(2,1)} %in_proj.1) | copy-start | bytes 196612
  15.7 10.0 %copy-start.6 = (bf16[128,128]{1,0:T(8,128)(2,1)S(1)}, bf16[128,128]{1,0:T(8,128)(2,1)}, u32[]{:S(2)}) copy-start(bf16[128,128]{1,0:T(8,128)(2,1)} %in_gate.1) | copy-start | bytes 98308
  15.7 10.0 %copy-start.7 = (bf16[128,128]{1,0:T(8,128)(2,1)S(1)}, bf16[128,128]{1,0:T(8,128)(2,1)}, u32[]{:S(2)}) copy-start(bf16[128,128]{1,0:T(8,128)(2,1)} %att_gate.1) | copy-start | bytes 98308
  15.7 10.0 %copy-start.8 = (bf16[128,128]{1,0:T(8,128)(2,1)S(1)}, bf16[128,128]{1,0:T(8,128)(2,1)}, u32[]{:S(2)}) copy-start(bf16[128,128]{1,0:T(8,128)(2,1)} %att_out.1) | copy-start | bytes 98308
  15.7 10.0 %copy-start.9 = (bf16[64,128]{1,0:T(8,128)(2,1)S(1)}, bf16[64,128]{1,0:T(8,128)(2,1)}, u32[]{:S(2)}) copy-start(bf16[64,128]{1,0:T(8,128)(2,1)} %out_final.1) | copy-start | bytes 49156
  15.7 10.0 %copy-start.10 = (bf16[64,128]{1,0:T(8,128)(2,1)S(1)}, bf16[64,128]{1,0:T(8,128)(2,1)}, u32[]{:S(2)}) copy-start(bf16[64,128]{1,0:T(8,128)(2,1)} %in_final.1) | copy-start | bytes 49156
  15.7 21.9 %all-to-all-start.1 = ((bf16[64,32,128]{2,1,0:T(8,128)(2,1)}), bf16[64,32,128]{2,1,0:T(8,128)(2,1)S(1)}, u32[]{:S(2)}, u32[]{:S(2)}) async-start(bf16[64,32,128]{2,1,0:T(8,128)(2,1)} %shard_map.202), calls=%async_computation.1 | async-start | bytes 1048576 | tf_op jit(solution)/shard_map/all_to_all | solution.py:428
  25.4 0.8 copy-start.5
  25.4 0.8 copy-start.17
  25.6 0.7 copy-start.14
  25.6 0.7 copy-start.15
  25.6 0.7 copy-start.16
  37.6 1.9 %copy-start.11 = (s32[512]{0:T(512)S(1)}, s32[512]{0:T(512)}, u32[]{:S(2)}) copy-start(s32[512]{0:T(512)} %param.21) | copy-start | bytes 6148
  37.6 1.9 %collective-permute-start = (bf16[64,32,128]{2,1,0:T(8,128)(2,1)S(1)}, bf16[64,32,128]{2,1,0:T(8,128)(2,1)S(1)}, u32[]{:S(2)}, u32[]{:S(2)}) collective-permute-start(bf16[64,32,128]{2,1,0:T(8,128)(2,1)S(1)} %all-to-all-done.1.mine), channel_id=1, source_target_pairs={{0,8},{8,0},{1,9},{9,1},{2,10},{10,2},{3,11},{11,3},{4,12},{12,4},... | collective-permute-start | bytes 1572872 | tf_op jit(solution)/shard_map/ppermute | solution.py:424
  60.0 17.0 %all-to-all-start.3 = ((bf16[64,32,128]{2,1,0:T(8,128)(2,1)}), bf16[64,32,128]{2,1,0:T(8,128)(2,1)S(1)}, u32[]{:S(2)}, u32[]{:S(2)}) async-start(bf16[64,32,128]{2,1,0:T(8,128)(2,1)} %get-tuple-element.42), calls=%async_computation.3 | async-start | bytes 1048576 | tf_op jit(solution)/shard_map/all_to_all | solution.py:428
  65.7 13.3 %copy-start.12 = (s32[512]{0:T(512)S(1)}, s32[512]{0:T(512)}, u32[]{:S(2)}) copy-start(s32[512]{0:T(512)} %param.22) | copy-start | bytes 6148
  77.0 1.9 %collective-permute-start.1 = (bf16[64,32,128]{2,1,0:T(8,128)(2,1)S(1)}, bf16[64,32,128]{2,1,0:T(8,128)(2,1)S(1)}, u32[]{:S(2)}, u32[]{:S(2)}) collective-permute-start(bf16[64,32,128]{2,1,0:T(8,128)(2,1)S(1)} %all-to-all-done.3.mine), channel_id=1, source_target_pairs={{0,8},{8,0},{1,9},{9,1},{2,10},{10,2},{3,11},{11,3},{4,12},{12,4},... | collective-permute-start | bytes 1572872 | tf_op jit(solution)/shard_map/ppermute | solution.py:424
  100.3 22.1 %all-to-all-start.5 = ((bf16[64,64,128]{2,1,0:T(8,128)(2,1)}), bf16[64,64,128]{2,1,0:T(8,128)(2,1)S(1)}, u32[]{:S(2)}, u32[]{:S(2)}) async-start(bf16[64,64,128]{2,1,0:T(8,128)(2,1)} %get-tuple-element.47), calls=%async_computation.5 | async-start | bytes 2097152 | tf_op jit(solution)/shard_map/all_to_all | solution.py:428
  122.4 2.7 %collective-permute-start.2 = (bf16[64,64,128]{2,1,0:T(8,128)(2,1)S(1)}, bf16[64,64,128]{2,1,0:T(8,128)(2,1)S(1)}, u32[]{:S(2)}, u32[]{:S(2)}) collective-permute-start(bf16[64,64,128]{2,1,0:T(8,128)(2,1)S(1)} %all-to-all-done.5.mine), channel_id=1, source_target_pairs={{0,8},{8,0},{1,9},{9,1},{2,10},{10,2},{3,11},{11,3},{4,12},{12,4},... | collective-permute-start | bytes 3145736 | tf_op jit(solution)/shard_map/ppermute | solution.py:424

commit v3 on v2

--- a/solution.py
+++ b/solution.py
@@ -78,10 +78,6 @@
         ],
         compiler_params=pltpu.CompilerParams(vmem_limit_bytes=mib * 1024 * 1024),
     )(*[placed(place, value) for place, value in ins])
-
-
-def span_of(r):
-    return pl.ds(r * NT, NT)
 
 
 def start(copies):
@@ -138,11 +134,20 @@
 PACKED = 1168
 
 
-def prepare(
-    out_norm_gain, out_gate, out_final_gain, out_final, in_norm_gain, in_proj, in_gate,
-    in_final_gain, in_final, att_norm_gain, att_qkv, att_bias, att_gate, att_out,
-    packed, finals, gains,
-):
+def prepare(*refs):
+    sources, (packed, finals, gains), targets, sems = refs[:14], refs[14:17], refs[17:31], refs[31]
+    wait(
+        start(
+            [
+                pltpu.make_async_copy(source, target, sems.at[at])
+                for at, (source, target) in enumerate(zip(sources, targets))
+            ]
+        )
+    )
+    (
+        out_norm_gain, out_gate, out_final_gain, out_final, in_norm_gain, in_proj, in_gate,
+        in_final_gain, in_final, att_norm_gain, att_qkv, att_bias, att_gate, att_out,
+    ) = targets
     packed[OUT_GATE, :] = flipped(out_gate[...])
     packed[IN_PROJ, :] = flipped(in_proj[...])
     packed[IN_GATE, :] = flipped(in_gate[...])
@@ -151,7 +156,7 @@
     packed[VALUE, :] = flipped(att_qkv[:, 256:384])
     packed[ATT_GATE, :] = flipped(att_gate[...])
     packed[ATT_OUT, :] = flipped(att_out[...])
-    turned = jnp.concatenate([flipped(att_bias[...]), jnp.zeros((16 - HEADS, CZ), BF16)], axis=0)
+    turned = jnp.concatenate([att_bias[...], jnp.zeros((16 - HEADS, CZ), BF16)], axis=0)
     packed[BIAS.start : PACKED, :] = turned
     finals[:, 0:CM] = flipped(out_final[...])
     finals[:, CM : 2 * CM] = flipped(in_final[...])
@@ -280,8 +285,8 @@
 
 
 def bias_rows(
-    recv, state_in, gate, packed, finals, gains, out, state_out_h, check_row, check_col,
-    recv_stage, bias_stage, turn, state_out, sems,
+    recv, state_in, gate, packed, finals, gains, out, state_out, check_row, check_col,
+    recv_stage, bias_stage, turn,
 ):
     gain_col = gains[:, 2:3]
     final_col = gains[0:CM, 4:5]
@@ -297,15 +302,10 @@
     check_row[...] = turn[0, pl.ds(pl.multiple_of(lax.rem(p, 4) * 32, 32), 32), :]
     turn[1] = jnp.transpose(rows_of(20 + q // 2))
     check_col[...] = turn[1, pl.ds(pl.multiple_of(lax.rem(q, 2) * 64, 64), 64), :]
-    stores = []
     for r in range(4):
         span = slice(r * NT, (r + 1) * NT)
         state = update_rows(recv_stage, 24, r, state_in[:, span], gate[:, span], final_col, final_t)
         state_out[:, span] = state.astype(BF16)
-        copy = pltpu.make_async_copy(
-            state_out.at[:, span_of(r)], state_out_h.at[:, span_of(r)], sems.at[r]
-        )
-        stores += start([copy])
         normed = norm(state, gain_col)
         bias = dot(weight_t, normed, 1, 0) * LOG2E
         for chunk in range(CHUNKS):
@@ -313,46 +313,24 @@
                 0:HEADS, chunk * LANES : (chunk + 1) * LANES
             ]
     out[...] = jnp.broadcast_to(bias_stage[...].astype(BF16)[None], (64, 64, LANES))
-    wait(stores)
-
-
-def attention_inputs(
-    state, packed, gains, query_h, key_h, value_h, gate_h,
-    query_out, key_out, value_out, gate_out, sems,
-):
+
+
+def attention_inputs(state, packed, gains, query_out, key_out, value_out, gate_out):
     gain_col = gains[:, 2:3]
-    query_t = packed[QUERY, :]
-    value_t = packed[VALUE, :]
-    gate_t = packed[ATT_GATE, :]
     for r in range(4):
         span = slice(r * NT, (r + 1) * NT)
         rows = norm(state[:, span].astype(F32), gain_col)
-        query_out[:, span] = (dot(query_t, rows, 1, 0) * (LOG2E * DH ** (-0.5))).astype(BF16)
+        query_out[:, span] = (dot(packed[QUERY, :], rows, 1, 0) * (LOG2E * DH ** (-0.5))).astype(
+            BF16
+        )
         key_out[span, :] = dot(rows, packed[KEY, :], 0, 0).astype(BF16)
-        value_out[:, span] = dot(value_t, rows, 1, 0).astype(BF16)
-        gate_out[:, span] = sigmoid(dot(gate_t, rows, 1, 0))
-    pairs = ((query_out, query_h), (key_out, key_h), (value_out, value_h), (gate_out, gate_h))
-    wait(
-        start(
-            [
-                pltpu.make_async_copy(source, target, sems.at[at])
-                for at, (source, target) in enumerate(pairs)
-            ]
-        )
-    )
+        value_out[:, span] = dot(packed[VALUE, :], rows, 1, 0).astype(BF16)
+        gate_out[:, span] = sigmoid(dot(packed[ATT_GATE, :], rows, 1, 0)).astype(BF16)
 
 
 def attend(
-    mask_v, mine, other, query_h, key_h, value_h, gate_h, state_h, packed, out,
-    bias_stage, bias, query, key, value, gate, state, sems,
+    mask_v, mine, other, query, key, value, gate, state, packed, out, bias_stage, bias
 ):
-    pairs = ((query_h, query), (key_h, key), (value_h, value), (gate_h, gate), (state_h, state))
-    loads = start(
-        [
-            pltpu.make_async_copy(source, target, sems.at[at])
-            for at, (source, target) in enumerate(pairs)
-        ]
-    )
     core = lax.axis_index("core")
     bias_stage[core] = mine[...].astype(F32).reshape(64 * 64, LANES)
     bias_stage[1 - core] = other[...].astype(F32).reshape(64 * 64, LANES)
@@ -385,7 +363,7 @@
         return both[0:DH] / both[DH : DH + 1], both[DH : DH + 1]
 
     def finish(r, span, parts):
-        attended = jnp.concatenate(parts, axis=0) * gate[:, span]
+        attended = jnp.concatenate(parts, axis=0) * gate[:, span].astype(F32)
         result = state[:, span].astype(F32) + dot(weight_t, attended.astype(BF16), 1, 0)
         out[:, r, :, :] = jnp.transpose(result).astype(BF16).reshape(8, 64, CZ)
 
@@ -393,8 +371,6 @@
     parts = [[] for _ in range(4)]
     for h in range(HEADS):
         turn_bias(h)
-        if h == 0:
-            wait(loads)
         for r in range(4):
             span = slice(r * NT, (r + 1) * NT)
             weights = jnp.exp2(scores(h, query[:, span], key[span, :]))
@@ -459,21 +435,21 @@
         project_tile,
         [((CM, 32, LANES), BF16)],
         [((CM * 32, LANES), F32)],
-        [("s", token_mask), ("v", mask_v), ("v", pair_input.reshape(tokens, CZ)),
-         ("v", row(out_norm_gain)), ("v", out_proj)],
+        [("s", token_mask), ("w", mask_v), ("w", pair_input.reshape(tokens, CZ)),
+         ("w", row(out_norm_gain)), ("w", out_proj)],
     )
     state_rows, sent = lax.optimization_barrier((state_rows, sent))
     mine = exchange(sent, PLANE)
     gain_out, _ = lax.optimization_barrier((row(out_norm_gain), sent))
+    weights = (
+        gain_out, out_gate, row(out_final_gain), out_final, row(in_norm_gain), in_proj, in_gate,
+        row(in_final_gain), in_final, row(att_norm_gain), att_qkv, att_bias.T, att_gate, att_out,
+    )
     packed, finals, gains = call(
         prepare,
         [((PACKED, CZ), BF16), ((CZ, CZ), BF16), ((CZ, 8), F32)],
-        [],
-        [("v", value) for value in (
-            gain_out, out_gate, row(out_final_gain), out_final,
-            row(in_norm_gain), in_proj, in_gate, row(in_final_gain), in_final,
-            row(att_norm_gain), att_qkv, att_bias, att_gate, att_out,
-        )],
+        [(value.shape, value.dtype) for value in weights] + [((14,), None)],
+        [("h", value) for value in weights],
     )
     wide = (CZ, tokens)
     state, gate = call(
@@ -499,11 +475,12 @@
          ("v", packed), ("v", finals), ("v", gains)],
     )
     mine = exchange(sent, PLANE)
+    mine, state = lax.optimization_barrier((mine, state))
+    other = swap(mine)
     (gate,) = call(
         gate_only, [(wide, BF16)], [], [("v", state), ("v", packed), ("v", gains)]
     )
-    mine, gate = lax.optimization_barrier((mine, gate))
-    other = swap(mine)
+    other, gate = lax.optimization_barrier((other, gate))
     (sent,) = call(
         product_cols,
         [((64, 24, LANES), BF16)],
@@ -514,27 +491,26 @@
     recv = exchange(sent, PLANE)
     sent, state, check_row, check_col = call(
         bias_rows,
-        [((64, 64, LANES), BF16), (wide, BF16, "h"), ((32, CM), F32), ((64, CM), F32)],
-        [((CM * 24, LANES), F32), ((64, LANES), F32), ((2, LANES, CM), F32), (wide, BF16),
-         ((4,), None)],
+        [((64, 64, LANES), BF16), (wide, BF16), ((32, CM), F32), ((64, CM), F32)],
+        [((CM * 24, LANES), F32), ((64, LANES), F32), ((2, LANES, CM), F32)],
         [("v", recv), ("v", state), ("v", gate), ("v", packed), ("v", finals), ("v", gains)],
     )
     mine = exchange(sent, PLANE)
+    mine, state = lax.optimization_barrier((mine, state))
+    other = swap(mine)
     query, key, value, gate = call(
         attention_inputs,
-        [(wide, BF16, "h"), ((tokens, CZ), BF16, "h"), (wide, BF16, "h"), (wide, F32, "h")],
-        [(wide, BF16), ((tokens, CZ), BF16), (wide, BF16), (wide, F32), ((4,), None)],
-        [("w", state), ("v", packed), ("v", gains)],
-    )
-    mine, query = lax.optimization_barrier((mine, query))
-    other = swap(mine)
+        [(wide, BF16), ((tokens, CZ), BF16), (wide, BF16), (wide, BF16)],
+        [],
+        [("v", state), ("v", packed), ("v", gains)],
+    )
+    other, query = lax.optimization_barrier((other, query))
     (sent,) = call(
         attend,
         [((8, 4, 64, CZ), BF16)],
-        [((2, 64 * 64, LANES), F32), ((HEADS, NT, NT), F32), (wide, BF16), ((tokens, CZ), BF16),
-         (wide, BF16), (wide, F32), (wide, BF16), ((5,), None)],
-        [("v", mask_v), ("v", mine), ("v", other), ("h", query), ("h", key), ("h", value),
-         ("h", gate), ("h", state), ("v", packed)],
+        [((2, 64 * 64, LANES), F32), ((HEADS, NT, NT), F32)],
+        [("v", mask_v), ("v", mine), ("v", other), ("v", query), ("v", key), ("v", value),
+         ("v", gate), ("v", state), ("v", packed)],
     )
     result = exchange(sent, "q").reshape(32, 64, CZ)
     return result, check_row, check_col

time: 157 us -> 153 us (0.975)
  blocking collectives: 46.3 us -> 85.1 us
  waiting for transfers between devices: 46.6 us -> 20.1 us
  starting transfers between devices: 25.6 us -> 15 us
  Pallas kernels: 34.3 us -> 30.3 us
    all_to_all x3 -> x5, blocking collectives: 46.3 us -> 85.1 us  [exchange(): return lax.all_to_all(values, axes, 0, 0, tiled=True)]
    all_to_all x4 -> x2, waiting for transfers between devices: 40.1 us -> 15.2 us  [exchange(): return lax.all_to_all(values, axes, 0, 0, tiled=True)]
    all_to_all x4 -> x2, starting transfers between devices: 25.6 us -> 15 us  [exchange(): return lax.all_to_all(values, axes, 0, 0, tiled=True)]
    pallas_call x10, Pallas kernels: 34.3 us -> 30.3 us  [call(): pl.pallas_call(kernel, out_shape=tuple((shape_of(*out) for out in outs)),...]
  transfers between devices with their start and end apart: 7 -> 5, of which waited for: 7 -> 5; matrix products, arithmetic and copies ran while one was open for 0% -> 0% of each run, Pallas kernels for 6% -> 5%
where the time goes in v3:
time: 153 us; the launch traced here: 152 us
  blocking collectives  85.1 us (56%)
  Pallas kernels  30.3 us (20%)
  waiting for transfers between devices  20.1 us (13%)
  starting transfers between devices  15 us (10%)
    all_to_all x5, blocking collectives, exchange(): return lax.all_to_all(values, axes, 0, 0, tiled=True)  85.1 us
    pallas_call x10, Pallas kernels, call(): pl.pallas_call(kernel, out_shape=tuple((shape_of(*out) for out in outs)),...  30.3 us
    all_to_all x2, waiting for transfers between devices, exchange(): return lax.all_to_all(values, axes, 0, 0, tiled=True)  15.2 us
    all_to_all x2, starting transfers between devices, exchange(): return lax.all_to_all(values, axes, 0, 0, tiled=True)  15 us
    ppermute x3, waiting for transfers between devices, swap(): return lax.ppermute(values, 'core', [(0, 1), (1, 0)])  4.92 us
  transfers between devices with their start and end apart: 5, of which 5 were waited for; matrix products, arithmetic and copies ran while one was open for 0% of the time, Pallas kernels for 5%

profile of v3, /device:TPU:0, one launch (start us, length us, event | category | flops | bytes accessed | tf_op | source)
XLA Modules:
  0.0 152.0 jit_solution(762473591707539091)
XLA Ops:
  0.6 5.4 %all-to-all-start = ((bf16[8,4,64,128]{3,2,1,0:T(8,128)(2,1)}), bf16[8,4,64,128]{3,2,1,0:T(8,128)(2,1)S(1)}, u32[]{:S(2)}, u32[]{:S(2)}) async-start(bf16[8,4,64,128]{3,2,1,0:T(8,128)(2,1)} %bitcast.17), calls=%async_computation | async-start | bytes 1048576 | tf_op jit(solution)/shard_map/all_to_all | solution.py:404
  6.0 3.8 %shard_map.202 = bf16[64,32,128]{2,1,0:T(8,128)(2,1)} custom-call(s32[512]{0:T(512)} %mask_s.3, s32[1,512]{1,0:T(1,128)} %bitcast.12, bf16[2048,128]{1,0:T(8,128)(2,1)} %bitcast.18, f32[1,128]{1,0:T(1,128)} %bitcast.20, bf16[128,256]{1,0:T(8,128)(2,1)} %weight.1), custom_call_target="tpu_custom_call" | custom-call | tf_op jit(solution)/shard_map/pallas_call | solution.py:70
  9.8 5.7 %all-to-all-done.x = bf16[8,4,64,128]{3,2,1,0:T(8,128)(2,1)S(1)} async-done(((bf16[8,4,64,128]{3,2,1,0:T(8,128)(2,1)}), bf16[8,4,64,128]{3,2,1,0:T(8,128)(2,1)S(1)}, u32[]{:S(2)}, u32[]{:S(2)}) %all-to-all-start) | async-done | bytes 524320 | tf_op jit(solution)/shard_map/all_to_all | solution.py:404
  15.5 9.6 %all-to-all-start.1 = ((bf16[64,32,128]{2,1,0:T(8,128)(2,1)}), bf16[64,32,128]{2,1,0:T(8,128)(2,1)S(1)}, u32[]{:S(2)}, u32[]{:S(2)}) async-start(bf16[64,32,128]{2,1,0:T(8,128)(2,1)} %shard_map.202), calls=%async_computation.1 | async-start | bytes 1048576 | tf_op jit(solution)/shard_map/all_to_all | solution.py:404
  25.1 1.5 %shard_map.203 = (bf16[1168,128]{1,0:T(8,128)(2,1)S(1)}, bf16[128,128]{1,0:T(8,128)(2,1)S(1)}, f32[128,8]{1,0:T(8,128)S(1)}) custom-call(f32[1,128]{1,0:T(1,128)} %bitcast.21, bf16[128,128]{1,0:T(8,128)(2,1)} %refs_1_.1, f32[1,64]{1,0:T(1,128)} %bitcast.23, bf16[64,128]{1,0:T(8,128)(2,1)} %refs_3_.1, f32[1,128]{1,0:T(1,128)} %bitcast.24, ...), custom_call_target="tpu_custom_call" | custom-call | tf_op jit(solution)/shard_map/pallas_call | solution.py:70
  26.6 1.2 shard_map.204
  27.9 9.4 %all-to-all-done.1.mine = bf16[64,32,128]{2,1,0:T(8,128)(2,1)S(1)} async-done(((bf16[64,32,128]{2,1,0:T(8,128)(2,1)}), bf16[64,32,128]{2,1,0:T(8,128)(2,1)S(1)}, u32[]{:S(2)}, u32[]{:S(2)}) %all-to-all-start.1) | async-done | bytes 524320 | tf_op jit(solution)/shard_map/all_to_all | solution.py:404
  37.3 0.0 copy-start.1
  37.3 0.0 collective-permute-start
  37.3 1.9 %collective-permute-done.other = bf16[64,32,128]{2,1,0:T(8,128)(2,1)S(1)} collective-permute-done((bf16[64,32,128]{2,1,0:T(8,128)(2,1)S(1)}, bf16[64,32,128]{2,1,0:T(8,128)(2,1)S(1)}, u32[]{:S(2)}, u32[]{:S(2)}) %collective-permute-start) | collective-permute-done | bytes 524320 | tf_op jit(solution)/shard_map/ppermute | solution.py:400
  39.2 0.0 copy-done.1
  39.2 1.1 shard_map.205
  40.3 0.0 copy-start
  40.3 16.0 %all_to_all.35.recv = bf16[64,16,128]{2,1,0:T(8,128)(2,1)S(1)} all-to-all(bf16[64,16,128]{2,1,0:T(8,128)(2,1)S(1)} %get-tuple-element.42), channel_id=1, replica_groups=mesh['p'=8,'core'=2,'q'=8] {'p','q'}, dimensions={0} | all-to-all | bytes 524288 | tf_op jit(solution)/shard_map/all_to_all | solution.py:404
  56.3 0.0 copy-done
  56.3 2.7 %shard_map.206 = (bf16[64,32,128]{2,1,0:T(8,128)(2,1)S(1)}, bf16[128,2048]{1,0:T(8,128)(2,1)S(1)}) custom-call(s32[512]{0:T(512)S(1)} %copy-done, s32[1,512]{1,0:T(1,128)S(1)} %bitcast.13, bf16[64,16,128]{2,1,0:T(8,128)(2,1)S(1)} %all_to_all.35.recv, bf16[128,2048]{1,0:T(8,128)(2,1)S(1)} %get-tuple-element.43.state_in, ...), custom_call_target="tpu_custom_call" | custom-call | tf_op jit(solution)/shard_map/pallas_call | solution.py:70
  59.0 16.8 %all_to_all.36.mine = bf16[64,32,128]{2,1,0:T(8,128)(2,1)S(1)} all-to-all(bf16[64,32,128]{2,1,0:T(8,128)(2,1)S(1)} %get-tuple-element.46), channel_id=1, replica_groups=mesh['p'=8,'core'=2,'q'=8] {'p','q'}, dimensions={0} | all-to-all | bytes 1048576 | tf_op jit(solution)/shard_map/all_to_all | solution.py:404
  75.8 0.0 collective-permute-start.1
  75.8 0.6 shard_map.207.gate
  76.4 0.0 copy-start.2
  76.4 1.3 collective-permute-done.1.other
  77.7 0.0 copy-done.2
  77.7 1.4 shard_map.208
  79.1 17.2 %all_to_all.37.recv = bf16[64,24,128]{2,1,0:T(8,128)(2,1)S(1)} all-to-all(bf16[64,24,128]{2,1,0:T(8,128)(2,1)S(1)} %shard_map.208), channel_id=1, replica_groups=mesh['p'=8,'core'=2,'q'=8] {'p','q'}, dimensions={0} | all-to-all | bytes 786432 | tf_op jit(solution)/shard_map/all_to_all | solution.py:404
  96.3 1.9 %shard_map.209 = (bf16[64,64,128]{2,1,0:T(8,128)(2,1)S(1)}, bf16[128,2048]{1,0:T(8,128)(2,1)S(1)}, f32[32,64]{1,0:T(8,128)}, f32[64,64]{1,0:T(8,128)}) custom-call(bf16[64,24,128]{2,1,0:T(8,128)(2,1)S(1)} %all_to_all.37.recv, bf16[128,2048]{1,0:T(8,128)(2,1)S(1)} %get-tuple-element.49.state.state_in, bf16[128,2048]{1,0:T(8,128)(2,1)S(1)} %shard_map.207.gate, ...), custom_call_target="tpu_custom_call" | custom-call | tf_op jit(solution)/shard_map/pallas_call | solution.py:70
  98.2 21.9 %all_to_all.38.mine = bf16[64,64,128]{2,1,0:T(8,128)(2,1)S(1)} all-to-all(bf16[64,64,128]{2,1,0:T(8,128)(2,1)S(1)} %get-tuple-element.53), channel_id=1, replica_groups=mesh['p'=8,'core'=2,'q'=8] {'p','q'}, dimensions={0} | all-to-all | bytes 2097152 | tf_op jit(solution)/shard_map/all_to_all | solution.py:404
  120.1 0.0 collective-permute-start.2
  120.1 1.0 shard_map.210
  121.1 1.7 %collective-permute-done.2.other = bf16[64,64,128]{2,1,0:T(8,128)(2,1)S(1)} collective-permute-done((bf16[64,64,128]{2,1,0:T(8,128)(2,1)S(1)}, bf16[64,64,128]{2,1,0:T(8,128)(2,1)S(1)}, u32[]{:S(2)}, u32[]{:S(2)}) %collective-permute-start.2) | collective-permute-done | bytes 1048608 | tf_op jit(solution)/shard_map/ppermute | solution.py:400
  122.8 15.2 %shard_map.211 = bf16[8,4,64,128]{3,2,1,0:T(8,128)(2,1)S(1)} custom-call(s32[1,512]{1,0:T(1,128)S(1)} %bitcast.14, bf16[64,64,128]{2,1,0:T(8,128)(2,1)S(1)} %all_to_all.38.mine, bf16[64,64,128]{2,1,0:T(8,128)(2,1)S(1)} %collective-permute-done.2.other, bf16[128,2048]{1,0:T(8,128)(2,1)S(1)} %get-tuple-element.59.query, ...), custom_call_target="tpu_custom_call" | custom-call | tf_op jit(solution)/shard_map/pallas_call | solution.py:70
  137.9 13.3 %all_to_all.39 = bf16[8,4,64,128]{3,2,1,0:T(8,128)(2,1)S(1)} all-to-all(bf16[8,4,64,128]{3,2,1,0:T(8,128)(2,1)S(1)} %shard_map.211), channel_id=1, replica_groups=mesh['p'=8,'core'=2,'q'=8] {'q'}, dimensions={0} | all-to-all | bytes 1048576 | tf_op jit(solution)/shard_map/all_to_all | solution.py:404
  151.2 0.8 copy.23
Async XLA Ops:
  0.6 14.9 %all-to-all-start = ((bf16[8,4,64,128]{3,2,1,0:T(8,128)(2,1)}), bf16[8,4,64,128]{3,2,1,0:T(8,128)(2,1)S(1)}, u32[]{:S(2)}, u32[]{:S(2)}) async-start(bf16[8,4,64,128]{3,2,1,0:T(8,128)(2,1)} %bitcast.17), calls=%async_computation | async-start | bytes 1048576 | tf_op jit(solution)/shard_map/all_to_all | solution.py:404
  15.5 21.8 %all-to-all-start.1 = ((bf16[64,32,128]{2,1,0:T(8,128)(2,1)}), bf16[64,32,128]{2,1,0:T(8,128)(2,1)S(1)}, u32[]{:S(2)}, u32[]{:S(2)}) async-start(bf16[64,32,128]{2,1,0:T(8,128)(2,1)} %shard_map.202), calls=%async_computation.1 | async-start | bytes 1048576 | tf_op jit(solution)/shard_map/all_to_all | solution.py:404
  37.3 1.9 %copy-start.1 = (s32[512]{0:T(512)S(1)}, s32[512]{0:T(512)}, u32[]{:S(2)}) copy-start(s32[512]{0:T(512)} %param.21) | copy-start | bytes 6148
  37.3 1.9 %collective-permute-start = (bf16[64,32,128]{2,1,0:T(8,128)(2,1)S(1)}, bf16[64,32,128]{2,1,0:T(8,128)(2,1)S(1)}, u32[]{:S(2)}, u32[]{:S(2)}) collective-permute-start(bf16[64,32,128]{2,1,0:T(8,128)(2,1)S(1)} %all-to-all-done.1.mine), channel_id=1, source_target_pairs={{0,8},{8,0},{1,9},{9,1},{2,10},{10,2},{3,11},{11,3},{4,12},{12,4},... | collective-permute-start | bytes 1572872 | tf_op jit(solution)/shard_map/ppermute | solution.py:400
  40.3 16.0 %copy-start = (s32[512]{0:T(512)S(1)}, s32[512]{0:T(512)}, u32[]{:S(2)}) copy-start(s32[512]{0:T(512)} %mask_s.3) | copy-start | bytes 6148
  75.8 1.9 %collective-permute-start.1 = (bf16[64,32,128]{2,1,0:T(8,128)(2,1)S(1)}, bf16[64,32,128]{2,1,0:T(8,128)(2,1)S(1)}, u32[]{:S(2)}, u32[]{:S(2)}) collective-permute-start(bf16[64,32,128]{2,1,0:T(8,128)(2,1)S(1)} %all_to_all.36.mine), channel_id=1, source_target_pairs={{0,8},{8,0},{1,9},{9,1},{2,10},{10,2},{3,11},{11,3},{4,12},{12,4},... | collective-permute-start | bytes 1572872 | tf_op jit(solution)/shard_map/ppermute | solution.py:400
  76.4 1.3 copy-start.2
  120.1 2.7 %collective-permute-start.2 = (bf16[64,64,128]{2,1,0:T(8,128)(2,1)S(1)}, bf16[64,64,128]{2,1,0:T(8,128)(2,1)S(1)}, u32[]{:S(2)}, u32[]{:S(2)}) collective-permute-start(bf16[64,64,128]{2,1,0:T(8,128)(2,1)S(1)} %all_to_all.38.mine), channel_id=1, source_target_pairs={{0,8},{8,0},{1,9},{9,1},{2,10},{10,2},{3,11},{11,3},{4,12},{12,4},... | collective-permute-start | bytes 3145736 | tf_op jit(solution)/shard_map/ppermute | solution.py:400

commit v4 on v3

--- a/solution.py
+++ b/solution.py
@@ -132,10 +132,15 @@
 ATT_OUT = slice(1024, 1152)
 BIAS = slice(1152, 1156)
 PACKED = 1168
+COUNT = 17
+MASK = slice(0, 1)
+OUT_CHECK = slice(8, 16)
+IN_CHECK = slice(16, 24)
 
 
 def prepare(*refs):
-    sources, (packed, finals, gains), targets, sems = refs[:14], refs[14:17], refs[17:31], refs[31]
+    sources, (packed, finals, gains, lines) = refs[:COUNT], refs[COUNT : COUNT + 4]
+    targets, sems = refs[COUNT + 4 : 2 * COUNT + 4], refs[2 * COUNT + 4]
     wait(
         start(
             [
@@ -147,7 +152,10 @@
     (
         out_norm_gain, out_gate, out_final_gain, out_final, in_norm_gain, in_proj, in_gate,
         in_final_gain, in_final, att_norm_gain, att_qkv, att_bias, att_gate, att_out,
+        mask, out_check, in_check,
     ) = targets
+    for at, line in enumerate((mask, out_check, in_check)):
+        lines[at * 8 : (at + 1) * 8, :] = jnp.broadcast_to(line[...].astype(F32), (8, NT))
     packed[OUT_GATE, :] = flipped(out_gate[...])
     packed[IN_PROJ, :] = flipped(in_proj[...])
     packed[IN_GATE, :] = flipped(in_gate[...])
@@ -184,7 +192,7 @@
         gate_out[:, span] = sigmoid(dot(weight_t, norm(state, gain_col), 1, 0)).astype(BF16)
 
 
-def product_rows(mine, other, weights, out, check_out, left, right, stage):
+def product_rows(mine, other, lines, out, check_out, left, right, stage):
     core = lax.axis_index("core")
     low = lax.broadcasted_iota(jnp.int32, (16, LANES), 1) < 64
 
@@ -208,7 +216,7 @@
     for chunk in range(CHUNKS):
         stage[pl.ds(chunk, 256, stride=4), :] = product[:, chunk * LANES : (chunk + 1) * LANES]
     out[...] = stage[...].astype(BF16).reshape(64, 16, LANES)
-    weight_rows = jnp.broadcast_to(weights[...].astype(F32), (8, NT)).astype(BF16)
+    weight_rows = lines[OUT_CHECK, :].astype(BF16)
     total = sum(dot(part, left[...], 1, 1) for part in thirds(dot(weight_rows, right[...], 1, 0)))
     check_out[...] = total / NT
 
@@ -222,10 +230,10 @@
 
 
 def project_rows(
-    mask_s, mask_v, recv, state_in, gate, packed, finals, gains, out, state_out, stage, recv_stage
+    mask_s, lines, recv, state_in, gate, packed, finals, gains, out, state_out, stage, recv_stage
 ):
     row0 = first_row() + 4 * lax.axis_index("q")
-    mask_all = mask_v[...].astype(F32)
+    mask_all = lines[MASK, :]
     gain_col = gains[:, 1:2]
     final_col = gains[0:CM, 3:4]
     final_t = finals[:, 0:CM]
@@ -257,7 +265,7 @@
         gate_out[:, span] = sigmoid(dot(weight_t, normed, 1, 0)).astype(BF16)
 
 
-def product_cols(mine, other, weights, check_in, out, left, right, product, stage, stage_out):
+def product_cols(mine, other, lines, check_in, out, left, right, product, stage, stage_out):
     core = lax.axis_index("core")
     for side, buf in enumerate((mine, other)):
         stage[...] = buf[...].astype(F32).reshape(64 * 32, LANES)
@@ -274,7 +282,7 @@
                 :, chunk * LANES : (chunk + 1) * LANES
             ]
     out[:, 0:16, :] = stage_out[...].astype(BF16).reshape(64, 16, LANES)
-    weight_rows = jnp.broadcast_to(weights[...].astype(F32), (8, NT)).astype(BF16)
+    weight_rows = lines[IN_CHECK, :].astype(BF16)
     total = sum(dot(part, right[...], 1, 0) for part in thirds(dot(weight_rows, left[...], 1, 1)))
     high = check_in[...].astype(BF16).astype(F32)
     lines = []
@@ -285,23 +293,13 @@
 
 
 def bias_rows(
-    recv, state_in, gate, packed, finals, gains, out, state_out, check_row, check_col,
-    recv_stage, bias_stage, turn,
+    recv, state_in, gate, packed, finals, gains, out, state_out, recv_stage, bias_stage
 ):
     gain_col = gains[:, 2:3]
     final_col = gains[0:CM, 4:5]
     final_t = finals[:, CM : 2 * CM]
     weight_t = packed[BIAS.start : PACKED, :]
     recv_stage[...] = recv[...].astype(F32).reshape(CM * 24, LANES)
-    p, q = lax.axis_index("p"), lax.axis_index("q")
-
-    def rows_of(at):
-        return recv_stage[pl.ds(at, CM, stride=24), :]
-
-    turn[0] = jnp.transpose(rows_of(16 + p // 4) + rows_of(18 + p // 4))
-    check_row[...] = turn[0, pl.ds(pl.multiple_of(lax.rem(p, 4) * 32, 32), 32), :]
-    turn[1] = jnp.transpose(rows_of(20 + q // 2))
-    check_col[...] = turn[1, pl.ds(pl.multiple_of(lax.rem(q, 2) * 64, 64), 64), :]
     for r in range(4):
         span = slice(r * NT, (r + 1) * NT)
         state = update_rows(recv_stage, 24, r, state_in[:, span], gate[:, span], final_col, final_t)
@@ -315,8 +313,21 @@
     out[...] = jnp.broadcast_to(bias_stage[...].astype(BF16)[None], (64, 64, LANES))
 
 
-def attention_inputs(state, packed, gains, query_out, key_out, value_out, gate_out):
+def attention_inputs(
+    recv, state, packed, gains, query_out, key_out, value_out, gate_out, check_row, check_col,
+    recv_stage, turn,
+):
     gain_col = gains[:, 2:3]
+    recv_stage[...] = recv[:, 16:24, :].astype(F32).reshape(CM * 8, LANES)
+    p, q = lax.axis_index("p"), lax.axis_index("q")
+
+    def rows_of(at):
+        return recv_stage[pl.ds(at, CM, stride=8), :]
+
+    turn[0] = jnp.transpose(rows_of(p // 4) + rows_of(2 + p // 4))
+    check_row[...] = turn[0, pl.ds(pl.multiple_of(lax.rem(p, 4) * 32, 32), 32), :]
+    turn[1] = jnp.transpose(rows_of(4 + q // 2))
+    check_col[...] = turn[1, pl.ds(pl.multiple_of(lax.rem(q, 2) * 64, 64), 64), :]
     for r in range(4):
         span = slice(r * NT, (r + 1) * NT)
         rows = norm(state[:, span].astype(F32), gain_col)
@@ -329,12 +340,12 @@
 
 
 def attend(
-    mask_v, mine, other, query, key, value, gate, state, packed, out, bias_stage, bias
+    lines, mine, other, query, key, value, gate, state, packed, out, bias_stage, bias
 ):
     core = lax.axis_index("core")
     bias_stage[core] = mine[...].astype(F32).reshape(64 * 64, LANES)
     bias_stage[1 - core] = other[...].astype(F32).reshape(64 * 64, LANES)
-    key_bias = jnp.where(mask_v[...] > 0, 0.0, -1000000000.0 * LOG2E).astype(F32)
+    key_bias = jnp.where(lines[MASK, :] > 0, 0.0, -1000000000.0 * LOG2E).astype(F32)
     key_cols = [column(key_bias[:, c * LANES : (c + 1) * LANES]) for c in range(CHUNKS)]
     weight_t = packed[ATT_OUT, :]
 
@@ -438,19 +449,23 @@
         [("s", token_mask), ("w", mask_v), ("w", pair_input.reshape(tokens, CZ)),
          ("w", row(out_norm_gain)), ("w", out_proj)],
     )
-    state_rows, sent = lax.optimization_barrier((state_rows, sent))
+    weights = (
+        row(out_norm_gain), out_gate, row(out_final_gain), out_final, row(in_norm_gain), in_proj, in_gate,
+        row(in_final_gain), in_final, row(att_norm_gain), att_qkv, att_bias.T, att_gate, att_out,
+        mask_v, row(out_check_weights), row(in_check_weights),
+    )
+    packed, finals, gains, lines = call(
+        prepare,
+        [((PACKED, CZ), BF16), ((CZ, CZ), BF16), ((CZ, 8), F32), ((24, NT), F32)],
+        [(value.shape, value.dtype) for value in weights] + [((COUNT,), None)],
+        [("h", value) for value in weights],
+    )
+    state_rows, sent, packed, finals, gains, lines = lax.optimization_barrier(
+        (state_rows, sent, packed, finals, gains, lines)
+    )
     mine = exchange(sent, PLANE)
-    gain_out, _ = lax.optimization_barrier((row(out_norm_gain), sent))
-    weights = (
-        gain_out, out_gate, row(out_final_gain), out_final, row(in_norm_gain), in_proj, in_gate,
-        row(in_final_gain), in_final, row(att_norm_gain), att_qkv, att_bias.T, att_gate, att_out,
-    )
-    packed, finals, gains = call(
-        prepare,
-        [((PACKED, CZ), BF16), ((CZ, CZ), BF16), ((CZ, 8), F32)],
-        [(value.shape, value.dtype) for value in weights] + [((14,), None)],
-        [("h", value) for value in weights],
-    )
+    mine, state_rows = lax.optimization_barrier((mine, state_rows))
+    other = swap(mine)
     wide = (CZ, tokens)
     state, gate = call(
         gate_rows,
@@ -458,20 +473,19 @@
         [],
         [("v", state_rows), ("v", packed), ("v", gains)],
     )
-    mine, state, gate = lax.optimization_barrier((mine, state, gate))
-    other = swap(mine)
+    other, state, gate = lax.optimization_barrier((other, state, gate))
     sent, check_out = call(
         product_rows,
         [((64, 16, LANES), BF16), ((8, 256), F32)],
         [((256, NT), BF16), ((NT, NT), BF16), ((1024, LANES), F32)],
-        [("v", mine), ("v", other), ("v", row(out_check_weights))],
+        [("v", mine), ("v", other), ("v", lines)],
     )
     recv = exchange(sent, PLANE)
     sent, state = call(
         project_rows,
         [((CM, 32, LANES), BF16), (wide, BF16)],
         [((CM * 32, LANES), F32), ((CM * 16, LANES), F32)],
-        [("s", token_mask), ("v", mask_v), ("v", recv), ("v", state), ("v", gate),
+        [("s", token_mask), ("v", lines), ("v", recv), ("v", state), ("v", gate),
          ("v", packed), ("v", finals), ("v", gains)],
     )
     mine = exchange(sent, PLANE)
@@ -486,30 +500,31 @@
         [((64, 24, LANES), BF16)],
         [((NT, NT), BF16), ((NT, NT), BF16), ((NT, NT), F32), ((64 * 32, LANES), F32),
          ((1024, LANES), F32)],
-        [("v", mine), ("v", other), ("v", row(in_check_weights)), ("v", check_out)],
+        [("v", mine), ("v", other), ("v", lines), ("v", check_out)],
     )
     recv = exchange(sent, PLANE)
-    sent, state, check_row, check_col = call(
+    sent, state = call(
         bias_rows,
-        [((64, 64, LANES), BF16), (wide, BF16), ((32, CM), F32), ((64, CM), F32)],
-        [((CM * 24, LANES), F32), ((64, LANES), F32), ((2, LANES, CM), F32)],
+        [((64, 64, LANES), BF16), (wide, BF16)],
+        [((CM * 24, LANES), F32), ((64, LANES), F32)],
         [("v", recv), ("v", state), ("v", gate), ("v", packed), ("v", finals), ("v", gains)],
     )
     mine = exchange(sent, PLANE)
     mine, state = lax.optimization_barrier((mine, state))
     other = swap(mine)
-    query, key, value, gate = call(
+    query, key, value, gate, check_row, check_col = call(
         attention_inputs,
-        [(wide, BF16), ((tokens, CZ), BF16), (wide, BF16), (wide, BF16)],
-        [],
-        [("v", state), ("v", packed), ("v", gains)],
+        [(wide, BF16), ((tokens, CZ), BF16), (wide, BF16), (wide, BF16), ((32, CM), F32),
+         ((64, CM), F32)],
+        [((CM * 8, LANES), F32), ((2, LANES, CM), F32)],
+        [("v", recv), ("v", state), ("v", packed), ("v", gains)],
     )
     other, query = lax.optimization_barrier((other, query))
     (sent,) = call(
         attend,
         [((8, 4, 64, CZ), BF16)],
         [((2, 64 * 64, LANES), F32), ((HEADS, NT, NT), F32)],
-        [("v", mask_v), ("v", mine), ("v", other), ("v", query), ("v", key), ("v", value),
+        [("v", lines), ("v", mine), ("v", other), ("v", query), ("v", key), ("v", value),
          ("v", gate), ("v", state), ("v", packed)],
     )
     result = exchange(sent, "q").reshape(32, 64, CZ)

time: 153 us -> 152 us (level)
  blocking collectives: 85.1 us -> 107 us
  waiting for transfers between devices: 20.1 us -> 8.06 us
  starting transfers between devices: 15 us -> 5.42 us
    all_to_all x5 -> x6, blocking collectives: 85.1 us -> 107 us  [exchange(): return lax.all_to_all(values, axes, 0, 0, tiled=True)]
    all_to_all x2 -> x1, waiting for transfers between devices: 15.2 us -> 4.94 us  [exchange(): return lax.all_to_all(values, axes, 0, 0, tiled=True)]
    all_to_all x2 -> x1, starting transfers between devices: 15 us -> 5.41 us  [exchange(): return lax.all_to_all(values, axes, 0, 0, tiled=True)]
    ppermute x3, waiting for transfers between devices: 4.92 us -> 3.12 us  [swap(): return lax.ppermute(values, 'core', [(0, 1), (1, 0)])]
  transfers between devices with their start and end apart: 5 -> 4, of which waited for: 5 -> 4; matrix products, arithmetic and copies ran while one was open for 0% -> 0% of each run, Pallas kernels for 5% -> 5%
where the time goes in v4:
time: 152 us; the launch traced here: 151 us
  blocking collectives  107 us (70%)
  Pallas kernels  29.5 us (19%)
  waiting for transfers between devices  8.06 us (5%)
  starting transfers between devices  5.42 us (4%)
    all_to_all x6, blocking collectives, exchange(): return lax.all_to_all(values, axes, 0, 0, tiled=True)  107 us
    pallas_call x10, Pallas kernels, call(): pl.pallas_call(kernel, out_shape=tuple((shape_of(*out) for out in outs)),...  29.5 us
    all_to_all x1, starting transfers between devices, exchange(): return lax.all_to_all(values, axes, 0, 0, tiled=True)  5.41 us
    all_to_all x1, waiting for transfers between devices, exchange(): return lax.all_to_all(values, axes, 0, 0, tiled=True)  4.94 us
    ppermute x3, waiting for transfers between devices, swap(): return lax.ppermute(values, 'core', [(0, 1), (1, 0)])  3.12 us
  transfers between devices with their start and end apart: 4, of which 4 were waited for; matrix products, arithmetic and copies ran while one was open for 0% of the time, Pallas kernels for 5%

profile of v4, /device:TPU:0, one launch (start us, length us, event | category | flops | bytes accessed | tf_op | source)
XLA Modules:
  0.0 151.2 jit_solution(4215038675713931045)
XLA Ops:
  0.6 5.4 %all-to-all-start = ((bf16[8,4,64,128]{3,2,1,0:T(8,128)(2,1)}), bf16[8,4,64,128]{3,2,1,0:T(8,128)(2,1)S(1)}, u32[]{:S(2)}, u32[]{:S(2)}) async-start(bf16[8,4,64,128]{3,2,1,0:T(8,128)(2,1)} %bitcast.14), calls=%async_computation | async-start | bytes 1048576 | tf_op jit(solution)/shard_map/all_to_all | solution.py:415
  6.0 3.0 %shard_map.202 = bf16[64,32,128]{2,1,0:T(8,128)(2,1)S(1)} custom-call(s32[512]{0:T(512)} %mask_s.3, s32[1,512]{1,0:T(1,128)} %bitcast.12, bf16[2048,128]{1,0:T(8,128)(2,1)} %bitcast.15, f32[1,128]{1,0:T(1,128)} %bitcast.19, bf16[128,256]{1,0:T(8,128)(2,1)} %weight.1), custom_call_target="tpu_custom_call" | custom-call | tf_op jit(solution)/shard_map/pallas_call | solution.py:70
  9.0 1.6 %shard_map.203 = (bf16[1168,128]{1,0:T(8,128)(2,1)S(1)}, bf16[128,128]{1,0:T(8,128)(2,1)S(1)}, f32[128,8]{1,0:T(8,128)S(1)}, f32[24,512]{1,0:T(8,128)S(1)}) custom-call(f32[1,128]{1,0:T(1,128)} %bitcast.20, bf16[128,128]{1,0:T(8,128)(2,1)} %refs_1_.1, f32[1,64]{1,0:T(1,128)} %bitcast.22, bf16[64,128]{1,0:T(8,128)(2,1)} %refs_3_.1, f32[1,128]{1,0:T(1,128)} %bitcast.23, ...), custom_call_target="tpu_custom_call" | custom-call | tf_op jit(solution)/shard_map/pallas_call | solution.py:70
  10.6 4.9 %all-to-all-done.x = bf16[8,4,64,128]{3,2,1,0:T(8,128)(2,1)S(1)} async-done(((bf16[8,4,64,128]{3,2,1,0:T(8,128)(2,1)}), bf16[8,4,64,128]{3,2,1,0:T(8,128)(2,1)S(1)}, u32[]{:S(2)}, u32[]{:S(2)}) %all-to-all-start) | async-done | bytes 524320 | tf_op jit(solution)/shard_map/all_to_all | solution.py:415
  15.5 21.6 %all_to_all.35.mine = bf16[64,32,128]{2,1,0:T(8,128)(2,1)S(1)} all-to-all(bf16[64,32,128]{2,1,0:T(8,128)(2,1)S(1)} %shard_map.202), channel_id=1, replica_groups=mesh['p'=8,'core'=2,'q'=8] {'p','q'}, dimensions={0} | all-to-all | bytes 1048576 | tf_op jit(solution)/shard_map/all_to_all | solution.py:415
  37.1 0.0 collective-permute-start
  37.1 1.2 shard_map.204
  38.3 0.7 collective-permute-done.other
  39.0 1.1 shard_map.205
  40.1 0.0 copy-start
  40.1 16.0 %all_to_all.36.recv = bf16[64,16,128]{2,1,0:T(8,128)(2,1)S(1)} all-to-all(bf16[64,16,128]{2,1,0:T(8,128)(2,1)S(1)} %get-tuple-element.54), channel_id=1, replica_groups=mesh['p'=8,'core'=2,'q'=8] {'p','q'}, dimensions={0} | all-to-all | bytes 524288 | tf_op jit(solution)/shard_map/all_to_all | solution.py:415
  56.1 0.0 copy-done
  56.1 2.7 %shard_map.206 = (bf16[64,32,128]{2,1,0:T(8,128)(2,1)S(1)}, bf16[128,2048]{1,0:T(8,128)(2,1)S(1)}) custom-call(s32[512]{0:T(512)S(1)} %copy-done, f32[24,512]{1,0:T(8,128)S(1)} %get-tuple-element.44.lines, bf16[64,16,128]{2,1,0:T(8,128)(2,1)S(1)} %all_to_all.36.recv, bf16[128,2048]{1,0:T(8,128)(2,1)S(1)} %get-tuple-element.55.state_in, ...), custom_call_target="tpu_custom_call" | custom-call | tf_op jit(solution)/shard_map/pallas_call | solution.py:70
  58.8 16.8 %all_to_all.37.mine = bf16[64,32,128]{2,1,0:T(8,128)(2,1)S(1)} all-to-all(bf16[64,32,128]{2,1,0:T(8,128)(2,1)S(1)} %get-tuple-element.58), channel_id=1, replica_groups=mesh['p'=8,'core'=2,'q'=8] {'p','q'}, dimensions={0} | all-to-all | bytes 1048576 | tf_op jit(solution)/shard_map/all_to_all | solution.py:415
  75.6 0.0 collective-permute-start.1
  75.6 0.6 shard_map.207.gate
  76.2 1.3 collective-permute-done.1.other
  77.5 1.4 shard_map.208
  78.9 17.2 %all_to_all.38.recv = bf16[64,24,128]{2,1,0:T(8,128)(2,1)S(1)} all-to-all(bf16[64,24,128]{2,1,0:T(8,128)(2,1)S(1)} %shard_map.208), channel_id=1, replica_groups=mesh['p'=8,'core'=2,'q'=8] {'p','q'}, dimensions={0} | all-to-all | bytes 786432 | tf_op jit(solution)/shard_map/all_to_all | solution.py:415
  96.1 1.3 shard_map.209
  97.4 21.9 %all_to_all.39.mine = bf16[64,64,128]{2,1,0:T(8,128)(2,1)S(1)} all-to-all(bf16[64,64,128]{2,1,0:T(8,128)(2,1)S(1)} %get-tuple-element.65), channel_id=1, replica_groups=mesh['p'=8,'core'=2,'q'=8] {'p','q'}, dimensions={0} | all-to-all | bytes 2097152 | tf_op jit(solution)/shard_map/all_to_all | solution.py:415
  119.3 0.0 collective-permute-start.2
  119.3 1.5 %shard_map.210 = (bf16[128,2048]{1,0:T(8,128)(2,1)S(1)}, bf16[2048,128]{1,0:T(8,128)(2,1)S(1)}, bf16[128,2048]{1,0:T(8,128)(2,1)S(1)}, bf16[128,2048]{1,0:T(8,12...) custom-call(bf16[64,24,128]{2,1,0:T(8,128)(2,1)S(1)} %all_to_all.38.recv, ...), custom_call_target="tpu_custom_call" | custom-call | tf_op jit(solution)/shard_map/pallas_call | solution.py:70
  120.8 1.1 collective-permute-done.2.other
  121.9 15.2 %shard_map.211 = bf16[8,4,64,128]{3,2,1,0:T(8,128)(2,1)S(1)} custom-call(f32[24,512]{1,0:T(8,128)S(1)} %get-tuple-element.44.lines, bf16[64,64,128]{2,1,0:T(8,128)(2,1)S(1)} %all_to_all.39.mine, bf16[64,64,128]{2,1,0:T(8,128)(2,1)S(1)} %collective-permute-done.2.other, bf16[128,2048]{1,0:T(8,128)(2,1)S(1)} %get-tuple-element.71.query, ...), custom_call_target="tpu_custom_call" | custom-call | tf_op jit(solution)/shard_map/pallas_call | solution.py:70
  137.1 13.3 %all_to_all.40 = bf16[8,4,64,128]{3,2,1,0:T(8,128)(2,1)S(1)} all-to-all(bf16[8,4,64,128]{3,2,1,0:T(8,128)(2,1)S(1)} %shard_map.211), channel_id=1, replica_groups=mesh['p'=8,'core'=2,'q'=8] {'q'}, dimensions={0} | all-to-all | bytes 1048576 | tf_op jit(solution)/shard_map/all_to_all | solution.py:415
  150.4 0.8 copy.23
Async XLA Ops:
  0.6 14.9 %all-to-all-start = ((bf16[8,4,64,128]{3,2,1,0:T(8,128)(2,1)}), bf16[8,4,64,128]{3,2,1,0:T(8,128)(2,1)S(1)}, u32[]{:S(2)}, u32[]{:S(2)}) async-start(bf16[8,4,64,128]{3,2,1,0:T(8,128)(2,1)} %bitcast.14), calls=%async_computation | async-start | bytes 1048576 | tf_op jit(solution)/shard_map/all_to_all | solution.py:415
  37.1 1.9 %collective-permute-start = (bf16[64,32,128]{2,1,0:T(8,128)(2,1)S(1)}, bf16[64,32,128]{2,1,0:T(8,128)(2,1)S(1)}, u32[]{:S(2)}, u32[]{:S(2)}) collective-permute-start(bf16[64,32,128]{2,1,0:T(8,128)(2,1)S(1)} %all_to_all.35.mine), channel_id=1, source_target_pairs={{0,8},{8,0},{1,9},{9,1},{2,10},{10,2},{3,11},{11,3},{4,12},{12,4},... | collective-permute-start | bytes 1572872 | tf_op jit(solution)/shard_map/ppermute | solution.py:411
  40.1 16.0 %copy-start = (s32[512]{0:T(512)S(1)}, s32[512]{0:T(512)}, u32[]{:S(2)}) copy-start(s32[512]{0:T(512)} %mask_s.3) | copy-start | bytes 6148
  75.6 1.9 %collective-permute-start.1 = (bf16[64,32,128]{2,1,0:T(8,128)(2,1)S(1)}, bf16[64,32,128]{2,1,0:T(8,128)(2,1)S(1)}, u32[]{:S(2)}, u32[]{:S(2)}) collective-permute-start(bf16[64,32,128]{2,1,0:T(8,128)(2,1)S(1)} %all_to_all.37.mine), channel_id=1, source_target_pairs={{0,8},{8,0},{1,9},{9,1},{2,10},{10,2},{3,11},{11,3},{4,12},{12,4},... | collective-permute-start | bytes 1572872 | tf_op jit(solution)/shard_map/ppermute | solution.py:411
  119.3 2.7 %collective-permute-start.2 = (bf16[64,64,128]{2,1,0:T(8,128)(2,1)S(1)}, bf16[64,64,128]{2,1,0:T(8,128)(2,1)S(1)}, u32[]{:S(2)}, u32[]{:S(2)}) collective-permute-start(bf16[64,64,128]{2,1,0:T(8,128)(2,1)S(1)} %all_to_all.39.mine), channel_id=1, source_target_pairs={{0,8},{8,0},{1,9},{9,1},{2,10},{10,2},{3,11},{11,3},{4,12},{12,4},... | collective-permute-start | bytes 3145736 | tf_op jit(solution)/shard_map/ppermute | solution.py:411

commit v5 on v4

--- a/solution.py
+++ b/solution.py
@@ -42,11 +42,15 @@
     return jnp.where(rows == cols, 1.0, 0.0).astype(BF16)
 
 
-def norm(values, gain_col):
+def centre(values, gain_col):
     mean = jnp.mean(values, axis=0, keepdims=True)
     centered = values - mean
     variance = jnp.mean(centered * centered, axis=0, keepdims=True)
-    return (centered * lax.rsqrt(variance + 1e-05) * gain_col).astype(BF16)
+    return centered * lax.rsqrt(variance + 1e-05) * gain_col
+
+
+def norm(values, gain_col):
+    return centre(values, gain_col).astype(BF16)
 
 
 def sigmoid(values):
@@ -60,7 +64,7 @@
     return high, middle, (rest - middle.astype(F32)).astype(BF16)
 
 
-def call(kernel, outs, scratch, ins, mib=48):
+def call(kernel, outs, scratch, ins, mib=24):
     def shape_of(shape, kind, place="v"):
         return (pltpu.HBM if place == "h" else jax.ShapeDtypeStruct)(shape, kind)
 
@@ -132,6 +136,7 @@
 ATT_OUT = slice(1024, 1152)
 BIAS = slice(1152, 1156)
 PACKED = 1168
+LARGE = 3e38
 COUNT = 17
 MASK = slice(0, 1)
 OUT_CHECK = slice(8, 16)
@@ -166,8 +171,8 @@
     packed[ATT_OUT, :] = flipped(att_out[...])
     turned = jnp.concatenate([att_bias[...], jnp.zeros((16 - HEADS, CZ), BF16)], axis=0)
     packed[BIAS.start : PACKED, :] = turned
-    finals[:, 0:CM] = flipped(out_final[...])
-    finals[:, CM : 2 * CM] = flipped(in_final[...])
+    for at, weight in enumerate((out_final, out_final, in_final, in_final)):
+        finals[:, at * CM : (at + 1) * CM] = flipped(weight[...])
     pad = jnp.zeros((1, CM), F32)
     rows = [
         out_norm_gain[...],
@@ -225,7 +230,10 @@
     product = jnp.concatenate(
         [recv_stage[pl.ds(r * 4 + chunk, CM, stride=stride), :] for chunk in range(CHUNKS)], axis=1
     )
-    update = dot(final_t, norm(product, final_gain), 1, 0)
+    normed = centre(product, final_gain)
+    high = normed.astype(BF16)
+    low = (normed - high.astype(F32)).astype(BF16)
+    update = dot(final_t, jnp.concatenate([high, low], axis=0), 1, 0)
     return state.astype(F32) + gate.astype(F32) * update
 
 
@@ -236,7 +244,7 @@
     mask_all = lines[MASK, :]
     gain_col = gains[:, 1:2]
     final_col = gains[0:CM, 3:4]
-    final_t = finals[:, 0:CM]
+    final_t = finals[:, 0 : 2 * CM]
     weight_t = packed[IN_PROJ, :]
     recv_stage[...] = recv[...].astype(F32).reshape(CM * 16, LANES)
     for r in range(4):
@@ -244,7 +252,7 @@
         state = update_rows(
             recv_stage, 16, r, state_in[:, span], gate[:, span], final_col, final_t
         )
-        state_out[:, span] = state.astype(BF16)
+        state_out[:, span] = state
         mixed = dot(weight_t, norm(state, gain_col), 1, 0)
         mask = mask_all * mask_s[row0 + r].astype(F32)
         left = sigmoid(mixed[0:CM]) * mixed[CM : 2 * CM] * mask
@@ -293,11 +301,13 @@
 
 
 def bias_rows(
-    recv, state_in, gate, packed, finals, gains, out, state_out, recv_stage, bias_stage
+    lines, recv, state_in, gate, packed, finals, gains, out, state_out, normed_out,
+    recv_stage, bias_stage,
 ):
+    live = jnp.broadcast_to(lines[MASK, :], (PACKED - BIAS.start, NT)) > 0
     gain_col = gains[:, 2:3]
     final_col = gains[0:CM, 4:5]
-    final_t = finals[:, CM : 2 * CM]
+    final_t = finals[:, 2 * CM : 4 * CM]
     weight_t = packed[BIAS.start : PACKED, :]
     recv_stage[...] = recv[...].astype(F32).reshape(CM * 24, LANES)
     for r in range(4):
@@ -305,7 +315,10 @@
         state = update_rows(recv_stage, 24, r, state_in[:, span], gate[:, span], final_col, final_t)
         state_out[:, span] = state.astype(BF16)
         normed = norm(state, gain_col)
+        normed_out[:, span] = normed
         bias = dot(weight_t, normed, 1, 0) * LOG2E
+        top = jnp.max(jnp.where(live, bias, -LARGE), axis=1, keepdims=True)
+        bias = bias - jnp.where(top > -LARGE, top, 0.0)
         for chunk in range(CHUNKS):
             bias_stage[pl.ds(r * 16 + chunk, HEADS, stride=4), :] = bias[
                 0:HEADS, chunk * LANES : (chunk + 1) * LANES
@@ -314,10 +327,11 @@
 
 
 def attention_inputs(
-    recv, state, packed, gains, query_out, key_out, value_out, gate_out, check_row, check_col,
+    recv, mine, normed, packed,
+    query_out, key_out, value_out, gate_out, check_row, check_col, mine_out,
     recv_stage, turn,
 ):
-    gain_col = gains[:, 2:3]
+    mine_out[...] = mine[...].astype(F32).reshape(64 * 64, LANES)
     recv_stage[...] = recv[:, 16:24, :].astype(F32).reshape(CM * 8, LANES)
     p, q = lax.axis_index("p"), lax.axis_index("q")
 
@@ -330,7 +344,7 @@
     check_col[...] = turn[1, pl.ds(pl.multiple_of(lax.rem(q, 2) * 64, 64), 64), :]
     for r in range(4):
         span = slice(r * NT, (r + 1) * NT)
-        rows = norm(state[:, span].astype(F32), gain_col)
+        rows = normed[:, span]
         query_out[:, span] = (dot(packed[QUERY, :], rows, 1, 0) * (LOG2E * DH ** (-0.5))).astype(
             BF16
         )
@@ -340,22 +354,21 @@
 
 
 def attend(
-    lines, mine, other, query, key, value, gate, state, packed, out, bias_stage, bias
+    lines, mine, bias_other, query, key, value, gate, state, packed, out, other, bias
 ):
-    core = lax.axis_index("core")
-    bias_stage[core] = mine[...].astype(F32).reshape(64 * 64, LANES)
-    bias_stage[1 - core] = other[...].astype(F32).reshape(64 * 64, LANES)
+    first = lax.axis_index("core") == 0
+    other[...] = bias_other[...].astype(F32).reshape(64 * 64, LANES)
     key_bias = jnp.where(lines[MASK, :] > 0, 0.0, -1000000000.0 * LOG2E).astype(F32)
     key_cols = [column(key_bias[:, c * LANES : (c + 1) * LANES]) for c in range(CHUNKS)]
     weight_t = packed[ATT_OUT, :]
 
     def turn_bias(h):
         for chunk in range(CHUNKS):
-            blocks = [
-                bias_stage[plane, pl.ds(p * 512 + h * 4 + chunk, 32, stride=16), :]
-                for p in range(8)
-                for plane in range(2)
-            ]
+            blocks = []
+            for p in range(8):
+                rows = pl.ds(p * 512 + h * 4 + chunk, 32, stride=16)
+                here, there = mine[rows, :], other[rows, :]
+                blocks += [jnp.where(first, here, there), jnp.where(first, there, here)]
             turned = jnp.transpose(jnp.concatenate(blocks, axis=0))
             bias[h, chunk * LANES : (chunk + 1) * LANES, :] = turned + key_cols[chunk]
 
@@ -456,7 +469,7 @@
     )
     packed, finals, gains, lines = call(
         prepare,
-        [((PACKED, CZ), BF16), ((CZ, CZ), BF16), ((CZ, 8), F32), ((24, NT), F32)],
+        [((PACKED, CZ), BF16), ((CZ, 4 * CM), BF16), ((CZ, 8), F32), ((24, NT), F32)],
         [(value.shape, value.dtype) for value in weights] + [((COUNT,), None)],
         [("h", value) for value in weights],
     )
@@ -483,7 +496,7 @@
     recv = exchange(sent, PLANE)
     sent, state = call(
         project_rows,
-        [((CM, 32, LANES), BF16), (wide, BF16)],
+        [((CM, 32, LANES), BF16), (wide, F32)],
         [((CM * 32, LANES), F32), ((CM * 16, LANES), F32)],
         [("s", token_mask), ("v", lines), ("v", recv), ("v", state), ("v", gate),
          ("v", packed), ("v", finals), ("v", gains)],
@@ -503,28 +516,29 @@
         [("v", mine), ("v", other), ("v", lines), ("v", check_out)],
     )
     recv = exchange(sent, PLANE)
-    sent, state = call(
+    sent, state, normed = call(
         bias_rows,
-        [((64, 64, LANES), BF16), (wide, BF16)],
+        [((64, 64, LANES), BF16), (wide, BF16), (wide, BF16)],
         [((CM * 24, LANES), F32), ((64, LANES), F32)],
-        [("v", recv), ("v", state), ("v", gate), ("v", packed), ("v", finals), ("v", gains)],
+        [("v", lines), ("v", recv), ("v", state), ("v", gate), ("v", packed), ("v", finals),
+         ("v", gains)],
     )
     mine = exchange(sent, PLANE)
-    mine, state = lax.optimization_barrier((mine, state))
+    mine, normed = lax.optimization_barrier((mine, normed))
     other = swap(mine)
-    query, key, value, gate, check_row, check_col = call(
+    query, key, value, gate, check_row, check_col, staged = call(
         attention_inputs,
         [(wide, BF16), ((tokens, CZ), BF16), (wide, BF16), (wide, BF16), ((32, CM), F32),
-         ((64, CM), F32)],
+         ((64, CM), F32), ((64 * 64, LANES), F32)],
         [((CM * 8, LANES), F32), ((2, LANES, CM), F32)],
-        [("v", recv), ("v", state), ("v", packed), ("v", gains)],
+        [("v", recv), ("v", mine), ("v", normed), ("v", packed)],
     )
     other, query = lax.optimization_barrier((other, query))
     (sent,) = call(
         attend,
         [((8, 4, 64, CZ), BF16)],
-        [((2, 64 * 64, LANES), F32), ((HEADS, NT, NT), F32)],
-        [("v", lines), ("v", mine), ("v", other), ("v", query), ("v", key), ("v", value),
+        [((64 * 64, LANES), F32), ((HEADS, NT, NT), F32)],
+        [("v", lines), ("v", staged), ("v", other), ("v", query), ("v", key), ("v", value),
          ("v", gate), ("v", state), ("v", packed)],
     )
     result = exchange(sent, "q").reshape(32, 64, CZ)

time: 152 us -> 143 us (0.941)
  Pallas kernels: 29.5 us -> 20.4 us
    pallas_call x10, Pallas kernels: 29.5 us -> 20.4 us  [call(): pl.pallas_call(kernel, out_shape=tuple((shape_of(*out) for out in outs)),...]
where the time goes in v5:
time: 143 us; the launch traced here: 142 us
  blocking collectives  107 us (75%)
  Pallas kernels  20.4 us (14%)
  waiting for transfers between devices  8.26 us (6%)
  starting transfers between devices  5.42 us (4%)
    all_to_all x6, blocking collectives, exchange(): return lax.all_to_all(values, axes, 0, 0, tiled=True)  107 us
    pallas_call x10, Pallas kernels, call(): pl.pallas_call(kernel, out_shape=tuple((shape_of(*out) for out in outs)),...  20.4 us
    all_to_all x1, starting transfers between devices, exchange(): return lax.all_to_all(values, axes, 0, 0, tiled=True)  5.41 us
    all_to_all x1, waiting for transfers between devices, exchange(): return lax.all_to_all(values, axes, 0, 0, tiled=True)  4.96 us
    ppermute x3, waiting for transfers between devices, swap(): return lax.ppermute(values, 'core', [(0, 1), (1, 0)])  3.3 us
  transfers between devices with their start and end apart: 4, of which 4 were waited for; matrix products, arithmetic and copies ran while one was open for 0% of the time, Pallas kernels for 5%

profile of v5, /device:TPU:0, one launch (start us, length us, event | category | flops | bytes accessed | tf_op | source)
XLA Modules:
  0.0 142.2 jit_solution(10053182971778752968)
XLA Ops:
  0.6 5.4 %all-to-all-start = ((bf16[8,4,64,128]{3,2,1,0:T(8,128)(2,1)}), bf16[8,4,64,128]{3,2,1,0:T(8,128)(2,1)S(1)}, u32[]{:S(2)}, u32[]{:S(2)}) async-start(bf16[8,4,64,128]{3,2,1,0:T(8,128)(2,1)} %bitcast.14), calls=%async_computation | async-start | bytes 1048576 | tf_op jit(solution)/shard_map/all_to_all | solution.py:428
  6.0 3.0 %shard_map.202 = bf16[64,32,128]{2,1,0:T(8,128)(2,1)S(1)} custom-call(s32[512]{0:T(512)} %mask_s.3, s32[1,512]{1,0:T(1,128)} %bitcast.12, bf16[2048,128]{1,0:T(8,128)(2,1)} %bitcast.15, f32[1,128]{1,0:T(1,128)} %bitcast.19, bf16[128,256]{1,0:T(8,128)(2,1)} %weight.1), custom_call_target="tpu_custom_call" | custom-call | tf_op jit(solution)/shard_map/pallas_call | solution.py:74
  9.0 0.0 copy-start
  9.0 1.5 %shard_map.203 = (bf16[1168,128]{1,0:T(8,128)(2,1)S(1)}, bf16[128,256]{1,0:T(8,128)(2,1)S(1)}, f32[128,8]{1,0:T(8,128)S(1)}, f32[24,512]{1,0:T(8,128)S(1)}) custom-call(f32[1,128]{1,0:T(1,128)} %bitcast.20, bf16[128,128]{1,0:T(8,128)(2,1)} %refs_1_.1, f32[1,64]{1,0:T(1,128)} %bitcast.22, bf16[64,128]{1,0:T(8,128)(2,1)} %refs_3_.1, f32[1,128]{1,0:T(1,128)} %bitcast.23, ...), custom_call_target="tpu_custom_call" | custom-call | tf_op jit(solution)/shard_map/pallas_call | solution.py:74
  10.6 5.0 %all-to-all-done.x = bf16[8,4,64,128]{3,2,1,0:T(8,128)(2,1)S(1)} async-done(((bf16[8,4,64,128]{3,2,1,0:T(8,128)(2,1)}), bf16[8,4,64,128]{3,2,1,0:T(8,128)(2,1)S(1)}, u32[]{:S(2)}, u32[]{:S(2)}) %all-to-all-start) | async-done | bytes 524320 | tf_op jit(solution)/shard_map/all_to_all | solution.py:428
  15.5 21.6 %all_to_all.35.mine = bf16[64,32,128]{2,1,0:T(8,128)(2,1)S(1)} all-to-all(bf16[64,32,128]{2,1,0:T(8,128)(2,1)S(1)} %shard_map.202), channel_id=1, replica_groups=mesh['p'=8,'core'=2,'q'=8] {'p','q'}, dimensions={0} | all-to-all | bytes 1048576 | tf_op jit(solution)/shard_map/all_to_all | solution.py:428
  37.1 0.0 collective-permute-start
  37.1 1.2 shard_map.204
  38.3 0.7 collective-permute-done.other
  39.0 1.1 shard_map.205
  40.1 15.9 %all_to_all.36.recv = bf16[64,16,128]{2,1,0:T(8,128)(2,1)S(1)} all-to-all(bf16[64,16,128]{2,1,0:T(8,128)(2,1)S(1)} %get-tuple-element.56), channel_id=1, replica_groups=mesh['p'=8,'core'=2,'q'=8] {'p','q'}, dimensions={0} | all-to-all | bytes 524288 | tf_op jit(solution)/shard_map/all_to_all | solution.py:428
  56.0 0.0 copy-done
  56.0 2.7 %shard_map.206 = (bf16[64,32,128]{2,1,0:T(8,128)(2,1)S(1)}, f32[128,2048]{1,0:T(8,128)S(1)}) custom-call(s32[512]{0:T(512)S(1)} %copy-done, f32[24,512]{1,0:T(8,128)S(1)} %get-tuple-element.46.lines, bf16[64,16,128]{2,1,0:T(8,128)(2,1)S(1)} %all_to_all.36.recv, bf16[128,2048]{1,0:T(8,128)(2,1)S(1)} %get-tuple-element.57.state_in, ...), custom_call_target="tpu_custom_call" | custom-call | tf_op jit(solution)/shard_map/pallas_call | solution.py:74
  58.6 16.8 %all_to_all.37.mine = bf16[64,32,128]{2,1,0:T(8,128)(2,1)S(1)} all-to-all(bf16[64,32,128]{2,1,0:T(8,128)(2,1)S(1)} %get-tuple-element.60), channel_id=1, replica_groups=mesh['p'=8,'core'=2,'q'=8] {'p','q'}, dimensions={0} | all-to-all | bytes 1048576 | tf_op jit(solution)/shard_map/all_to_all | solution.py:428
  75.5 0.0 collective-permute-start.1
  75.5 0.5 shard_map.207.gate
  76.0 1.4 collective-permute-done.1.other
  77.4 1.4 shard_map.208
  78.7 17.2 %all_to_all.38.recv = bf16[64,24,128]{2,1,0:T(8,128)(2,1)S(1)} all-to-all(bf16[64,24,128]{2,1,0:T(8,128)(2,1)S(1)} %shard_map.208), channel_id=1, replica_groups=mesh['p'=8,'core'=2,'q'=8] {'p','q'}, dimensions={0} | all-to-all | bytes 786432 | tf_op jit(solution)/shard_map/all_to_all | solution.py:428
  95.9 1.4 shard_map.209
  97.3 21.9 %all_to_all.39.mine = bf16[64,64,128]{2,1,0:T(8,128)(2,1)S(1)} all-to-all(bf16[64,64,128]{2,1,0:T(8,128)(2,1)S(1)} %get-tuple-element.67), channel_id=1, replica_groups=mesh['p'=8,'core'=2,'q'=8] {'p','q'}, dimensions={0} | all-to-all | bytes 2097152 | tf_op jit(solution)/shard_map/all_to_all | solution.py:428
  119.2 0.0 collective-permute-start.2
  119.2 1.4 shard_map.210
  120.6 1.3 collective-permute-done.2.bias_other
  121.9 6.3 %shard_map.211 = bf16[8,4,64,128]{3,2,1,0:T(8,128)(2,1)S(1)} custom-call(f32[24,512]{1,0:T(8,128)S(1)} %get-tuple-element.46.lines, f32[4096,128]{1,0:T(8,128)S(1)} %get-tuple-element.71.mine, bf16[64,64,128]{2,1,0:T(8,128)(2,1)S(1)} %collective-permute-done.2.bias_other, bf16[128,2048]{1,0:T(8,128)(2,1)S(1)} %get-tuple-element.74.query, ...), custom_call_target="tpu_custom_call" | custom-call | tf_op jit(solution)/shard_map/pallas_call | solution.py:74
  128.1 13.3 %all_to_all.40 = bf16[8,4,64,128]{3,2,1,0:T(8,128)(2,1)S(1)} all-to-all(bf16[8,4,64,128]{3,2,1,0:T(8,128)(2,1)S(1)} %shard_map.211), channel_id=1, replica_groups=mesh['p'=8,'core'=2,'q'=8] {'q'}, dimensions={0} | all-to-all | bytes 1048576 | tf_op jit(solution)/shard_map/all_to_all | solution.py:428
  141.4 0.8 copy.23
Async XLA Ops:
  0.6 14.9 %all-to-all-start = ((bf16[8,4,64,128]{3,2,1,0:T(8,128)(2,1)}), bf16[8,4,64,128]{3,2,1,0:T(8,128)(2,1)S(1)}, u32[]{:S(2)}, u32[]{:S(2)}) async-start(bf16[8,4,64,128]{3,2,1,0:T(8,128)(2,1)} %bitcast.14), calls=%async_computation | async-start | bytes 1048576 | tf_op jit(solution)/shard_map/all_to_all | solution.py:428
  9.0 47.0 %copy-start = (s32[512]{0:T(512)S(1)}, s32[512]{0:T(512)}, u32[]{:S(2)}) copy-start(s32[512]{0:T(512)} %mask_s.3) | copy-start | bytes 6148
  37.1 1.9 %collective-permute-start = (bf16[64,32,128]{2,1,0:T(8,128)(2,1)S(1)}, bf16[64,32,128]{2,1,0:T(8,128)(2,1)S(1)}, u32[]{:S(2)}, u32[]{:S(2)}) collective-permute-start(bf16[64,32,128]{2,1,0:T(8,128)(2,1)S(1)} %all_to_all.35.mine), channel_id=1, source_target_pairs={{0,8},{8,0},{1,9},{9,1},{2,10},{10,2},{3,11},{11,3},{4,12},{12,4},... | collective-permute-start | bytes 1572872 | tf_op jit(solution)/shard_map/ppermute | solution.py:424
  75.5 1.9 %collective-permute-start.1 = (bf16[64,32,128]{2,1,0:T(8,128)(2,1)S(1)}, bf16[64,32,128]{2,1,0:T(8,128)(2,1)S(1)}, u32[]{:S(2)}, u32[]{:S(2)}) collective-permute-start(bf16[64,32,128]{2,1,0:T(8,128)(2,1)S(1)} %all_to_all.37.mine), channel_id=1, source_target_pairs={{0,8},{8,0},{1,9},{9,1},{2,10},{10,2},{3,11},{11,3},{4,12},{12,4},... | collective-permute-start | bytes 1572872 | tf_op jit(solution)/shard_map/ppermute | solution.py:424
  119.2 2.7 %collective-permute-start.2 = (bf16[64,64,128]{2,1,0:T(8,128)(2,1)S(1)}, bf16[64,64,128]{2,1,0:T(8,128)(2,1)S(1)}, u32[]{:S(2)}, u32[]{:S(2)}) collective-permute-start(bf16[64,64,128]{2,1,0:T(8,128)(2,1)S(1)} %all_to_all.39.mine), channel_id=1, source_target_pairs={{0,8},{8,0},{1,9},{9,1},{2,10},{10,2},{3,11},{11,3},{4,12},{12,4},... | collective-permute-start | bytes 3145736 | tf_op jit(solution)/shard_map/ppermute | solution.py:424

commit v6 on v5

--- a/solution.py
+++ b/solution.py
@@ -61,7 +61,11 @@
     high = values.astype(BF16)
     rest = values - high.astype(F32)
     middle = rest.astype(BF16)
-    return high, middle, (rest - middle.astype(F32)).astype(BF16)
+    return jnp.concatenate([high, middle, (rest - middle.astype(F32)).astype(BF16)], axis=0)
+
+
+def folded(parts):
+    return parts[0:8] + (parts[8:16] + parts[16:24])
 
 
 def call(kernel, outs, scratch, ins, mib=24):
@@ -136,6 +140,7 @@
 ATT_OUT = slice(1024, 1152)
 BIAS = slice(1152, 1156)
 PACKED = 1168
+GROUP = 4
 LARGE = 3e38
 COUNT = 17
 MASK = slice(0, 1)
@@ -197,7 +202,7 @@
         gate_out[:, span] = sigmoid(dot(weight_t, norm(state, gain_col), 1, 0)).astype(BF16)
 
 
-def product_rows(mine, other, lines, out, check_out, left, right, stage):
+def product_rows(mine, other, out, left, right, stage):
     core = lax.axis_index("core")
     low = lax.broadcasted_iota(jnp.int32, (16, LANES), 1) < 64
 
@@ -221,14 +226,16 @@
     for chunk in range(CHUNKS):
         stage[pl.ds(chunk, 256, stride=4), :] = product[:, chunk * LANES : (chunk + 1) * LANES]
     out[...] = stage[...].astype(BF16).reshape(64, 16, LANES)
-    weight_rows = lines[OUT_CHECK, :].astype(BF16)
-    total = sum(dot(part, left[...], 1, 1) for part in thirds(dot(weight_rows, right[...], 1, 0)))
-    check_out[...] = total / NT
-
-
-def update_rows(recv_stage, stride, r, state, gate, final_gain, final_t):
+
+
+def update_rows(recv_stage, stride, members, state, gate, final_gain, final_t):
     product = jnp.concatenate(
-        [recv_stage[pl.ds(r * 4 + chunk, CM, stride=stride), :] for chunk in range(CHUNKS)], axis=1
+        [
+            recv_stage[pl.ds(r * 4 + chunk, CM, stride=stride), :]
+            for r in members
+            for chunk in range(CHUNKS)
+        ],
+        axis=1,
     )
     normed = centre(product, final_gain)
     high = normed.astype(BF16)
@@ -247,24 +254,29 @@
     final_t = finals[:, 0 : 2 * CM]
     weight_t = packed[IN_PROJ, :]
     recv_stage[...] = recv[...].astype(F32).reshape(CM * 16, LANES)
-    for r in range(4):
-        span = slice(r * NT, (r + 1) * NT)
+    for group in range(0, 4, GROUP):
+        members = range(group, group + GROUP)
+        span = slice(group * NT, (group + GROUP) * NT)
         state = update_rows(
-            recv_stage, 16, r, state_in[:, span], gate[:, span], final_col, final_t
+            recv_stage, 16, members, state_in[:, span], gate[:, span], final_col, final_t
         )
         state_out[:, span] = state
         mixed = dot(weight_t, norm(state, gain_col), 1, 0)
-        mask = mask_all * mask_s[row0 + r].astype(F32)
+        mask = jnp.concatenate([mask_all * mask_s[row0 + r].astype(F32) for r in members], axis=1)
         left = sigmoid(mixed[0:CM]) * mixed[CM : 2 * CM] * mask
         right = sigmoid(mixed[2 * CM : 3 * CM]) * mixed[3 * CM : 4 * CM] * mask
-        for chunk in range(CHUNKS):
-            lanes = slice(chunk * LANES, (chunk + 1) * LANES)
-            stage[pl.ds(r * 8 + chunk, CM, stride=32), :] = left[:, lanes]
-            stage[pl.ds(r * 8 + 4 + chunk, CM, stride=32), :] = right[:, lanes]
+        for at, r in enumerate(members):
+            for chunk in range(CHUNKS):
+                lanes = slice(at * NT + chunk * LANES, at * NT + (chunk + 1) * LANES)
+                stage[pl.ds(r * 8 + chunk, CM, stride=32), :] = left[:, lanes]
+                stage[pl.ds(r * 8 + 4 + chunk, CM, stride=32), :] = right[:, lanes]
     out[...] = stage[...].astype(BF16).reshape(CM, 32, LANES)
 
 
-def gate_only(state, packed, gains, gate_out):
+def gate_and_check(state, packed, gains, left, right, lines, gate_out, check_out):
+    weight_rows = lines[OUT_CHECK, :].astype(BF16)
+    total = folded(dot(thirds(dot(weight_rows, right[...], 1, 0)), left[...], 1, 1))
+    check_out[...] = total / NT
     gain_col = gains[:, 1:2]
     weight_t = packed[IN_GATE, :]
     for r in range(4):
@@ -291,7 +303,7 @@
             ]
     out[:, 0:16, :] = stage_out[...].astype(BF16).reshape(64, 16, LANES)
     weight_rows = lines[IN_CHECK, :].astype(BF16)
-    total = sum(dot(part, right[...], 1, 0) for part in thirds(dot(weight_rows, left[...], 1, 1)))
+    total = folded(dot(thirds(dot(weight_rows, left[...], 1, 1)), right[...], 1, 0))
     high = check_in[...].astype(BF16).astype(F32)
     lines = []
     for part, count in ((high, 2), (check_in[...] - high, 2), (total / NT, 4)):
@@ -310,19 +322,24 @@
     final_t = finals[:, 2 * CM : 4 * CM]
     weight_t = packed[BIAS.start : PACKED, :]
     recv_stage[...] = recv[...].astype(F32).reshape(CM * 24, LANES)
-    for r in range(4):
-        span = slice(r * NT, (r + 1) * NT)
-        state = update_rows(recv_stage, 24, r, state_in[:, span], gate[:, span], final_col, final_t)
+    for group in range(0, 4, GROUP):
+        members = range(group, group + GROUP)
+        span = slice(group * NT, (group + GROUP) * NT)
+        state = update_rows(
+            recv_stage, 24, members, state_in[:, span], gate[:, span], final_col, final_t
+        )
         state_out[:, span] = state.astype(BF16)
         normed = norm(state, gain_col)
         normed_out[:, span] = normed
-        bias = dot(weight_t, normed, 1, 0) * LOG2E
-        top = jnp.max(jnp.where(live, bias, -LARGE), axis=1, keepdims=True)
-        bias = bias - jnp.where(top > -LARGE, top, 0.0)
-        for chunk in range(CHUNKS):
-            bias_stage[pl.ds(r * 16 + chunk, HEADS, stride=4), :] = bias[
-                0:HEADS, chunk * LANES : (chunk + 1) * LANES
-            ]
+        bias_all = dot(weight_t, normed, 1, 0) * LOG2E
+        for at, r in enumerate(members):
+            bias = bias_all[:, at * NT : (at + 1) * NT]
+            top = jnp.max(jnp.where(live, bias, -LARGE), axis=1, keepdims=True)
+            bias = bias - jnp.where(top > -LARGE, top, 0.0)
+            for chunk in range(CHUNKS):
+                bias_stage[pl.ds(r * 16 + chunk, HEADS, stride=4), :] = bias[
+                    0:HEADS, chunk * LANES : (chunk + 1) * LANES
+                ]
     out[...] = jnp.broadcast_to(bias_stage[...].astype(BF16)[None], (64, 64, LANES))
 
 
@@ -487,11 +504,11 @@
         [("v", state_rows), ("v", packed), ("v", gains)],
     )
     other, state, gate = lax.optimization_barrier((other, state, gate))
-    sent, check_out = call(
+    sent, left, right = call(
         product_rows,
-        [((64, 16, LANES), BF16), ((8, 256), F32)],
-        [((256, NT), BF16), ((NT, NT), BF16), ((1024, LANES), F32)],
-        [("v", mine), ("v", other), ("v", lines)],
+        [((64, 16, LANES), BF16), ((256, NT), BF16), ((NT, NT), BF16)],
+        [((1024, LANES), F32)],
+        [("v", mine), ("v", other)],
     )
     recv = exchange(sent, PLANE)
     sent, state = call(
@@ -504,10 +521,13 @@
     mine = exchange(sent, PLANE)
     mine, state = lax.optimization_barrier((mine, state))
     other = swap(mine)
-    (gate,) = call(
-        gate_only, [(wide, BF16)], [], [("v", state), ("v", packed), ("v", gains)]
-    )
-    other, gate = lax.optimization_barrier((other, gate))
+    gate, check_out = call(
+        gate_and_check,
+        [(wide, BF16), ((8, 256), F32)],
+        [],
+        [("v", state), ("v", packed), ("v", gains), ("v", left), ("v", right), ("v", lines)],
+    )
+    other, gate, check_out = lax.optimization_barrier((other, gate, check_out))
     (sent,) = call(
         product_cols,
         [((64, 24, LANES), BF16)],

time: 143 us -> 142 us (level)
  no operation moved by 1% of the time
where the time goes in v6:
time: 142 us; the launch traced here: 141 us
  blocking collectives  107 us (75%)
  Pallas kernels  19.4 us (14%)
  waiting for transfers between devices  8.2 us (6%)
  starting transfers between devices  5.42 us (4%)
    all_to_all x6, blocking collectives, exchange(): return lax.all_to_all(values, axes, 0, 0, tiled=True)  107 us
    pallas_call x10, Pallas kernels, call(): pl.pallas_call(kernel, out_shape=tuple((shape_of(*out) for out in outs)),...  19.4 us
    all_to_all x1, starting transfers between devices, exchange(): return lax.all_to_all(values, axes, 0, 0, tiled=True)  5.41 us
    all_to_all x1, waiting for transfers between devices, exchange(): return lax.all_to_all(values, axes, 0, 0, tiled=True)  4.96 us
    ppermute x3, waiting for transfers between devices, swap(): return lax.ppermute(values, 'core', [(0, 1), (1, 0)])  3.24 us
  transfers between devices with their start and end apart: 4, of which 4 were waited for; matrix products, arithmetic and copies ran while one was open for 0% of the time, Pallas kernels for 5%

profile of v6, /device:TPU:0, one launch (start us, length us, event | category | flops | bytes accessed | tf_op | source)
XLA Modules:
  0.0 141.3 jit_solution(12668384956102206117)
XLA Ops:
  0.6 5.4 %all-to-all-start = ((bf16[8,4,64,128]{3,2,1,0:T(8,128)(2,1)}), bf16[8,4,64,128]{3,2,1,0:T(8,128)(2,1)S(1)}, u32[]{:S(2)}, u32[]{:S(2)}) async-start(bf16[8,4,64,128]{3,2,1,0:T(8,128)(2,1)} %bitcast.14), calls=%async_computation | async-start | bytes 1048576 | tf_op jit(solution)/shard_map/all_to_all | solution.py:445
  6.0 3.0 %shard_map.202 = bf16[64,32,128]{2,1,0:T(8,128)(2,1)S(1)} custom-call(s32[512]{0:T(512)} %mask_s.3, s32[1,512]{1,0:T(1,128)} %bitcast.12, bf16[2048,128]{1,0:T(8,128)(2,1)} %bitcast.15, f32[1,128]{1,0:T(1,128)} %bitcast.19, bf16[128,256]{1,0:T(8,128)(2,1)} %weight.1), custom_call_target="tpu_custom_call" | custom-call | tf_op jit(solution)/shard_map/pallas_call | solution.py:78
  9.0 0.0 copy-start
  9.0 1.5 %shard_map.203 = (bf16[1168,128]{1,0:T(8,128)(2,1)S(1)}, bf16[128,256]{1,0:T(8,128)(2,1)S(1)}, f32[128,8]{1,0:T(8,128)S(1)}, f32[24,512]{1,0:T(8,128)S(1)}) custom-call(f32[1,128]{1,0:T(1,128)} %bitcast.20, bf16[128,128]{1,0:T(8,128)(2,1)} %refs_1_.1, f32[1,64]{1,0:T(1,128)} %bitcast.22, bf16[64,128]{1,0:T(8,128)(2,1)} %refs_3_.1, f32[1,128]{1,0:T(1,128)} %bitcast.23, ...), custom_call_target="tpu_custom_call" | custom-call | tf_op jit(solution)/shard_map/pallas_call | solution.py:78
  10.6 5.0 %all-to-all-done.x = bf16[8,4,64,128]{3,2,1,0:T(8,128)(2,1)S(1)} async-done(((bf16[8,4,64,128]{3,2,1,0:T(8,128)(2,1)}), bf16[8,4,64,128]{3,2,1,0:T(8,128)(2,1)S(1)}, u32[]{:S(2)}, u32[]{:S(2)}) %all-to-all-start) | async-done | bytes 524320 | tf_op jit(solution)/shard_map/all_to_all | solution.py:445
  15.5 21.6 %all_to_all.35.mine = bf16[64,32,128]{2,1,0:T(8,128)(2,1)S(1)} all-to-all(bf16[64,32,128]{2,1,0:T(8,128)(2,1)S(1)} %shard_map.202), channel_id=1, replica_groups=mesh['p'=8,'core'=2,'q'=8] {'p','q'}, dimensions={0} | all-to-all | bytes 1048576 | tf_op jit(solution)/shard_map/all_to_all | solution.py:445
  37.1 0.0 collective-permute-start
  37.1 1.2 shard_map.204
  38.3 0.7 collective-permute-done.other
  39.0 0.7 shard_map.205
  39.6 15.9 %all_to_all.36.recv = bf16[64,16,128]{2,1,0:T(8,128)(2,1)S(1)} all-to-all(bf16[64,16,128]{2,1,0:T(8,128)(2,1)S(1)} %get-tuple-element.60), channel_id=1, replica_groups=mesh['p'=8,'core'=2,'q'=8] {'p','q'}, dimensions={0} | all-to-all | bytes 524288 | tf_op jit(solution)/shard_map/all_to_all | solution.py:445
  55.5 0.0 copy-done
  55.5 2.2 %shard_map.206 = (bf16[64,32,128]{2,1,0:T(8,128)(2,1)S(1)}, f32[128,2048]{1,0:T(8,128)S(1)}) custom-call(s32[512]{0:T(512)S(1)} %copy-done, f32[24,512]{1,0:T(8,128)S(1)} %get-tuple-element.50.lines, bf16[64,16,128]{2,1,0:T(8,128)(2,1)S(1)} %all_to_all.36.recv, bf16[128,2048]{1,0:T(8,128)(2,1)S(1)} %get-tuple-element.61.state_in, ...), custom_call_target="tpu_custom_call" | custom-call | tf_op jit(solution)/shard_map/pallas_call | solution.py:78
  57.8 16.8 %all_to_all.37.mine = bf16[64,32,128]{2,1,0:T(8,128)(2,1)S(1)} all-to-all(bf16[64,32,128]{2,1,0:T(8,128)(2,1)S(1)} %get-tuple-element.64), channel_id=1, replica_groups=mesh['p'=8,'core'=2,'q'=8] {'p','q'}, dimensions={0} | all-to-all | bytes 1048576 | tf_op jit(solution)/shard_map/all_to_all | solution.py:445
  74.6 0.0 collective-permute-start.1
  74.6 0.6 shard_map.207
  75.2 1.3 collective-permute-done.1.other
  76.5 1.3 shard_map.208
  77.8 17.2 %all_to_all.38.recv = bf16[64,24,128]{2,1,0:T(8,128)(2,1)S(1)} all-to-all(bf16[64,24,128]{2,1,0:T(8,128)(2,1)S(1)} %shard_map.208), channel_id=1, replica_groups=mesh['p'=8,'core'=2,'q'=8] {'p','q'}, dimensions={0} | all-to-all | bytes 786432 | tf_op jit(solution)/shard_map/all_to_all | solution.py:445
  94.9 1.0 shard_map.209
  96.0 22.1 %all_to_all.39.mine = bf16[64,64,128]{2,1,0:T(8,128)(2,1)S(1)} all-to-all(bf16[64,64,128]{2,1,0:T(8,128)(2,1)S(1)} %get-tuple-element.75), channel_id=1, replica_groups=mesh['p'=8,'core'=2,'q'=8] {'p','q'}, dimensions={0} | all-to-all | bytes 2097152 | tf_op jit(solution)/shard_map/all_to_all | solution.py:445
  118.1 0.0 collective-permute-start.2
  118.1 1.4 shard_map.210
  119.5 1.3 collective-permute-done.2.bias_other
  120.7 6.5 %shard_map.211 = bf16[8,4,64,128]{3,2,1,0:T(8,128)(2,1)S(1)} custom-call(f32[24,512]{1,0:T(8,128)S(1)} %get-tuple-element.50.lines, f32[4096,128]{1,0:T(8,128)S(1)} %get-tuple-element.79.mine, bf16[64,64,128]{2,1,0:T(8,128)(2,1)S(1)} %collective-permute-done.2.bias_other, bf16[128,2048]{1,0:T(8,128)(2,1)S(1)} %get-tuple-element.82.query, ...), custom_call_target="tpu_custom_call" | custom-call | tf_op jit(solution)/shard_map/pallas_call | solution.py:78
  127.3 13.3 %all_to_all.40 = bf16[8,4,64,128]{3,2,1,0:T(8,128)(2,1)S(1)} all-to-all(bf16[8,4,64,128]{3,2,1,0:T(8,128)(2,1)S(1)} %shard_map.211), channel_id=1, replica_groups=mesh['p'=8,'core'=2,'q'=8] {'q'}, dimensions={0} | all-to-all | bytes 1048576 | tf_op jit(solution)/shard_map/all_to_all | solution.py:445
  140.5 0.8 copy.23
Async XLA Ops:
  0.6 14.9 %all-to-all-start = ((bf16[8,4,64,128]{3,2,1,0:T(8,128)(2,1)}), bf16[8,4,64,128]{3,2,1,0:T(8,128)(2,1)S(1)}, u32[]{:S(2)}, u32[]{:S(2)}) async-start(bf16[8,4,64,128]{3,2,1,0:T(8,128)(2,1)} %bitcast.14), calls=%async_computation | async-start | bytes 1048576 | tf_op jit(solution)/shard_map/all_to_all | solution.py:445
  9.0 46.5 %copy-start = (s32[512]{0:T(512)S(1)}, s32[512]{0:T(512)}, u32[]{:S(2)}) copy-start(s32[512]{0:T(512)} %mask_s.3) | copy-start | bytes 6148
  37.1 1.9 %collective-permute-start = (bf16[64,32,128]{2,1,0:T(8,128)(2,1)S(1)}, bf16[64,32,128]{2,1,0:T(8,128)(2,1)S(1)}, u32[]{:S(2)}, u32[]{:S(2)}) collective-permute-start(bf16[64,32,128]{2,1,0:T(8,128)(2,1)S(1)} %all_to_all.35.mine), channel_id=1, source_target_pairs={{0,8},{8,0},{1,9},{9,1},{2,10},{10,2},{3,11},{11,3},{4,12},{12,4},... | collective-permute-start | bytes 1572872 | tf_op jit(solution)/shard_map/ppermute | solution.py:441
  74.6 1.9 %collective-permute-start.1 = (bf16[64,32,128]{2,1,0:T(8,128)(2,1)S(1)}, bf16[64,32,128]{2,1,0:T(8,128)(2,1)S(1)}, u32[]{:S(2)}, u32[]{:S(2)}) collective-permute-start(bf16[64,32,128]{2,1,0:T(8,128)(2,1)S(1)} %all_to_all.37.mine), channel_id=1, source_target_pairs={{0,8},{8,0},{1,9},{9,1},{2,10},{10,2},{3,11},{11,3},{4,12},{12,4},... | collective-permute-start | bytes 1572872 | tf_op jit(solution)/shard_map/ppermute | solution.py:441
  118.1 2.7 %collective-permute-start.2 = (bf16[64,64,128]{2,1,0:T(8,128)(2,1)S(1)}, bf16[64,64,128]{2,1,0:T(8,128)(2,1)S(1)}, u32[]{:S(2)}, u32[]{:S(2)}) collective-permute-start(bf16[64,64,128]{2,1,0:T(8,128)(2,1)S(1)} %all_to_all.39.mine), channel_id=1, source_target_pairs={{0,8},{8,0},{1,9},{9,1},{2,10},{10,2},{3,11},{11,3},{4,12},{12,4},... | collective-permute-start | bytes 3145736 | tf_op jit(solution)/shard_map/ppermute | solution.py:441

commit v7 on v6

--- a/solution.py
+++ b/solution.py
@@ -410,14 +410,22 @@
 
     low = high = jnp.ones((1, NT), F32)
     parts = [[] for _ in range(4)]
-    for h in range(HEADS):
-        turn_bias(h)
-        for r in range(4):
-            span = slice(r * NT, (r + 1) * NT)
-            weights = jnp.exp2(scores(h, query[:, span], key[span, :]))
-            part, total = weighted(h, weights, value[:, span])
-            low, high = jnp.minimum(low, total), jnp.maximum(high, total)
-            parts[r].append(part)
+    def weights_of(h, r):
+        span = slice(r * NT, (r + 1) * NT)
+        return jnp.exp2(scores(h, query[:, span], key[span, :])).astype(BF16)
+
+    turn_bias(0)
+    order = [(h, r) for h in range(HEADS) for r in range(4)]
+    ahead = weights_of(0, 0)
+    for at, (h, r) in enumerate(order):
+        weights = ahead
+        if at + 1 < len(order):
+            if r == 2 and h + 1 < HEADS:
+                turn_bias(h + 1)
+            ahead = weights_of(*order[at + 1])
+        part, total = weighted(h, weights, value[:, r * NT : (r + 1) * NT])
+        low, high = jnp.minimum(low, total), jnp.maximum(high, total)
+        parts[r].append(part)
     for r in range(4):
         finish(r, slice(r * NT, (r + 1) * NT), parts[r])
     in_range = jnp.logical_and(jnp.min(low) > 1e-25, jnp.max(high) < 1e30)

time: 142 us -> 141 us (level)
  no operation moved by 1% of the time
where the time goes in v7:
time: 141 us
  blocking collectives  107 us (76%)
  Pallas kernels  18.7 us (13%)
  waiting for transfers between devices  8.2 us (6%)
  starting transfers between devices  5.42 us (4%)
    all_to_all x6, blocking collectives, exchange(): return lax.all_to_all(values, axes, 0, 0, tiled=True)  107 us
    pallas_call x10, Pallas kernels, call(): pl.pallas_call(kernel, out_shape=tuple((shape_of(*out) for out in outs)),...  18.7 us
    all_to_all x1, starting transfers between devices, exchange(): return lax.all_to_all(values, axes, 0, 0, tiled=True)  5.41 us
    all_to_all x1, waiting for transfers between devices, exchange(): return lax.all_to_all(values, axes, 0, 0, tiled=True)  4.96 us
    ppermute x3, waiting for transfers between devices, swap(): return lax.ppermute(values, 'core', [(0, 1), (1, 0)])  3.24 us
  transfers between devices with their start and end apart: 4, of which 4 were waited for; matrix products, arithmetic and copies ran while one was open for 0% of the time, Pallas kernels for 5%

profile of v7, /device:TPU:0, one launch (start us, length us, event | category | flops | bytes accessed | tf_op | source)
XLA Modules:
  0.0 140.6 jit_solution(2920187937444194203)
XLA Ops:
  0.6 5.4 %all-to-all-start = ((bf16[8,4,64,128]{3,2,1,0:T(8,128)(2,1)}), bf16[8,4,64,128]{3,2,1,0:T(8,128)(2,1)S(1)}, u32[]{:S(2)}, u32[]{:S(2)}) async-start(bf16[8,4,64,128]{3,2,1,0:T(8,128)(2,1)} %bitcast.14), calls=%async_computation | async-start | bytes 1048576 | tf_op jit(solution)/shard_map/all_to_all | solution.py:453
  6.0 3.0 %shard_map.202 = bf16[64,32,128]{2,1,0:T(8,128)(2,1)S(1)} custom-call(s32[512]{0:T(512)} %mask_s.3, s32[1,512]{1,0:T(1,128)} %bitcast.12, bf16[2048,128]{1,0:T(8,128)(2,1)} %bitcast.15, f32[1,128]{1,0:T(1,128)} %bitcast.19, bf16[128,256]{1,0:T(8,128)(2,1)} %weight.1), custom_call_target="tpu_custom_call" | custom-call | tf_op jit(solution)/shard_map/pallas_call | solution.py:78
  9.0 0.0 copy-start
  9.0 1.5 %shard_map.203 = (bf16[1168,128]{1,0:T(8,128)(2,1)S(1)}, bf16[128,256]{1,0:T(8,128)(2,1)S(1)}, f32[128,8]{1,0:T(8,128)S(1)}, f32[24,512]{1,0:T(8,128)S(1)}) custom-call(f32[1,128]{1,0:T(1,128)} %bitcast.20, bf16[128,128]{1,0:T(8,128)(2,1)} %refs_1_.1, f32[1,64]{1,0:T(1,128)} %bitcast.22, bf16[64,128]{1,0:T(8,128)(2,1)} %refs_3_.1, f32[1,128]{1,0:T(1,128)} %bitcast.23, ...), custom_call_target="tpu_custom_call" | custom-call | tf_op jit(solution)/shard_map/pallas_call | solution.py:78
  10.6 5.0 %all-to-all-done.x = bf16[8,4,64,128]{3,2,1,0:T(8,128)(2,1)S(1)} async-done(((bf16[8,4,64,128]{3,2,1,0:T(8,128)(2,1)}), bf16[8,4,64,128]{3,2,1,0:T(8,128)(2,1)S(1)}, u32[]{:S(2)}, u32[]{:S(2)}) %all-to-all-start) | async-done | bytes 524320 | tf_op jit(solution)/shard_map/all_to_all | solution.py:453
  15.5 21.6 %all_to_all.35.mine = bf16[64,32,128]{2,1,0:T(8,128)(2,1)S(1)} all-to-all(bf16[64,32,128]{2,1,0:T(8,128)(2,1)S(1)} %shard_map.202), channel_id=1, replica_groups=mesh['p'=8,'core'=2,'q'=8] {'p','q'}, dimensions={0} | all-to-all | bytes 1048576 | tf_op jit(solution)/shard_map/all_to_all | solution.py:453
  37.1 0.0 collective-permute-start
  37.1 1.2 shard_map.204
  38.3 0.7 collective-permute-done.other
  39.0 0.7 shard_map.205
  39.6 15.9 %all_to_all.36.recv = bf16[64,16,128]{2,1,0:T(8,128)(2,1)S(1)} all-to-all(bf16[64,16,128]{2,1,0:T(8,128)(2,1)S(1)} %get-tuple-element.60), channel_id=1, replica_groups=mesh['p'=8,'core'=2,'q'=8] {'p','q'}, dimensions={0} | all-to-all | bytes 524288 | tf_op jit(solution)/shard_map/all_to_all | solution.py:453
  55.5 0.0 copy-done
  55.5 2.2 %shard_map.206 = (bf16[64,32,128]{2,1,0:T(8,128)(2,1)S(1)}, f32[128,2048]{1,0:T(8,128)S(1)}) custom-call(s32[512]{0:T(512)S(1)} %copy-done, f32[24,512]{1,0:T(8,128)S(1)} %get-tuple-element.50.lines, bf16[64,16,128]{2,1,0:T(8,128)(2,1)S(1)} %all_to_all.36.recv, bf16[128,2048]{1,0:T(8,128)(2,1)S(1)} %get-tuple-element.61.state_in, ...), custom_call_target="tpu_custom_call" | custom-call | tf_op jit(solution)/shard_map/pallas_call | solution.py:78
  57.8 16.8 %all_to_all.37.mine = bf16[64,32,128]{2,1,0:T(8,128)(2,1)S(1)} all-to-all(bf16[64,32,128]{2,1,0:T(8,128)(2,1)S(1)} %get-tuple-element.64), channel_id=1, replica_groups=mesh['p'=8,'core'=2,'q'=8] {'p','q'}, dimensions={0} | all-to-all | bytes 1048576 | tf_op jit(solution)/shard_map/all_to_all | solution.py:453
  74.6 0.0 collective-permute-start.1
  74.6 0.6 shard_map.207
  75.2 1.3 collective-permute-done.1.other
  76.5 1.3 shard_map.208
  77.8 17.2 %all_to_all.38.recv = bf16[64,24,128]{2,1,0:T(8,128)(2,1)S(1)} all-to-all(bf16[64,24,128]{2,1,0:T(8,128)(2,1)S(1)} %shard_map.208), channel_id=1, replica_groups=mesh['p'=8,'core'=2,'q'=8] {'p','q'}, dimensions={0} | all-to-all | bytes 786432 | tf_op jit(solution)/shard_map/all_to_all | solution.py:453
  94.9 1.0 shard_map.209
  96.0 22.1 %all_to_all.39.mine = bf16[64,64,128]{2,1,0:T(8,128)(2,1)S(1)} all-to-all(bf16[64,64,128]{2,1,0:T(8,128)(2,1)S(1)} %get-tuple-element.75), channel_id=1, replica_groups=mesh['p'=8,'core'=2,'q'=8] {'p','q'}, dimensions={0} | all-to-all | bytes 2097152 | tf_op jit(solution)/shard_map/all_to_all | solution.py:453
  118.1 0.0 collective-permute-start.2
  118.1 1.4 shard_map.210
  119.5 1.3 collective-permute-done.2.bias_other
  120.7 5.8 %shard_map.211 = bf16[8,4,64,128]{3,2,1,0:T(8,128)(2,1)S(1)} custom-call(f32[24,512]{1,0:T(8,128)S(1)} %get-tuple-element.50.lines, f32[4096,128]{1,0:T(8,128)S(1)} %get-tuple-element.79.mine, bf16[64,64,128]{2,1,0:T(8,128)(2,1)S(1)} %collective-permute-done.2.bias_other, bf16[128,2048]{1,0:T(8,128)(2,1)S(1)} %get-tuple-element.82.query, ...), custom_call_target="tpu_custom_call" | custom-call | tf_op jit(solution)/shard_map/pallas_call | solution.py:78
  126.5 13.3 %all_to_all.40 = bf16[8,4,64,128]{3,2,1,0:T(8,128)(2,1)S(1)} all-to-all(bf16[8,4,64,128]{3,2,1,0:T(8,128)(2,1)S(1)} %shard_map.211), channel_id=1, replica_groups=mesh['p'=8,'core'=2,'q'=8] {'q'}, dimensions={0} | all-to-all | bytes 1048576 | tf_op jit(solution)/shard_map/all_to_all | solution.py:453
  139.8 0.8 copy.23
Async XLA Ops:
  0.6 14.9 %all-to-all-start = ((bf16[8,4,64,128]{3,2,1,0:T(8,128)(2,1)}), bf16[8,4,64,128]{3,2,1,0:T(8,128)(2,1)S(1)}, u32[]{:S(2)}, u32[]{:S(2)}) async-start(bf16[8,4,64,128]{3,2,1,0:T(8,128)(2,1)} %bitcast.14), calls=%async_computation | async-start | bytes 1048576 | tf_op jit(solution)/shard_map/all_to_all | solution.py:453
  9.0 46.5 %copy-start = (s32[512]{0:T(512)S(1)}, s32[512]{0:T(512)}, u32[]{:S(2)}) copy-start(s32[512]{0:T(512)} %mask_s.3) | copy-start | bytes 6148
  37.1 1.9 %collective-permute-start = (bf16[64,32,128]{2,1,0:T(8,128)(2,1)S(1)}, bf16[64,32,128]{2,1,0:T(8,128)(2,1)S(1)}, u32[]{:S(2)}, u32[]{:S(2)}) collective-permute-start(bf16[64,32,128]{2,1,0:T(8,128)(2,1)S(1)} %all_to_all.35.mine), channel_id=1, source_target_pairs={{0,8},{8,0},{1,9},{9,1},{2,10},{10,2},{3,11},{11,3},{4,12},{12,4},... | collective-permute-start | bytes 1572872 | tf_op jit(solution)/shard_map/ppermute | solution.py:449
  74.6 1.9 %collective-permute-start.1 = (bf16[64,32,128]{2,1,0:T(8,128)(2,1)S(1)}, bf16[64,32,128]{2,1,0:T(8,128)(2,1)S(1)}, u32[]{:S(2)}, u32[]{:S(2)}) collective-permute-start(bf16[64,32,128]{2,1,0:T(8,128)(2,1)S(1)} %all_to_all.37.mine), channel_id=1, source_target_pairs={{0,8},{8,0},{1,9},{9,1},{2,10},{10,2},{3,11},{11,3},{4,12},{12,4},... | collective-permute-start | bytes 1572872 | tf_op jit(solution)/shard_map/ppermute | solution.py:449
  118.1 2.7 %collective-permute-start.2 = (bf16[64,64,128]{2,1,0:T(8,128)(2,1)S(1)}, bf16[64,64,128]{2,1,0:T(8,128)(2,1)S(1)}, u32[]{:S(2)}, u32[]{:S(2)}) collective-permute-start(bf16[64,64,128]{2,1,0:T(8,128)(2,1)S(1)} %all_to_all.39.mine), channel_id=1, source_target_pairs={{0,8},{8,0},{1,9},{9,1},{2,10},{10,2},{3,11},{11,3},{4,12},{12,4},... | collective-permute-start | bytes 3145736 | tf_op jit(solution)/shard_map/ppermute | solution.py:449

commit v8 on v7

--- a/solution.py
+++ b/solution.py
@@ -174,8 +174,7 @@
     packed[VALUE, :] = flipped(att_qkv[:, 256:384])
     packed[ATT_GATE, :] = flipped(att_gate[...])
     packed[ATT_OUT, :] = flipped(att_out[...])
-    turned = jnp.concatenate([att_bias[...], jnp.zeros((16 - HEADS, CZ), BF16)], axis=0)
-    packed[BIAS.start : PACKED, :] = turned
+    packed[BIAS.start : PACKED, :] = att_bias[...]
     for at, weight in enumerate((out_final, out_final, in_final, in_final)):
         finals[:, at * CM : (at + 1) * CM] = flipped(weight[...])
     pad = jnp.zeros((1, CM), F32)
@@ -487,9 +486,10 @@
         [("s", token_mask), ("w", mask_v), ("w", pair_input.reshape(tokens, CZ)),
          ("w", row(out_norm_gain)), ("w", out_proj)],
     )
+    heads_t = jnp.pad(att_bias.T, ((0, 16 - HEADS), (0, 0)))
     weights = (
         row(out_norm_gain), out_gate, row(out_final_gain), out_final, row(in_norm_gain), in_proj, in_gate,
-        row(in_final_gain), in_final, row(att_norm_gain), att_qkv, att_bias.T, att_gate, att_out,
+        row(in_final_gain), in_final, row(att_norm_gain), att_qkv, heads_t, att_gate, att_out,
         mask_v, row(out_check_weights), row(in_check_weights),
     )
     packed, finals, gains, lines = call(

time: 141 us -> 141 us (level)
  transfers between devices with their start and end apart: 4 -> 4, of which waited for: 4 -> 4; matrix products, arithmetic and copies ran while one was open for 0% -> 1% of each run, Pallas kernels for 5% -> 5%
where the time goes in v8:
time: 141 us
  blocking collectives  107 us (76%)
  Pallas kernels  18.7 us (13%)
  waiting for transfers between devices  6.96 us (5%)
  starting transfers between devices  5.42 us (4%)
  local copies, waits for them, and re-layouts  2.08 us (1%)
    all_to_all x6, blocking collectives, exchange(): return lax.all_to_all(values, axes, 0, 0, tiled=True)  107 us
    pallas_call x10, Pallas kernels, call(): pl.pallas_call(kernel, out_shape=tuple((shape_of(*out) for out in outs)),...  18.7 us
    all_to_all x1, starting transfers between devices, exchange(): return lax.all_to_all(values, axes, 0, 0, tiled=True)  5.41 us
    all_to_all x1, waiting for transfers between devices, exchange(): return lax.all_to_all(values, axes, 0, 0, tiled=True)  3.71 us
    ppermute x3, waiting for transfers between devices, swap(): return lax.ppermute(values, 'core', [(0, 1), (1, 0)])  3.25 us
  transfers between devices with their start and end apart: 4, of which 4 were waited for; matrix products, arithmetic and copies ran while one was open for 1% of the time, Pallas kernels for 5%

profile of v8, /device:TPU:0, one launch (start us, length us, event | category | flops | bytes accessed | tf_op | source)
XLA Modules:
  0.0 140.6 jit_solution(11508083196718935422)
XLA Ops:
  0.6 5.4 %all-to-all-start = ((bf16[8,4,64,128]{3,2,1,0:T(8,128)(2,1)}), bf16[8,4,64,128]{3,2,1,0:T(8,128)(2,1)S(1)}, u32[]{:S(2)}, u32[]{:S(2)}) async-start(bf16[8,4,64,128]{3,2,1,0:T(8,128)(2,1)} %bitcast.14), calls=%async_computation | async-start | bytes 1048576 | tf_op jit(solution)/shard_map/all_to_all | solution.py:452
  6.0 1.3 pad.4.refs_11_
  7.3 2.9 %shard_map.202 = bf16[64,32,128]{2,1,0:T(8,128)(2,1)S(1)} custom-call(s32[512]{0:T(512)} %mask_s.3, s32[1,512]{1,0:T(1,128)} %bitcast.12, bf16[2048,128]{1,0:T(8,128)(2,1)} %bitcast.15, f32[1,128]{1,0:T(1,128)} %bitcast.19, bf16[128,256]{1,0:T(8,128)(2,1)} %weight.1), custom_call_target="tpu_custom_call" | custom-call | tf_op jit(solution)/shard_map/pallas_call | solution.py:78
  10.3 0.0 copy-start
  10.3 1.5 %shard_map.203 = (bf16[1168,128]{1,0:T(8,128)(2,1)S(1)}, bf16[128,256]{1,0:T(8,128)(2,1)S(1)}, f32[128,8]{1,0:T(8,128)S(1)}, f32[24,512]{1,0:T(8,128)S(1)}) custom-call(f32[1,128]{1,0:T(1,128)} %bitcast.20, bf16[128,128]{1,0:T(8,128)(2,1)} %refs_1_.1, f32[1,64]{1,0:T(1,128)} %bitcast.22, bf16[64,128]{1,0:T(8,128)(2,1)} %refs_3_.1, f32[1,128]{1,0:T(1,128)} %bitcast.23, ...), custom_call_target="tpu_custom_call" | custom-call | tf_op jit(solution)/shard_map/pallas_call | solution.py:78
  11.8 3.7 %all-to-all-done.x = bf16[8,4,64,128]{3,2,1,0:T(8,128)(2,1)S(1)} async-done(((bf16[8,4,64,128]{3,2,1,0:T(8,128)(2,1)}), bf16[8,4,64,128]{3,2,1,0:T(8,128)(2,1)S(1)}, u32[]{:S(2)}, u32[]{:S(2)}) %all-to-all-start) | async-done | bytes 524320 | tf_op jit(solution)/shard_map/all_to_all | solution.py:452
  15.5 21.6 %all_to_all.35.mine = bf16[64,32,128]{2,1,0:T(8,128)(2,1)S(1)} all-to-all(bf16[64,32,128]{2,1,0:T(8,128)(2,1)S(1)} %shard_map.202), channel_id=1, replica_groups=mesh['p'=8,'core'=2,'q'=8] {'p','q'}, dimensions={0} | all-to-all | bytes 1048576 | tf_op jit(solution)/shard_map/all_to_all | solution.py:452
  37.1 0.0 collective-permute-start
  37.1 1.2 shard_map.204
  38.3 0.7 collective-permute-done.other
  39.0 0.7 shard_map.205
  39.6 15.9 %all_to_all.36.recv = bf16[64,16,128]{2,1,0:T(8,128)(2,1)S(1)} all-to-all(bf16[64,16,128]{2,1,0:T(8,128)(2,1)S(1)} %get-tuple-element.60), channel_id=1, replica_groups=mesh['p'=8,'core'=2,'q'=8] {'p','q'}, dimensions={0} | all-to-all | bytes 524288 | tf_op jit(solution)/shard_map/all_to_all | solution.py:452
  55.5 0.0 copy-done
  55.5 2.2 %shard_map.206 = (bf16[64,32,128]{2,1,0:T(8,128)(2,1)S(1)}, f32[128,2048]{1,0:T(8,128)S(1)}) custom-call(s32[512]{0:T(512)S(1)} %copy-done, f32[24,512]{1,0:T(8,128)S(1)} %get-tuple-element.50.lines, bf16[64,16,128]{2,1,0:T(8,128)(2,1)S(1)} %all_to_all.36.recv, bf16[128,2048]{1,0:T(8,128)(2,1)S(1)} %get-tuple-element.61.state_in, ...), custom_call_target="tpu_custom_call" | custom-call | tf_op jit(solution)/shard_map/pallas_call | solution.py:78
  57.8 16.8 %all_to_all.37.mine = bf16[64,32,128]{2,1,0:T(8,128)(2,1)S(1)} all-to-all(bf16[64,32,128]{2,1,0:T(8,128)(2,1)S(1)} %get-tuple-element.64), channel_id=1, replica_groups=mesh['p'=8,'core'=2,'q'=8] {'p','q'}, dimensions={0} | all-to-all | bytes 1048576 | tf_op jit(solution)/shard_map/all_to_all | solution.py:452
  74.6 0.0 collective-permute-start.1
  74.6 0.6 shard_map.207
  75.2 1.3 collective-permute-done.1.other
  76.5 1.3 shard_map.208
  77.8 17.2 %all_to_all.38.recv = bf16[64,24,128]{2,1,0:T(8,128)(2,1)S(1)} all-to-all(bf16[64,24,128]{2,1,0:T(8,128)(2,1)S(1)} %shard_map.208), channel_id=1, replica_groups=mesh['p'=8,'core'=2,'q'=8] {'p','q'}, dimensions={0} | all-to-all | bytes 786432 | tf_op jit(solution)/shard_map/all_to_all | solution.py:452
  94.9 1.0 shard_map.209
  96.0 22.1 %all_to_all.39.mine = bf16[64,64,128]{2,1,0:T(8,128)(2,1)S(1)} all-to-all(bf16[64,64,128]{2,1,0:T(8,128)(2,1)S(1)} %get-tuple-element.75), channel_id=1, replica_groups=mesh['p'=8,'core'=2,'q'=8] {'p','q'}, dimensions={0} | all-to-all | bytes 2097152 | tf_op jit(solution)/shard_map/all_to_all | solution.py:452
  118.1 0.0 collective-permute-start.2
  118.1 1.4 shard_map.210
  119.5 1.3 collective-permute-done.2.bias_other
  120.7 5.8 %shard_map.211 = bf16[8,4,64,128]{3,2,1,0:T(8,128)(2,1)S(1)} custom-call(f32[24,512]{1,0:T(8,128)S(1)} %get-tuple-element.50.lines, f32[4096,128]{1,0:T(8,128)S(1)} %get-tuple-element.79.mine, bf16[64,64,128]{2,1,0:T(8,128)(2,1)S(1)} %collective-permute-done.2.bias_other, bf16[128,2048]{1,0:T(8,128)(2,1)S(1)} %get-tuple-element.82.query, ...), custom_call_target="tpu_custom_call" | custom-call | tf_op jit(solution)/shard_map/pallas_call | solution.py:78
  126.5 13.3 %all_to_all.40 = bf16[8,4,64,128]{3,2,1,0:T(8,128)(2,1)S(1)} all-to-all(bf16[8,4,64,128]{3,2,1,0:T(8,128)(2,1)S(1)} %shard_map.211), channel_id=1, replica_groups=mesh['p'=8,'core'=2,'q'=8] {'q'}, dimensions={0} | all-to-all | bytes 1048576 | tf_op jit(solution)/shard_map/all_to_all | solution.py:452
  139.8 0.8 copy.23
Async XLA Ops:
  0.6 14.9 %all-to-all-start = ((bf16[8,4,64,128]{3,2,1,0:T(8,128)(2,1)}), bf16[8,4,64,128]{3,2,1,0:T(8,128)(2,1)S(1)}, u32[]{:S(2)}, u32[]{:S(2)}) async-start(bf16[8,4,64,128]{3,2,1,0:T(8,128)(2,1)} %bitcast.14), calls=%async_computation | async-start | bytes 1048576 | tf_op jit(solution)/shard_map/all_to_all | solution.py:452
  10.3 45.3 %copy-start = (s32[512]{0:T(512)S(1)}, s32[512]{0:T(512)}, u32[]{:S(2)}) copy-start(s32[512]{0:T(512)} %mask_s.3) | copy-start | bytes 6148
  37.1 1.9 %collective-permute-start = (bf16[64,32,128]{2,1,0:T(8,128)(2,1)S(1)}, bf16[64,32,128]{2,1,0:T(8,128)(2,1)S(1)}, u32[]{:S(2)}, u32[]{:S(2)}) collective-permute-start(bf16[64,32,128]{2,1,0:T(8,128)(2,1)S(1)} %all_to_all.35.mine), channel_id=1, source_target_pairs={{0,8},{8,0},{1,9},{9,1},{2,10},{10,2},{3,11},{11,3},{4,12},{12,4},... | collective-permute-start | bytes 1572872 | tf_op jit(solution)/shard_map/ppermute | solution.py:448
  74.6 1.9 %collective-permute-start.1 = (bf16[64,32,128]{2,1,0:T(8,128)(2,1)S(1)}, bf16[64,32,128]{2,1,0:T(8,128)(2,1)S(1)}, u32[]{:S(2)}, u32[]{:S(2)}) collective-permute-start(bf16[64,32,128]{2,1,0:T(8,128)(2,1)S(1)} %all_to_all.37.mine), channel_id=1, source_target_pairs={{0,8},{8,0},{1,9},{9,1},{2,10},{10,2},{3,11},{11,3},{4,12},{12,4},... | collective-permute-start | bytes 1572872 | tf_op jit(solution)/shard_map/ppermute | solution.py:448
  118.1 2.7 %collective-permute-start.2 = (bf16[64,64,128]{2,1,0:T(8,128)(2,1)S(1)}, bf16[64,64,128]{2,1,0:T(8,128)(2,1)S(1)}, u32[]{:S(2)}, u32[]{:S(2)}) collective-permute-start(bf16[64,64,128]{2,1,0:T(8,128)(2,1)S(1)} %all_to_all.39.mine), channel_id=1, source_target_pairs={{0,8},{8,0},{1,9},{9,1},{2,10},{10,2},{3,11},{11,3},{4,12},{12,4},... | collective-permute-start | bytes 3145736 | tf_op jit(solution)/shard_map/ppermute | solution.py:448

commit v9 on v8

--- a/solution.py
+++ b/solution.py
@@ -307,8 +307,9 @@
     lines = []
     for part, count in ((high, 2), (check_in[...] - high, 2), (total / NT, 4)):
         lines += [part[0:1, c * LANES : (c + 1) * LANES] for c in range(count)]
+    lines.append(jnp.zeros((8, LANES), F32))
     tail = jnp.concatenate(lines, axis=0).astype(BF16)
-    out[:, 16:24, :] = jnp.broadcast_to(tail[None], (64, 8, LANES))
+    out[:, 16:32, :] = jnp.broadcast_to(tail[None], (64, 16, LANES))
 
 
 def bias_rows(
@@ -320,12 +321,12 @@
     final_col = gains[0:CM, 4:5]
     final_t = finals[:, 2 * CM : 4 * CM]
     weight_t = packed[BIAS.start : PACKED, :]
-    recv_stage[...] = recv[...].astype(F32).reshape(CM * 24, LANES)
+    recv_stage[...] = recv[...].astype(F32).reshape(CM * 32, LANES)
     for group in range(0, 4, GROUP):
         members = range(group, group + GROUP)
         span = slice(group * NT, (group + GROUP) * NT)
         state = update_rows(
-            recv_stage, 24, members, state_in[:, span], gate[:, span], final_col, final_t
+            recv_stage, 32, members, state_in[:, span], gate[:, span], final_col, final_t
         )
         state_out[:, span] = state.astype(BF16)
         normed = norm(state, gain_col)
@@ -348,11 +349,11 @@
     recv_stage, turn,
 ):
     mine_out[...] = mine[...].astype(F32).reshape(64 * 64, LANES)
-    recv_stage[...] = recv[:, 16:24, :].astype(F32).reshape(CM * 8, LANES)
+    recv_stage[...] = recv[:, 16:32, :].astype(F32).reshape(CM * 16, LANES)
     p, q = lax.axis_index("p"), lax.axis_index("q")
 
     def rows_of(at):
-        return recv_stage[pl.ds(at, CM, stride=8), :]
+        return recv_stage[pl.ds(at, CM, stride=16), :]
 
     turn[0] = jnp.transpose(rows_of(p // 4) + rows_of(2 + p // 4))
     check_row[...] = turn[0, pl.ds(pl.multiple_of(lax.rem(p, 4) * 32, 32), 32), :]
@@ -538,7 +539,7 @@
     other, gate, check_out = lax.optimization_barrier((other, gate, check_out))
     (sent,) = call(
         product_cols,
-        [((64, 24, LANES), BF16)],
+        [((64, 32, LANES), BF16)],
         [((NT, NT), BF16), ((NT, NT), BF16), ((NT, NT), F32), ((64 * 32, LANES), F32),
          ((1024, LANES), F32)],
         [("v", mine), ("v", other), ("v", lines), ("v", check_out)],
@@ -547,7 +548,7 @@
     sent, state, normed = call(
         bias_rows,
         [((64, 64, LANES), BF16), (wide, BF16), (wide, BF16)],
-        [((CM * 24, LANES), F32), ((64, LANES), F32)],
+        [((CM * 32, LANES), F32), ((64, LANES), F32)],
         [("v", lines), ("v", recv), ("v", state), ("v", gate), ("v", packed), ("v", finals),
          ("v", gains)],
     )
@@ -558,7 +559,7 @@
         attention_inputs,
         [(wide, BF16), ((tokens, CZ), BF16), (wide, BF16), (wide, BF16), ((32, CM), F32),
          ((64, CM), F32), ((64 * 64, LANES), F32)],
-        [((CM * 8, LANES), F32), ((2, LANES, CM), F32)],
+        [((CM * 16, LANES), F32), ((2, LANES, CM), F32)],
         [("v", recv), ("v", mine), ("v", normed), ("v", packed)],
     )
     other, query = lax.optimization_barrier((other, query))

time: 141 us -> 143 us (1.014)
    all_to_all x6, blocking collectives: 107 us -> 108 us  [exchange(): return lax.all_to_all(values, axes, 0, 0, tiled=True)]
where the time goes in v9:
time: 143 us; the launch traced here: 142 us
  blocking collectives  108 us (76%)
  Pallas kernels  19 us (13%)
  waiting for transfers between devices  6.91 us (5%)
  starting transfers between devices  5.42 us (4%)
  local copies, waits for them, and re-layouts  2.08 us (1%)
    all_to_all x6, blocking collectives, exchange(): return lax.all_to_all(values, axes, 0, 0, tiled=True)  108 us
    pallas_call x10, Pallas kernels, call(): pl.pallas_call(kernel, out_shape=tuple((shape_of(*out) for out in outs)),...  19 us
    all_to_all x1, starting transfers between devices, exchange(): return lax.all_to_all(values, axes, 0, 0, tiled=True)  5.41 us
    all_to_all x1, waiting for transfers between devices, exchange(): return lax.all_to_all(values, axes, 0, 0, tiled=True)  3.71 us
    ppermute x3, waiting for transfers between devices, swap(): return lax.ppermute(values, 'core', [(0, 1), (1, 0)])  3.2 us
  transfers between devices with their start and end apart: 4, of which 4 were waited for; matrix products, arithmetic and copies ran while one was open for 1% of the time, Pallas kernels for 5%

profile of v9, /device:TPU:0, one launch (start us, length us, event | category | flops | bytes accessed | tf_op | source)
XLA Modules:
  0.0 142.3 jit_solution(15217681422650482958)
XLA Ops:
  0.6 5.4 %all-to-all-start = ((bf16[8,4,64,128]{3,2,1,0:T(8,128)(2,1)}), bf16[8,4,64,128]{3,2,1,0:T(8,128)(2,1)S(1)}, u32[]{:S(2)}, u32[]{:S(2)}) async-start(bf16[8,4,64,128]{3,2,1,0:T(8,128)(2,1)} %bitcast.14), calls=%async_computation | async-start | bytes 1048576 | tf_op jit(solution)/shard_map/all_to_all | solution.py:453
  6.0 1.3 pad.4.refs_11_
  7.3 2.9 %shard_map.202 = bf16[64,32,128]{2,1,0:T(8,128)(2,1)S(1)} custom-call(s32[512]{0:T(512)} %mask_s.3, s32[1,512]{1,0:T(1,128)} %bitcast.12, bf16[2048,128]{1,0:T(8,128)(2,1)} %bitcast.15, f32[1,128]{1,0:T(1,128)} %bitcast.19, bf16[128,256]{1,0:T(8,128)(2,1)} %weight.1), custom_call_target="tpu_custom_call" | custom-call | tf_op jit(solution)/shard_map/pallas_call | solution.py:78
  10.3 0.0 copy-start
  10.3 1.5 %shard_map.203 = (bf16[1168,128]{1,0:T(8,128)(2,1)S(1)}, bf16[128,256]{1,0:T(8,128)(2,1)S(1)}, f32[128,8]{1,0:T(8,128)S(1)}, f32[24,512]{1,0:T(8,128)S(1)}) custom-call(f32[1,128]{1,0:T(1,128)} %bitcast.20, bf16[128,128]{1,0:T(8,128)(2,1)} %refs_1_.1, f32[1,64]{1,0:T(1,128)} %bitcast.22, bf16[64,128]{1,0:T(8,128)(2,1)} %refs_3_.1, f32[1,128]{1,0:T(1,128)} %bitcast.23, ...), custom_call_target="tpu_custom_call" | custom-call | tf_op jit(solution)/shard_map/pallas_call | solution.py:78
  11.8 3.7 %all-to-all-done.x = bf16[8,4,64,128]{3,2,1,0:T(8,128)(2,1)S(1)} async-done(((bf16[8,4,64,128]{3,2,1,0:T(8,128)(2,1)}), bf16[8,4,64,128]{3,2,1,0:T(8,128)(2,1)S(1)}, u32[]{:S(2)}, u32[]{:S(2)}) %all-to-all-start) | async-done | bytes 524320 | tf_op jit(solution)/shard_map/all_to_all | solution.py:453
  15.5 21.6 %all_to_all.35.mine = bf16[64,32,128]{2,1,0:T(8,128)(2,1)S(1)} all-to-all(bf16[64,32,128]{2,1,0:T(8,128)(2,1)S(1)} %shard_map.202), channel_id=1, replica_groups=mesh['p'=8,'core'=2,'q'=8] {'p','q'}, dimensions={0} | all-to-all | bytes 1048576 | tf_op jit(solution)/shard_map/all_to_all | solution.py:453
  37.1 0.0 collective-permute-start
  37.1 1.2 shard_map.204
  38.3 0.7 collective-permute-done.other
  39.0 0.7 shard_map.205
  39.6 15.9 %all_to_all.36.recv = bf16[64,16,128]{2,1,0:T(8,128)(2,1)S(1)} all-to-all(bf16[64,16,128]{2,1,0:T(8,128)(2,1)S(1)} %get-tuple-element.60), channel_id=1, replica_groups=mesh['p'=8,'core'=2,'q'=8] {'p','q'}, dimensions={0} | all-to-all | bytes 524288 | tf_op jit(solution)/shard_map/all_to_all | solution.py:453
  55.5 0.0 copy-done
  55.5 2.2 %shard_map.206 = (bf16[64,32,128]{2,1,0:T(8,128)(2,1)S(1)}, f32[128,2048]{1,0:T(8,128)S(1)}) custom-call(s32[512]{0:T(512)S(1)} %copy-done, f32[24,512]{1,0:T(8,128)S(1)} %get-tuple-element.50.lines, bf16[64,16,128]{2,1,0:T(8,128)(2,1)S(1)} %all_to_all.36.recv, bf16[128,2048]{1,0:T(8,128)(2,1)S(1)} %get-tuple-element.61.state_in, ...), custom_call_target="tpu_custom_call" | custom-call | tf_op jit(solution)/shard_map/pallas_call | solution.py:78
  57.8 16.8 %all_to_all.37.mine = bf16[64,32,128]{2,1,0:T(8,128)(2,1)S(1)} all-to-all(bf16[64,32,128]{2,1,0:T(8,128)(2,1)S(1)} %get-tuple-element.64), channel_id=1, replica_groups=mesh['p'=8,'core'=2,'q'=8] {'p','q'}, dimensions={0} | all-to-all | bytes 1048576 | tf_op jit(solution)/shard_map/all_to_all | solution.py:453
  74.6 0.0 collective-permute-start.1
  74.6 0.6 shard_map.207
  75.2 1.3 collective-permute-done.1.other
  76.5 1.3 shard_map.208
  77.8 18.4 %all_to_all.38.recv = bf16[64,32,128]{2,1,0:T(8,128)(2,1)S(1)} all-to-all(bf16[64,32,128]{2,1,0:T(8,128)(2,1)S(1)} %shard_map.208), channel_id=1, replica_groups=mesh['p'=8,'core'=2,'q'=8] {'p','q'}, dimensions={0} | all-to-all | bytes 1048576 | tf_op jit(solution)/shard_map/all_to_all | solution.py:453
  96.2 1.3 shard_map.209
  97.5 22.3 %all_to_all.39.mine = bf16[64,64,128]{2,1,0:T(8,128)(2,1)S(1)} all-to-all(bf16[64,64,128]{2,1,0:T(8,128)(2,1)S(1)} %get-tuple-element.75), channel_id=1, replica_groups=mesh['p'=8,'core'=2,'q'=8] {'p','q'}, dimensions={0} | all-to-all | bytes 2097152 | tf_op jit(solution)/shard_map/all_to_all | solution.py:453
  119.8 0.0 collective-permute-start.2
  119.8 1.4 %shard_map.210 = (bf16[128,2048]{1,0:T(8,128)(2,1)S(1)}, bf16[2048,128]{1,0:T(8,128)(2,1)S(1)}, bf16[128,2048]{1,0:T(8,128)(2,1)S(1)}, bf16[128,2048]{1,0:T(8,12...) custom-call(bf16[64,32,128]{2,1,0:T(8,128)(2,1)S(1)} %all_to_all.38.recv, ...), custom_call_target="tpu_custom_call" | custom-call | tf_op jit(solution)/shard_map/pallas_call | solution.py:78
  121.2 1.2 collective-permute-done.2.bias_other
  122.5 5.8 %shard_map.211 = bf16[8,4,64,128]{3,2,1,0:T(8,128)(2,1)S(1)} custom-call(f32[24,512]{1,0:T(8,128)S(1)} %get-tuple-element.50.lines, f32[4096,128]{1,0:T(8,128)S(1)} %get-tuple-element.79.mine, bf16[64,64,128]{2,1,0:T(8,128)(2,1)S(1)} %collective-permute-done.2.bias_other, bf16[128,2048]{1,0:T(8,128)(2,1)S(1)} %get-tuple-element.82.query, ...), custom_call_target="tpu_custom_call" | custom-call | tf_op jit(solution)/shard_map/pallas_call | solution.py:78
  128.3 13.3 %all_to_all.40 = bf16[8,4,64,128]{3,2,1,0:T(8,128)(2,1)S(1)} all-to-all(bf16[8,4,64,128]{3,2,1,0:T(8,128)(2,1)S(1)} %shard_map.211), channel_id=1, replica_groups=mesh['p'=8,'core'=2,'q'=8] {'q'}, dimensions={0} | all-to-all | bytes 1048576 | tf_op jit(solution)/shard_map/all_to_all | solution.py:453
  141.5 0.8 copy.23
Async XLA Ops:
  0.6 14.9 %all-to-all-start = ((bf16[8,4,64,128]{3,2,1,0:T(8,128)(2,1)}), bf16[8,4,64,128]{3,2,1,0:T(8,128)(2,1)S(1)}, u32[]{:S(2)}, u32[]{:S(2)}) async-start(bf16[8,4,64,128]{3,2,1,0:T(8,128)(2,1)} %bitcast.14), calls=%async_computation | async-start | bytes 1048576 | tf_op jit(solution)/shard_map/all_to_all | solution.py:453
  10.3 45.3 %copy-start = (s32[512]{0:T(512)S(1)}, s32[512]{0:T(512)}, u32[]{:S(2)}) copy-start(s32[512]{0:T(512)} %mask_s.3) | copy-start | bytes 6148
  37.1 1.9 %collective-permute-start = (bf16[64,32,128]{2,1,0:T(8,128)(2,1)S(1)}, bf16[64,32,128]{2,1,0:T(8,128)(2,1)S(1)}, u32[]{:S(2)}, u32[]{:S(2)}) collective-permute-start(bf16[64,32,128]{2,1,0:T(8,128)(2,1)S(1)} %all_to_all.35.mine), channel_id=1, source_target_pairs={{0,8},{8,0},{1,9},{9,1},{2,10},{10,2},{3,11},{11,3},{4,12},{12,4},... | collective-permute-start | bytes 1572872 | tf_op jit(solution)/shard_map/ppermute | solution.py:449
  74.6 1.9 %collective-permute-start.1 = (bf16[64,32,128]{2,1,0:T(8,128)(2,1)S(1)}, bf16[64,32,128]{2,1,0:T(8,128)(2,1)S(1)}, u32[]{:S(2)}, u32[]{:S(2)}) collective-permute-start(bf16[64,32,128]{2,1,0:T(8,128)(2,1)S(1)} %all_to_all.37.mine), channel_id=1, source_target_pairs={{0,8},{8,0},{1,9},{9,1},{2,10},{10,2},{3,11},{11,3},{4,12},{12,4},... | collective-permute-start | bytes 1572872 | tf_op jit(solution)/shard_map/ppermute | solution.py:449
  119.8 2.7 %collective-permute-start.2 = (bf16[64,64,128]{2,1,0:T(8,128)(2,1)S(1)}, bf16[64,64,128]{2,1,0:T(8,128)(2,1)S(1)}, u32[]{:S(2)}, u32[]{:S(2)}) collective-permute-start(bf16[64,64,128]{2,1,0:T(8,128)(2,1)S(1)} %all_to_all.39.mine), channel_id=1, source_target_pairs={{0,8},{8,0},{1,9},{9,1},{2,10},{10,2},{3,11},{11,3},{4,12},{12,4},... | collective-permute-start | bytes 3145736 | tf_op jit(solution)/shard_map/ppermute | solution.py:449

commit v10 on v8

--- a/solution.py
+++ b/solution.py
@@ -284,7 +284,7 @@
         gate_out[:, span] = sigmoid(dot(weight_t, normed, 1, 0)).astype(BF16)
 
 
-def product_cols(mine, other, lines, check_in, out, left, right, product, stage, stage_out):
+def product_cols(mine, other, lines, check_in, out, left, right, turned, stage, stage_out):
     core = lax.axis_index("core")
     for side, buf in enumerate((mine, other)):
         stage[...] = buf[...].astype(F32).reshape(64 * 32, LANES)
@@ -293,13 +293,12 @@
             lanes = slice(chunk * LANES, (chunk + 1) * LANES)
             left[rows, lanes] = stage[pl.ds(chunk, 256, stride=8), :].astype(BF16)
             right[rows, lanes] = stage[pl.ds(4 + chunk, 256, stride=8), :].astype(BF16)
-    product[...] = dot(left[...], right[...], 0, 0)
-    for p in range(8):
-        rows = product[pl.ds(pl.multiple_of(p * 64 + core * 32, 32), 32), :]
-        for chunk in range(CHUNKS):
-            stage_out[pl.ds(p * 128 + chunk, 32, stride=4), :] = rows[
-                :, chunk * LANES : (chunk + 1) * LANES
-            ]
+    turned[...] = jnp.transpose(left[...].astype(F32)).astype(BF16)
+    chosen = [turned[pl.ds(pl.multiple_of(p * 64 + core * 32, 32), 32), :] for p in range(8)]
+    product = dot(jnp.concatenate(chosen, axis=0), right[...], 1, 0)
+    for chunk in range(CHUNKS):
+        lanes = slice(chunk * LANES, (chunk + 1) * LANES)
+        stage_out[pl.ds(chunk, 256, stride=4), :] = product[:, lanes]
     out[:, 0:16, :] = stage_out[...].astype(BF16).reshape(64, 16, LANES)
     weight_rows = lines[IN_CHECK, :].astype(BF16)
     total = folded(dot(thirds(dot(weight_rows, left[...], 1, 1)), right[...], 1, 0))
@@ -539,7 +538,7 @@
     (sent,) = call(
         product_cols,
         [((64, 24, LANES), BF16)],
-        [((NT, NT), BF16), ((NT, NT), BF16), ((NT, NT), F32), ((64 * 32, LANES), F32),
+        [((NT, NT), BF16), ((NT, NT), BF16), ((NT, NT), BF16), ((64 * 32, LANES), F32),
          ((1024, LANES), F32)],
         [("v", mine), ("v", other), ("v", lines), ("v", check_out)],
     )

time: 141 us -> 141 us (level)
  no operation moved by 1% of the time
where the time goes in v10:
time: 141 us; the launch traced here: 140 us
  blocking collectives  107 us (76%)
  Pallas kernels  18.6 us (13%)
  waiting for transfers between devices  6.95 us (5%)
  starting transfers between devices  5.42 us (4%)
  local copies, waits for them, and re-layouts  2.08 us (1%)
    all_to_all x6, blocking collectives, exchange(): return lax.all_to_all(values, axes, 0, 0, tiled=True)  107 us
    pallas_call x10, Pallas kernels, call(): pl.pallas_call(kernel, out_shape=tuple((shape_of(*out) for out in outs)),...  18.6 us
    all_to_all x1, starting transfers between devices, exchange(): return lax.all_to_all(values, axes, 0, 0, tiled=True)  5.41 us
    all_to_all x1, waiting for transfers between devices, exchange(): return lax.all_to_all(values, axes, 0, 0, tiled=True)  3.71 us
    ppermute x3, waiting for transfers between devices, swap(): return lax.ppermute(values, 'core', [(0, 1), (1, 0)])  3.24 us
  transfers between devices with their start and end apart: 4, of which 4 were waited for; matrix products, arithmetic and copies ran while one was open for 1% of the time, Pallas kernels for 5%

profile of v10, /device:TPU:0, one launch (start us, length us, event | category | flops | bytes accessed | tf_op | source)
XLA Modules:
  0.0 140.3 jit_solution(16065071779458858986)
XLA Ops:
  0.6 5.4 %all-to-all-start = ((bf16[8,4,64,128]{3,2,1,0:T(8,128)(2,1)}), bf16[8,4,64,128]{3,2,1,0:T(8,128)(2,1)S(1)}, u32[]{:S(2)}, u32[]{:S(2)}) async-start(bf16[8,4,64,128]{3,2,1,0:T(8,128)(2,1)} %bitcast.14), calls=%async_computation | async-start | bytes 1048576 | tf_op jit(solution)/shard_map/all_to_all | solution.py:451
  6.0 1.3 pad.4.refs_11_
  7.3 2.9 %shard_map.202 = bf16[64,32,128]{2,1,0:T(8,128)(2,1)S(1)} custom-call(s32[512]{0:T(512)} %mask_s.3, s32[1,512]{1,0:T(1,128)} %bitcast.12, bf16[2048,128]{1,0:T(8,128)(2,1)} %bitcast.15, f32[1,128]{1,0:T(1,128)} %bitcast.19, bf16[128,256]{1,0:T(8,128)(2,1)} %weight.1), custom_call_target="tpu_custom_call" | custom-call | tf_op jit(solution)/shard_map/pallas_call | solution.py:78
  10.3 0.0 copy-start
  10.3 1.5 %shard_map.203 = (bf16[1168,128]{1,0:T(8,128)(2,1)S(1)}, bf16[128,256]{1,0:T(8,128)(2,1)S(1)}, f32[128,8]{1,0:T(8,128)S(1)}, f32[24,512]{1,0:T(8,128)S(1)}) custom-call(f32[1,128]{1,0:T(1,128)} %bitcast.20, bf16[128,128]{1,0:T(8,128)(2,1)} %refs_1_.1, f32[1,64]{1,0:T(1,128)} %bitcast.22, bf16[64,128]{1,0:T(8,128)(2,1)} %refs_3_.1, f32[1,128]{1,0:T(1,128)} %bitcast.23, ...), custom_call_target="tpu_custom_call" | custom-call | tf_op jit(solution)/shard_map/pallas_call | solution.py:78
  11.8 3.7 %all-to-all-done.x = bf16[8,4,64,128]{3,2,1,0:T(8,128)(2,1)S(1)} async-done(((bf16[8,4,64,128]{3,2,1,0:T(8,128)(2,1)}), bf16[8,4,64,128]{3,2,1,0:T(8,128)(2,1)S(1)}, u32[]{:S(2)}, u32[]{:S(2)}) %all-to-all-start) | async-done | bytes 524320 | tf_op jit(solution)/shard_map/all_to_all | solution.py:451
  15.5 21.6 %all_to_all.35.mine = bf16[64,32,128]{2,1,0:T(8,128)(2,1)S(1)} all-to-all(bf16[64,32,128]{2,1,0:T(8,128)(2,1)S(1)} %shard_map.202), channel_id=1, replica_groups=mesh['p'=8,'core'=2,'q'=8] {'p','q'}, dimensions={0} | all-to-all | bytes 1048576 | tf_op jit(solution)/shard_map/all_to_all | solution.py:451
  37.1 0.0 collective-permute-start
  37.1 1.2 shard_map.204
  38.3 0.7 collective-permute-done.other
  39.0 0.7 shard_map.205
  39.6 15.9 %all_to_all.36.recv = bf16[64,16,128]{2,1,0:T(8,128)(2,1)S(1)} all-to-all(bf16[64,16,128]{2,1,0:T(8,128)(2,1)S(1)} %get-tuple-element.60), channel_id=1, replica_groups=mesh['p'=8,'core'=2,'q'=8] {'p','q'}, dimensions={0} | all-to-all | bytes 524288 | tf_op jit(solution)/shard_map/all_to_all | solution.py:451
  55.5 0.0 copy-done
  55.5 2.2 %shard_map.206 = (bf16[64,32,128]{2,1,0:T(8,128)(2,1)S(1)}, f32[128,2048]{1,0:T(8,128)S(1)}) custom-call(s32[512]{0:T(512)S(1)} %copy-done, f32[24,512]{1,0:T(8,128)S(1)} %get-tuple-element.50.lines, bf16[64,16,128]{2,1,0:T(8,128)(2,1)S(1)} %all_to_all.36.recv, bf16[128,2048]{1,0:T(8,128)(2,1)S(1)} %get-tuple-element.61.state_in, ...), custom_call_target="tpu_custom_call" | custom-call | tf_op jit(solution)/shard_map/pallas_call | solution.py:78
  57.8 16.8 %all_to_all.37.mine = bf16[64,32,128]{2,1,0:T(8,128)(2,1)S(1)} all-to-all(bf16[64,32,128]{2,1,0:T(8,128)(2,1)S(1)} %get-tuple-element.64), channel_id=1, replica_groups=mesh['p'=8,'core'=2,'q'=8] {'p','q'}, dimensions={0} | all-to-all | bytes 1048576 | tf_op jit(solution)/shard_map/all_to_all | solution.py:451
  74.6 0.0 collective-permute-start.1
  74.6 0.6 shard_map.207
  75.2 1.3 collective-permute-done.1.other
  76.5 1.1 shard_map.208
  77.6 17.2 %all_to_all.38.recv = bf16[64,24,128]{2,1,0:T(8,128)(2,1)S(1)} all-to-all(bf16[64,24,128]{2,1,0:T(8,128)(2,1)S(1)} %shard_map.208), channel_id=1, replica_groups=mesh['p'=8,'core'=2,'q'=8] {'p','q'}, dimensions={0} | all-to-all | bytes 786432 | tf_op jit(solution)/shard_map/all_to_all | solution.py:451
  94.8 1.0 shard_map.209
  95.8 21.9 %all_to_all.39.mine = bf16[64,64,128]{2,1,0:T(8,128)(2,1)S(1)} all-to-all(bf16[64,64,128]{2,1,0:T(8,128)(2,1)S(1)} %get-tuple-element.75), channel_id=1, replica_groups=mesh['p'=8,'core'=2,'q'=8] {'p','q'}, dimensions={0} | all-to-all | bytes 2097152 | tf_op jit(solution)/shard_map/all_to_all | solution.py:451
  117.7 0.0 collective-permute-start.2
  117.7 1.4 %shard_map.210 = (bf16[128,2048]{1,0:T(8,128)(2,1)S(1)}, bf16[2048,128]{1,0:T(8,128)(2,1)S(1)}, bf16[128,2048]{1,0:T(8,128)(2,1)S(1)}, bf16[128,2048]{1,0:T(8,12...) custom-call(bf16[64,24,128]{2,1,0:T(8,128)(2,1)S(1)} %all_to_all.38.recv, ...), custom_call_target="tpu_custom_call" | custom-call | tf_op jit(solution)/shard_map/pallas_call | solution.py:78
  119.1 1.3 collective-permute-done.2.bias_other
  120.4 5.8 %shard_map.211 = bf16[8,4,64,128]{3,2,1,0:T(8,128)(2,1)S(1)} custom-call(f32[24,512]{1,0:T(8,128)S(1)} %get-tuple-element.50.lines, f32[4096,128]{1,0:T(8,128)S(1)} %get-tuple-element.79.mine, bf16[64,64,128]{2,1,0:T(8,128)(2,1)S(1)} %collective-permute-done.2.bias_other, bf16[128,2048]{1,0:T(8,128)(2,1)S(1)} %get-tuple-element.82.query, ...), custom_call_target="tpu_custom_call" | custom-call | tf_op jit(solution)/shard_map/pallas_call | solution.py:78
  126.2 13.3 %all_to_all.40 = bf16[8,4,64,128]{3,2,1,0:T(8,128)(2,1)S(1)} all-to-all(bf16[8,4,64,128]{3,2,1,0:T(8,128)(2,1)S(1)} %shard_map.211), channel_id=1, replica_groups=mesh['p'=8,'core'=2,'q'=8] {'q'}, dimensions={0} | all-to-all | bytes 1048576 | tf_op jit(solution)/shard_map/all_to_all | solution.py:451
  139.5 0.8 copy.23
Async XLA Ops:
  0.6 14.9 %all-to-all-start = ((bf16[8,4,64,128]{3,2,1,0:T(8,128)(2,1)}), bf16[8,4,64,128]{3,2,1,0:T(8,128)(2,1)S(1)}, u32[]{:S(2)}, u32[]{:S(2)}) async-start(bf16[8,4,64,128]{3,2,1,0:T(8,128)(2,1)} %bitcast.14), calls=%async_computation | async-start | bytes 1048576 | tf_op jit(solution)/shard_map/all_to_all | solution.py:451
  10.3 45.3 %copy-start = (s32[512]{0:T(512)S(1)}, s32[512]{0:T(512)}, u32[]{:S(2)}) copy-start(s32[512]{0:T(512)} %mask_s.3) | copy-start | bytes 6148
  37.1 1.9 %collective-permute-start = (bf16[64,32,128]{2,1,0:T(8,128)(2,1)S(1)}, bf16[64,32,128]{2,1,0:T(8,128)(2,1)S(1)}, u32[]{:S(2)}, u32[]{:S(2)}) collective-permute-start(bf16[64,32,128]{2,1,0:T(8,128)(2,1)S(1)} %all_to_all.35.mine), channel_id=1, source_target_pairs={{0,8},{8,0},{1,9},{9,1},{2,10},{10,2},{3,11},{11,3},{4,12},{12,4},... | collective-permute-start | bytes 1572872 | tf_op jit(solution)/shard_map/ppermute | solution.py:447
  74.6 1.9 %collective-permute-start.1 = (bf16[64,32,128]{2,1,0:T(8,128)(2,1)S(1)}, bf16[64,32,128]{2,1,0:T(8,128)(2,1)S(1)}, u32[]{:S(2)}, u32[]{:S(2)}) collective-permute-start(bf16[64,32,128]{2,1,0:T(8,128)(2,1)S(1)} %all_to_all.37.mine), channel_id=1, source_target_pairs={{0,8},{8,0},{1,9},{9,1},{2,10},{10,2},{3,11},{11,3},{4,12},{12,4},... | collective-permute-start | bytes 1572872 | tf_op jit(solution)/shard_map/ppermute | solution.py:447
  117.7 2.7 %collective-permute-start.2 = (bf16[64,64,128]{2,1,0:T(8,128)(2,1)S(1)}, bf16[64,64,128]{2,1,0:T(8,128)(2,1)S(1)}, u32[]{:S(2)}, u32[]{:S(2)}) collective-permute-start(bf16[64,64,128]{2,1,0:T(8,128)(2,1)S(1)} %all_to_all.39.mine), channel_id=1, source_target_pairs={{0,8},{8,0},{1,9},{9,1},{2,10},{10,2},{3,11},{11,3},{4,12},{12,4},... | collective-permute-start | bytes 3145736 | tf_op jit(solution)/shard_map/ppermute | solution.py:447
